TPU v7x, 32 devices: a whole 2x2x4 slice. The times are simulated.
32 devices in a mesh: member: 4 (over y, x), section: 2 (over core), dp: 4 (over z).
Axes of the slice: x: 2, y: 2, z: 4, core: 2. Of those that a mesh axis runs over, the one named last changes fastest.
Arguments:
- tokens: int32 [16, 2, 512], P(('member', 'dp')), parts along dimension 0, may hold values from 0 to 50303
- margins: int32 [16], P(('member', 'dp')), parts along dimension 0, may hold values from 1 to 6, as said below
- tie_flags: int32 [16], P(('member', 'dp')), parts along dimension 0, may hold values 0 or 1
- embedding: float32 [3072, 50304], P(('member', 'section', 'dp')), parts along dimension 0, may hold values from -1.2 to 1.2
- embed_moment: float32 [3072, 50304], P(('member', 'section', 'dp')), parts along dimension 0, may hold values from -3.02732e-05 to 3.02732e-05
- embed_second: float32 [3072, 50304], P(('member', 'section', 'dp')), parts along dimension 0, may hold values from 4.7338158e-12 to 1.8935263e-11
- layer_blocks: float32 [8, 48, 384, 384], P(('member', 'section'), 'dp'), parts along dimension 0, may hold values from -0.21875 to 0.21875
- left_stats: float32 [8, 48, 384, 384], P(('member', 'section'), 'dp'), parts along dimension 0, may hold values from 0 to 1.56809423e-06, as said below
- right_stats: float32 [8, 48, 384, 384], P(('member', 'section'), 'dp'), parts along dimension 0, may hold values from 0 to 1.56809423e-06, as said below
- left_root: float32 [8, 48, 384, 384], P(('member', 'section'), 'dp'), parts along dimension 0, may hold values from -40.211745 to 60.31762, as said below
- right_root: float32 [8, 48, 384, 384], P(('member', 'section'), 'dp'), parts along dimension 0, may hold values from -40.211745 to 60.31762, as said below
- layer_vectors: float32 [8, 9984], P(('member', 'section'), 'dp'), parts along dimension 0, may hold values from -0.35 to 1.9
- vector_moment: float32 [8, 9984], P(('member', 'section'), 'dp'), parts along dimension 0, may hold values from -0.00030273202 to 0.00030273202
- vector_second: float32 [8, 9984], P(('member', 'section'), 'dp'), parts along dimension 0, may hold values from 4.7338156e-10 to 1.8935262e-09
- closing_vectors: float32 [9216], P(('member', 'section', 'dp')), parts along dimension 0, may hold values from -1.46969385 to 2
- final_moment: float32 [9216], P(('member', 'section', 'dp')), parts along dimension 0, may hold values from -0.00030273202 to 0.00030273202
- final_second: float32 [9216], P(('member', 'section', 'dp')), parts along dimension 0, may hold values from 4.7338156e-10 to 1.8935262e-09
Outputs:
- loss_sum: float32 [4], P('member'), parts along dimension 0
- grad_norm: float32 [4], P('member'), parts along dimension 0
- block_grads: float32 [8, 48, 384, 384], P(('member', 'section'), 'dp'), parts along dimension 0
- new_blocks: float32 [8, 48, 384, 384], P(('member', 'section'), 'dp'), parts along dimension 0
- new_left: float32 [8, 48, 384, 384], P(('member', 'section'), 'dp'), parts along dimension 0
- new_right: float32 [8, 48, 384, 384], P(('member', 'section'), 'dp'), parts along dimension 0
- vector_moments: float32 [8, 9984], P(('member', 'section'), 'dp'), parts along dimension 0
- vector_seconds: float32 [8, 9984], P(('member', 'section'), 'dp'), parts along dimension 0
- new_vectors: float32 [8, 9984], P(('member', 'section'), 'dp'), parts along dimension 0
- final_moments: float32 [9216], P(('member', 'section', 'dp')), parts along dimension 0
- final_seconds: float32 [9216], P(('member', 'section', 'dp')), parts along dimension 0
- new_final: float32 [9216], P(('member', 'section', 'dp')), parts along dimension 0
- embed_moments: float32 [3072, 50304], P(('member', 'section', 'dp')), parts along dimension 0
- embed_seconds: float32 [3072, 50304], P(('member', 'section', 'dp')), parts along dimension 0
- new_embedding: float32 [3072, 50304], P(('member', 'section', 'dp')), parts along dimension 0
There are 4 independent parts, one for each index of `member`. A program takes and returns all parts, laid end to end along the dimension named above; each array names one. Nothing has to cross between parts.
Inputs may be any that keep to these rules, and one draw needn't show every extreme that they name: margins never fall by more than 1 from one pair to the next. `left_stats`: diagonal, positive on the diagonal. `right_stats`: diagonal, positive on the diagonal. `left_root`: symmetric. `right_root`: symmetric.
All inputs are finite; a program needn't handle non-finite values. No bound on the sum of `tie_flags` on one device may be relied on, other than what follows from the above.
Results may differ from a plain program's by a relative error of at most 0.011.
The roundings to bfloat16 on the way count: a program that leaves them out, or rounds other values in their place, can miss the bound.
Values may be sent and summed in bfloat16 or wider, within the bound.
No kernel may reach another device: no remote copies, remote signals or barrier semaphores. Data moves between devices by JAX's collectives and lax.ppermute only.
A program may use at most 512 MiB of HBM per device.

v0:
```python
import math

import jax
import jax.numpy as jnp
from jax import lax
from jax.sharding import PartitionSpec as P

D = 768
HEADS = 12
ROT = 16
FF = 3072
STEP = 10


highest = lax.Precision.HIGHEST
norm_eps = 1e-05
beta_first = 0.9
beta_second = 0.999
adam_eps = 1e-08
clip_limit = 1.0
embed_rate = 0.2
embed_decay = 0.01
vector_rate = 0.5
shampoo_rate = 0.1
stats_decay = 0.95
rope_base = 10000.0


def passed_along(block, axis, distance):
    devices = range(lax.axis_size(axis))
    route = [(i - distance, i) for i in devices if i - distance in devices]
    return lax.ppermute(block, axis, route)


def layer_norm(values, gain, shift):
    centred = values - jnp.mean(values, axis=-1, keepdims=True)
    spread = jnp.mean(centred * centred, axis=-1, keepdims=True)
    return centred * lax.rsqrt(spread + norm_eps) * gain + shift


def rope_tables(positions, head_size):
    half_rot = ROT // 2
    lanes = jnp.arange(head_size)
    index = jnp.where(lanes < half_rot, lanes, lanes - half_rot).astype(jnp.float32)
    inverse_matrix = rope_base ** (-2.0 * index / ROT)
    angles = positions[:, None].astype(jnp.float32) * inverse_matrix[None, :]
    inside = lanes < ROT
    cosine = jnp.where(inside, jnp.cos(angles), 1.0)
    sine = jnp.where(inside, jnp.sin(angles), 0.0)
    return (cosine[:, None, :], sine[:, None, :])


def rotate(values, cosine, sine):
    half_rot = ROT // 2
    turned = jnp.concatenate(
        [-values[..., half_rot:ROT], values[..., :half_rot], values[..., ROT:]], axis=-1
    )
    return values * cosine + turned * sine


def blocks_to_mats(blocks, model_width, hidden, block_size):
    tiles_d = model_width // block_size
    tiles_f = hidden // block_size

    def build(start, row_tiles, col_tiles):
        piece = blocks[start : start + row_tiles * col_tiles].reshape(
            row_tiles, col_tiles, block_size, block_size
        )
        return piece.transpose(0, 2, 1, 3).reshape(row_tiles * block_size, col_tiles * block_size)

    first = tiles_d * 3 * tiles_d
    second = first + tiles_d * tiles_d
    third = second + tiles_d * tiles_f
    return (
        build(0, tiles_d, 3 * tiles_d),
        build(first, tiles_d, tiles_d),
        build(second, tiles_d, tiles_f),
        build(third, tiles_f, tiles_d),
    )


def mats_to_blocks(matrices, block_size):
    tiles = []
    for matrix in matrices:
        row_tiles = matrix.shape[0] // block_size
        col_tiles = matrix.shape[1] // block_size
        tiles.append(
            matrix.reshape(row_tiles, block_size, col_tiles, block_size)
            .transpose(0, 2, 1, 3)
            .reshape(-1, block_size, block_size)
        )
    return jnp.concatenate(tiles, axis=0)


def split_vectors(vectors, model_width, hidden):
    widths = [model_width] * 4 + [3 * model_width, model_width, hidden, model_width]
    parts = []
    start = 0
    for count in widths:
        parts.append(vectors[start : start + count])
        start = start + count
    return parts


def attention_scores(queries, kv_cache, positions, head_count, head_size):
    model_width = head_count * head_size
    length = kv_cache.shape[0]
    all_keys = kv_cache[:, :model_width].reshape(length, head_count, head_size)
    all_values = kv_cache[:, model_width:].reshape(length, head_count, head_size)
    scores = jnp.einsum(
        "qhd,khd->hqk", queries, all_keys, preferred_element_type=jnp.float32
    ) / math.sqrt(head_size)
    allowed = jnp.arange(length)[None, :] <= positions[:, None]
    return (jnp.where(allowed[None], scores, -1e30), all_keys, all_values)


def layer_forward(params, inputs, offset, kv_cache):
    (qkv_w, out_w, up_w, down_w), vectors = params
    gain_one, shift_one, gain_two, shift_two, qkv_bias, out_bias, up_bias, down_bias = vectors
    piece_rows, model_width = inputs.shape
    head_count = HEADS
    head_size = model_width // head_count
    positions = offset + jnp.arange(piece_rows)
    cosine, sine = rope_tables(positions, head_size)
    normed = layer_norm(inputs, gain_one, shift_one).astype(jnp.bfloat16)
    projected = jnp.dot(normed, qkv_w, preferred_element_type=jnp.float32) + qkv_bias
    queries = rotate(
        projected[:, :model_width].reshape(piece_rows, head_count, head_size), cosine, sine
    ).astype(jnp.bfloat16)
    keys_new = rotate(
        projected[:, model_width : 2 * model_width].reshape(piece_rows, head_count, head_size),
        cosine,
        sine,
    ).astype(jnp.bfloat16)
    values_new = projected[:, 2 * model_width :].astype(jnp.bfloat16)
    fresh = jnp.concatenate([keys_new.reshape(piece_rows, model_width), values_new], axis=1)
    kv_cache = fresh
    scores, all_keys, all_values = attention_scores(
        queries, kv_cache, positions, head_count, head_size
    )
    row_peak = jnp.max(scores, axis=-1, keepdims=True)
    expo = jnp.exp(scores - row_peak)
    total = jnp.sum(expo, axis=-1, keepdims=True)
    soft = (expo / total).astype(jnp.bfloat16)
    log_total = row_peak + jnp.log(total)
    attended = jnp.einsum("hqk,khd->qhd", soft, all_values, preferred_element_type=jnp.float32)
    attended = attended.reshape(piece_rows, model_width).astype(jnp.bfloat16)
    attn_out = jnp.dot(attended, out_w, preferred_element_type=jnp.float32) + out_bias
    second = layer_norm(inputs, gain_two, shift_two).astype(jnp.bfloat16)
    pre_act = jnp.dot(second, up_w, preferred_element_type=jnp.float32) + up_bias
    activated = jax.nn.gelu(pre_act, approximate=False).astype(jnp.bfloat16)
    branch = jnp.dot(activated, down_w, preferred_element_type=jnp.float32) + down_bias
    output = inputs + attn_out + branch
    return (output, kv_cache, (inputs, queries, attended, log_total, pre_act))


def layer_backward(params, grad_out, saved, offset, kv_cache, kv_grad):
    (qkv_w, out_w, up_w, down_w), vectors = params
    gain_one, shift_one, gain_two, shift_two, qkv_bias, out_bias, up_bias, down_bias = vectors
    inputs, queries, attended, log_total, pre_act = saved
    piece_rows, model_width = inputs.shape
    length = kv_cache.shape[0]
    head_count = queries.shape[1]
    head_size = queries.shape[2]
    scale_factor = 1.0 / math.sqrt(head_size)
    rounded = grad_out.astype(jnp.bfloat16)
    bias_grad = jnp.sum(rounded.astype(jnp.float32), axis=0)
    second = layer_norm(inputs, gain_two, shift_two).astype(jnp.bfloat16)
    activated = jax.nn.gelu(pre_act, approximate=False).astype(jnp.bfloat16)
    down_grad = jnp.dot(activated.T, rounded, preferred_element_type=jnp.float32)
    act_grad = jnp.dot(rounded, down_w.T, preferred_element_type=jnp.float32)
    gelu_back = jax.vjp(lambda point: jax.nn.gelu(point, approximate=False), pre_act)[1]
    pre_grad = gelu_back(act_grad)[0].astype(jnp.bfloat16)
    up_grad = jnp.dot(second.T, pre_grad, preferred_element_type=jnp.float32)
    up_bias_grad = jnp.sum(pre_grad.astype(jnp.float32), axis=0)
    second_grad = jnp.dot(pre_grad, up_w.T, preferred_element_type=jnp.float32)
    out_grad = jnp.dot(attended.T, rounded, preferred_element_type=jnp.float32)
    mix_grad = jnp.dot(rounded, out_w.T, preferred_element_type=jnp.float32).astype(jnp.bfloat16)
    mix_grad = mix_grad.reshape(piece_rows, head_count, head_size)
    positions = offset + jnp.arange(piece_rows)
    scores, all_keys, all_values = attention_scores(
        queries, kv_cache, positions, head_count, head_size
    )
    soft = jnp.exp(scores - log_total)
    soft_grad = jnp.einsum("qhd,khd->hqk", mix_grad, all_values, preferred_element_type=jnp.float32)
    value_grad = jnp.einsum(
        "hqk,qhd->khd", soft.astype(jnp.bfloat16), mix_grad, preferred_element_type=jnp.float32
    )
    centre = jnp.sum(soft * soft_grad, axis=-1, keepdims=True)
    score_gradient = (soft * (soft_grad - centre)).astype(jnp.bfloat16)
    query_grad = (
        jnp.einsum("hqk,khd->qhd", score_gradient, all_keys, preferred_element_type=jnp.float32)
        * scale_factor
    )
    key_grad = (
        jnp.einsum("hqk,qhd->khd", score_gradient, queries, preferred_element_type=jnp.float32)
        * scale_factor
    )
    kv_grad = kv_grad + jnp.concatenate(
        [key_grad.reshape(length, model_width), value_grad.reshape(length, model_width)], axis=1
    )
    cosine, sine = rope_tables(positions, head_size)
    rotary_backward = jax.vjp(
        lambda point: rotate(point, cosine, sine),
        jnp.zeros((piece_rows, head_count, head_size), jnp.float32),
    )[1]
    query_pre = rotary_backward(query_grad)[0].reshape(piece_rows, model_width)
    key_pre = rotary_backward(kv_grad[:, :model_width].reshape(piece_rows, head_count, head_size))[
        0
    ].reshape(piece_rows, model_width)
    proj_grad = jnp.concatenate([query_pre, key_pre, kv_grad[:, model_width:]], axis=1).astype(
        jnp.bfloat16
    )
    normed = layer_norm(inputs, gain_one, shift_one).astype(jnp.bfloat16)
    qkv_grad = jnp.dot(normed.T, proj_grad, preferred_element_type=jnp.float32)
    qkv_bias_grad = jnp.sum(proj_grad.astype(jnp.float32), axis=0)
    normed_grad = jnp.dot(proj_grad, qkv_w.T, preferred_element_type=jnp.float32)
    first_in, gain_one_grad, shift_one_grad = jax.vjp(layer_norm, inputs, gain_one, shift_one)[1](
        normed_grad
    )
    second_in, gain_two_grad, shift_two_grad = jax.vjp(layer_norm, inputs, gain_two, shift_two)[1](
        second_grad
    )
    grad_in = grad_out + first_in + second_in
    vector_grad = jnp.concatenate(
        [
            gain_one_grad,
            shift_one_grad,
            gain_two_grad,
            shift_two_grad,
            qkv_bias_grad,
            bias_grad,
            up_bias_grad,
            bias_grad,
        ]
    )
    return (grad_in, kv_grad, (qkv_grad, out_grad, up_grad, down_grad), vector_grad)


def adam_step(weight, moment, second, grad, rate, decay):
    moment_new = beta_first * moment + (1.0 - beta_first) * grad
    second_new = beta_second * second + (1.0 - beta_second) * grad * grad
    corrected = moment_new / (1.0 - beta_first**STEP)
    scaled = jnp.sqrt(second_new / (1.0 - beta_second**STEP)) + adam_eps
    return (moment_new, second_new, weight - rate * (corrected / scaled + decay * weight))


def local(
    tokens,
    margins,
    tie_flags,
    embedding,
    embed_moment,
    embed_second,
    layer_blocks,
    left_stats,
    right_stats,
    left_root,
    right_root,
    layer_vectors,
    vector_moment,
    vector_second,
    closing_vectors,
    final_moment,
    final_second,
):
    section_index = lax.axis_index("section")
    first_section = section_index == 0
    last_live = (section_index == 1).astype(jnp.float32)
    length = tokens.shape[2]
    model_width = D
    hidden = FF
    half_width = model_width // 2
    head_count = HEADS
    head_size = model_width // head_count
    block_size = layer_blocks.shape[2]
    pieces = 1
    piece_rows = length // pieces
    unit_count = 2 * pieces
    gathered_blocks, gathered_vectors = (
        lax.all_gather(layer_blocks.astype(jnp.bfloat16), "dp", axis=1, tiled=True),
        lax.all_gather(layer_vectors.astype(jnp.bfloat16), "dp", axis=1, tiled=True),
    )
    weights = blocks_to_mats(gathered_blocks[0], model_width, hidden, block_size)
    vectors = split_vectors(gathered_vectors[0].astype(jnp.float32), model_width, hidden)
    params = (weights, vectors)
    vector_total = gathered_vectors.shape[1]
    final_all = lax.all_gather(
        closing_vectors.astype(jnp.bfloat16), ("section", "dp"), axis=0, tiled=True
    ).astype(jnp.float32)
    final_gain = final_all[:model_width]
    final_shift = final_all[model_width : 2 * model_width]
    reward_head_weight = final_all[2 * model_width :]
    all_ids = lax.all_gather(tokens, "dp", axis=0, tiled=True)
    looked = jnp.moveaxis(jnp.take(embedding.astype(jnp.bfloat16), all_ids, axis=1), 0, -1)
    own_half = lax.all_to_all(looked, "dp", split_axis=0, concat_axis=3, tiled=True)[0]
    other_half = passed_along(own_half, "section", -1)
    embedded = jnp.concatenate([own_half, other_half], axis=2).astype(jnp.float32)
    kept_store = (
        jnp.zeros((unit_count, piece_rows, model_width), jnp.float32),
        jnp.zeros((unit_count, piece_rows, head_count, head_size), jnp.bfloat16),
        jnp.zeros((unit_count, piece_rows, model_width), jnp.bfloat16),
        jnp.zeros((unit_count, head_count, piece_rows, 1), jnp.float32),
        jnp.zeros((unit_count, piece_rows, hidden), jnp.float32),
    )
    caches = jnp.zeros((2, length, 2 * model_width), jnp.bfloat16)
    finals = jnp.zeros((2, length, model_width), jnp.float32)
    received = jnp.zeros((piece_rows, model_width), jnp.bfloat16)

    def run_forward(operand_list):
        values, start_row, memory, previous = operand_list
        return layer_forward(params, values, start_row, memory)

    def skip_forward(operand_list):
        values, start_row, memory, previous = operand_list
        return (jnp.zeros_like(values), memory, previous)

    for ticks in range(unit_count + 1):
        unit_index = ticks - section_index
        active = (unit_index >= 0) & (unit_index < unit_count)
        slot_index = jnp.clip(unit_index, 0, unit_count - 1)
        sequence_slot = slot_index // pieces
        offset = slot_index % pieces * piece_rows
        from_table = lax.dynamic_slice(
            embedded, (sequence_slot, offset, 0), (1, piece_rows, model_width)
        )[0]
        inputs = jnp.where(first_section, from_table, received.astype(jnp.float32))
        old_kept = tuple((store[slot_index] for store in kept_store))
        output, kv_cache, kept = lax.cond(
            active, run_forward, skip_forward, (inputs, offset, caches[sequence_slot], old_kept)
        )
        caches = caches.at[sequence_slot].set(kv_cache)
        kept_store = tuple(
            (store.at[slot_index].set(item) for store, item in zip(kept_store, kept))
        )
        previous_final = lax.dynamic_slice(
            finals, (sequence_slot, offset, 0), (1, piece_rows, model_width)
        )[0]
        finals = lax.dynamic_update_slice(
            finals, jnp.where(active, output, previous_final)[None], (sequence_slot, offset, 0)
        )
        if ticks < unit_count:
            received = passed_along(output.astype(jnp.bfloat16), "section", 1)
    final_normalized = layer_norm(finals, final_gain, final_shift)
    reduced_final_state = final_normalized.astype(jnp.bfloat16)
    token_scores = jnp.einsum(
        "ocg,g->oc",
        reduced_final_state,
        reward_head_weight.astype(jnp.bfloat16),
        preferred_element_type=jnp.float32,
    )
    rewards = jnp.mean(token_scores, axis=1)
    gap = rewards[0] - rewards[1]
    half_margin = 0.5 * margins[0].astype(jnp.float32)
    tie = tie_flags[0].astype(jnp.float32)
    pair_loss = (1.0 - tie) * jax.nn.softplus(half_margin - gap) + tie * 0.5 * (
        jax.nn.softplus(gap) + jax.nn.softplus(-gap)
    )
    gap_grad = -(1.0 - tie) * jax.nn.sigmoid(half_margin - gap) + tie * 0.5 * (
        jax.nn.sigmoid(gap) - jax.nn.sigmoid(-gap)
    )
    reward_grad = jnp.stack([gap_grad, -gap_grad]) * last_live / length
    summed_rows = jnp.sum(reduced_final_state, axis=1, dtype=jnp.float32)
    head_grad = jnp.sum(reward_grad[:, None] * summed_rows, axis=0)
    normed_grad = (
        reward_grad[:, None, None] * reward_head_weight[None, None, :] * jnp.ones_like(finals)
    )
    top_grad, gain_grad, shift_grad = jax.vjp(layer_norm, finals, final_gain, final_shift)[1](
        normed_grad
    )
    final_local = jnp.concatenate([gain_grad, shift_grad, head_grad])
    final_owned = lax.psum_scatter(final_local, ("section", "dp"), scatter_dimension=0, tiled=True)
    mat_grads = tuple((jnp.zeros(matrix.shape, jnp.float32) for matrix in weights))
    vector_grad = jnp.zeros((vector_total,), jnp.float32)
    kv_grads = jnp.zeros((length, 2 * model_width), jnp.float32)
    embed_grads = jnp.zeros((2, length, model_width), jnp.float32)
    received_grad = jnp.zeros((piece_rows, model_width), jnp.bfloat16)

    def run_backward(operand_list):
        grad_now, saved_now, start_row, memory, kv_now = operand_list
        return layer_backward(params, grad_now, saved_now, start_row, memory, kv_now)

    def skip_backward(operand_list):
        grad_now, saved_now, start_row, memory, kv_now = operand_list
        return (
            jnp.zeros_like(grad_now),
            kv_now,
            tuple((jnp.zeros(matrix.shape, jnp.float32) for matrix in weights)),
            jnp.zeros((vector_total,), jnp.float32),
        )

    for ticks in range(unit_count + 1):
        step_index = ticks - (1 - section_index)
        active = (step_index >= 0) & (step_index < unit_count)
        slot_index = jnp.clip(step_index, 0, unit_count - 1)
        unit_index = unit_count - 1 - slot_index
        sequence_slot = unit_index // pieces
        offset = unit_index % pieces * piece_rows
        head_piece = lax.dynamic_slice(
            top_grad, (sequence_slot, offset, 0), (1, piece_rows, model_width)
        )[0]
        grad_out = jnp.where(first_section, received_grad.astype(jnp.float32), head_piece)
        kv_start = jnp.where(
            offset == (pieces - 1) * piece_rows, jnp.zeros_like(kv_grads), kv_grads
        )
        saved = tuple((store[unit_index] for store in kept_store))
        grad_in, kv_grads, mat_step, vector_step = lax.cond(
            active,
            run_backward,
            skip_backward,
            (grad_out, saved, offset, caches[sequence_slot], kv_start),
        )
        mat_grads = tuple((total + part for total, part in zip(mat_grads, mat_step)))
        vector_grad = vector_grad + vector_step
        previous_grad = lax.dynamic_slice(
            embed_grads, (sequence_slot, offset, 0), (1, piece_rows, model_width)
        )[0]
        embed_grads = lax.dynamic_update_slice(
            embed_grads, jnp.where(active, grad_in, previous_grad)[None], (sequence_slot, offset, 0)
        )
        if ticks < unit_count:
            received_grad = passed_along(grad_in.astype(jnp.bfloat16), "section", -1)
    upper_half = passed_along(embed_grads[..., half_width:], "section", 1)
    mine = jnp.where(first_section, embed_grads[..., :half_width], upper_half)
    token_grads = lax.all_to_all(mine[None], "dp", split_axis=3, concat_axis=0, tiled=True)
    column_count = embedding.shape[0]
    table_grad = jax.ops.segment_sum(
        token_grads.reshape(-1, column_count), all_ids.reshape(-1), num_segments=embedding.shape[1]
    ).T
    grad_blocks = mats_to_blocks(mat_grads, block_size)
    owned_blocks, owned_vectors = (
        lax.psum_scatter(grad_blocks[None], "dp", scatter_dimension=1, tiled=True),
        lax.psum_scatter(vector_grad[None], "dp", scatter_dimension=1, tiled=True),
    )
    squares = (
        jnp.sum(owned_blocks * owned_blocks)
        + jnp.sum(owned_vectors * owned_vectors)
        + jnp.sum(final_owned * final_owned)
        + jnp.sum(table_grad * table_grad)
    )
    loss_total, square_total = lax.psum((pair_loss * last_live, squares), ("section", "dp"))
    norm_value = jnp.sqrt(square_total)
    factor = clip_limit / jnp.maximum(norm_value, clip_limit)
    block_grad = owned_blocks * factor
    new_left = stats_decay * left_stats + (1.0 - stats_decay) * jnp.einsum(
        "...ij,...kj->...ik", block_grad, block_grad, precision=highest
    )
    new_right = stats_decay * right_stats + (1.0 - stats_decay) * jnp.einsum(
        "...ji,...jk->...ik", block_grad, block_grad, precision=highest
    )
    inner = jnp.einsum("...ij,...jk->...ik", block_grad, right_root, precision=highest)
    direction = jnp.einsum("...ij,...jk->...ik", left_root, inner, precision=highest)
    new_blocks = layer_blocks - shampoo_rate * direction
    vector_m, vector_v, vector_w = adam_step(
        layer_vectors, vector_moment, vector_second, owned_vectors * factor, vector_rate, 0.0
    )
    final_m, final_v, final_w = adam_step(
        closing_vectors, final_moment, final_second, final_owned * factor, vector_rate, 0.0
    )
    embed_m, embed_v, embed_w = adam_step(
        embedding, embed_moment, embed_second, table_grad * factor, embed_rate, embed_decay
    )
    return (
        loss_total.reshape(1),
        norm_value.reshape(1),
        block_grad,
        new_blocks,
        new_left,
        new_right,
        vector_m,
        vector_v,
        vector_w,
        final_m,
        final_v,
        final_w,
        embed_m,
        embed_v,
        embed_w,
    )


def solution(mesh):
    return jax.shard_map(
        local,
        mesh=mesh,
        in_specs=(
            P(("member", "dp"), None, None),
            P(("member", "dp")),
            P(("member", "dp")),
            P(("member", "section", "dp"), None),
            P(("member", "section", "dp"), None),
            P(("member", "section", "dp"), None),
            P(("member", "section"), "dp", None, None),
            P(("member", "section"), "dp", None, None),
            P(("member", "section"), "dp", None, None),
            P(("member", "section"), "dp", None, None),
            P(("member", "section"), "dp", None, None),
            P(("member", "section"), "dp"),
            P(("member", "section"), "dp"),
            P(("member", "section"), "dp"),
            P(("member", "section", "dp")),
            P(("member", "section", "dp")),
            P(("member", "section", "dp")),
        ),
        out_specs=(
            P("member"),
            P("member"),
            P(("member", "section"), "dp", None, None),
            P(("member", "section"), "dp", None, None),
            P(("member", "section"), "dp", None, None),
            P(("member", "section"), "dp", None, None),
            P(("member", "section"), "dp"),
            P(("member", "section"), "dp"),
            P(("member", "section"), "dp"),
            P(("member", "section", "dp")),
            P(("member", "section", "dp")),
            P(("member", "section", "dp")),
            P(("member", "section", "dp"), None),
            P(("member", "section", "dp"), None),
            P(("member", "section", "dp"), None),
        ),
        check_vma=False,
    )
```

profile of v0, /device:TPU:0, one launch (start us, length us, event | category | flops | bytes accessed | tf_op | source)
XLA Modules:
  0.0 2338.6 jit_solution(12916494291285179685)
XLA Ops:
  12.5 11.7 convert_element_type.630
  24.2 15.0 copy.532
  39.2 15.5 all_gather.12
  54.7 17.4 gather_fusion
  73.7 16.4 all-to-all-start
  93.0 53.5 %all-reduce.19 = bf16[2304]{0:T(1024)(128)(2,1)S(1)} all-reduce(bf16[2304]{0:T(1024)(128)(2,1)S(1)} %dynamic-update-slice.55), channel_id=1, replica_groups=mesh['member'=4,'section'=2,'dp'=4] {'section','dp'}, use_global_device_ids=true, to_apply=%add.19 | all-reduce | flops 2304 | bytes 9216
  148.8 30.4 %all-reduce.18 = bf16[9984]{0:T(1024)(128)(2,1)S(1)} all-reduce(bf16[9984]{0:T(1024)(128)(2,1)S(1)} %dynamic-update-slice.54), channel_id=1, replica_groups=mesh['member'=4,'section'=2,'dp'=4] {'dp'}, use_global_device_ids=true, to_apply=%add.18 | all-reduce | flops 9984 | bytes 39936
  184.8 93.8 %all-gather.2.cloned.1.call-done = bf16[1,48,384,384]{3,2,0,1:T(8,128)(2,1)} async-done(((bf16[1,12,384,384]{3,2,0,1:T(8,128)(2,1)}), bf16[1,48,384,384]{3,2,0,1:T(8,128)(2,1)}) %all-gather.2.cloned.1.call-update) | async-done | bytes 14155792 | tf_op jit(solution)/shard_map/all_gather | solution.py:281
  282.7 12.3 copy.536
  302.0 7.2 fusion.456
  315.3 24.8 %copy.539 = bf16[8,384,2,384]{3,2,1,0:T(2,128)(2,1)} copy(bf16[8,384,2,384]{3,1,2,0:T(8,128)(2,1)} %bitcast.752) | data formatting | bytes 9437184 | tf_op jit(solution)/shard_map/transpose | solution.py:69
  346.9 76.4 %conditional.6 = (f32[512,768]{1,0:T(8,128)}, bf16[512,12,64]{0,2,1:T(8,128)(2,1)}, bf16[512,768]{0,1:T(8,128)(2,1)}, f32[512,3072]{1,0:T(8,128)}, f32[1,12,512,...) conditional(s32[]{:T(128)} %convert_element_type.629, () %tuple.182, (pred[]{:T(512)}, ...), branch_computations={%region_0.1_spmd, %region_1.6_spmd} | conditional | flops 8213163520 | bytes 262826208 | solution.py:329
  360.0 18.3 fusion.13
  442.6 25.2 %scatter.61 = f32[2,512,768]{1,0,2:T(2,128)S(1)} dynamic-update-slice(f32[2,512,768]{1,0,2:T(2,128)S(1)} %broadcast.2577.clone.1, f32[1,512,768]{1,0,2:T(1,128)} %copy.547, s32[]{:T(128)} %min.21, s32[]{:T(128)} %constant.1633.clone.1, s32[]{:T(128)} %constant.1633.clone.1) | dynamic-update-slice | bytes 3145732 | tf_op jit(solution)/shard_map/scatter | solution.py:334
  476.6 27.1 %scatter.65 = bf16[2,512,768]{1,0,2:T(2,128)(2,1)} dynamic-update-slice(bf16[2,512,768]{1,0,2:T(2,128)(2,1)} %broadcast_in_dim.480, bf16[1,512,768]{1,0,2:T(2,128)(2,1)} %copy.548, s32[]{:T(128)} %min.21, s32[]{:T(128)} %constant.1633.clone.1, s32[]{:T(128)} %constant.1633.clone.1) | dynamic-update-slice | bytes 1572868 | tf_op jit(solution)/shard_map/scatter | solution.py:334
  534.9 25.2 %dynamic_update_slice.24 = f32[2,512,768]{1,0,2:T(2,128)S(1)} dynamic-update-slice(f32[2,512,768]{1,0,2:T(2,128)S(1)} %broadcast.2577.clone, f32[1,512,768]{1,0,2:T(1,128)} %copy.544, s32[]{:T(128)} %min.21, s32[]{:T(128)} %constant.1633.clone.1, s32[]{:T(128)} %constant.1633.clone.1) | dynamic-update-slice | bytes 3145732 | tf_op jit(solution)/shard_map/dynamic_update_slice | solution.py:339
  573.4 99.3 %conditional.7 = (f32[512,768]{1,0:T(8,128)}, bf16[1,512,12,64]{1,3,2,0:T(8,128)(2,1)}, f32[1,12,512,1]{2,1,3,0:T(8,128)S(1)}, f32[1,512,3072]{2,1,0:T(8,128)}, ...) conditional(s32[]{:T(128)} %convert_element_type.635, ...), branch_computations={%region_8.9_spmd, %region_9.14_spmd} | conditional | flops 8218275328 | bytes 331364768 | solution.py:329
  582.6 17.4 fusion.78
  690.6 29.0 %scatter.71 = f32[2,512,768]{1,0,2:T(2,128)} dynamic-update-slice(f32[2,512,768]{1,0,2:T(2,128)} %copy-done.1, f32[1,512,768]{1,0,2:T(1,128)} %broadcast_select_fusion.3, s32[]{:T(128)} %min.22, s32[]{:T(128)} %constant.1633.clone.1, s32[]{:T(128)} %constant.1633.clone.1) | dynamic-update-slice | bytes 3145732 | tf_op jit(solution)/shard_map/scatter | solution.py:334
  729.8 27.1 %scatter.75 = bf16[2,512,768]{1,0,2:T(2,128)(2,1)} dynamic-update-slice(bf16[2,512,768]{1,0,2:T(2,128)(2,1)} %scatter.65, bf16[1,512,768]{1,0,2:T(2,128)(2,1)} %broadcast_select_fusion.2, s32[]{:T(128)} %min.22, s32[]{:T(128)} %constant.1633.clone.1, s32[]{:T(128)} %constant.1633.clone.1) | dynamic-update-slice | bytes 1572868 | tf_op jit(solution)/shard_map/scatter | solution.py:334
  766.4 9.9 select_dynamic-update-slice_fusion.1
  781.8 25.2 %dynamic_update_slice.25 = f32[2,512,768]{1,0,2:T(2,128)S(1)} dynamic-update-slice(f32[2,512,768]{1,0,2:T(2,128)S(1)} %dynamic_update_slice.24, f32[1,512,768]{1,0,2:T(1,128)} %broadcast_in_dim.483, s32[]{:T(128)} %min.22, s32[]{:T(128)} %constant.1633.clone.1, s32[]{:T(128)} %constant.1633.clone.1) | dynamic-update-slice | bytes 3145732 | tf_op jit(solution)/shard_map/dynamic_update_slice | solution.py:339
  820.2 10.9 conditional.8
  835.2 25.2 %dynamic_update_slice.26 = f32[2,512,768]{1,0,2:T(2,128)S(1)} dynamic-update-slice(f32[2,512,768]{1,0,2:T(2,128)S(1)} %dynamic_update_slice.25, f32[1,512,768]{1,0,2:T(1,128)} %broadcast_in_dim.484, s32[]{:T(128)} %min.23, s32[]{:T(128)} %constant.1633.clone.1, s32[]{:T(128)} %constant.1633.clone.1) | dynamic-update-slice | bytes 3145732 | tf_op jit(solution)/shard_map/dynamic_update_slice | solution.py:339
  863.6 11.8 convert_reduce_fusion.9
  879.7 16.8 multiply_reduce_fusion.23
  918.7 25.4 %scatter.85 = f32[2,512,768]{1,0,2:T(2,128)S(1)} dynamic-update-slice(f32[2,512,768]{1,0,2:T(2,128)S(1)} %copy-done.3, f32[1,512,768]{1,0,2:T(1,128)} %broadcast_select_fusion.1, s32[]{:T(128)} %min.23, s32[]{:T(128)} %constant.1633.clone.1, s32[]{:T(128)} %constant.1633.clone.1) | dynamic-update-slice | bytes 3145732 | tf_op jit(solution)/shard_map/scatter | solution.py:334
  944.1 9.7 select_dynamic-update-slice_fusion
  959.5 27.1 %scatter.89 = bf16[2,512,768]{1,0,2:T(2,128)(2,1)} dynamic-update-slice(bf16[2,512,768]{1,0,2:T(2,128)(2,1)} %scatter.75, bf16[1,512,768]{1,0,2:T(2,128)(2,1)} %broadcast_select_fusion, s32[]{:T(128)} %min.23, s32[]{:T(128)} %constant.1633.clone.1, s32[]{:T(128)} %constant.1633.clone.1) | dynamic-update-slice | bytes 1572868 | tf_op jit(solution)/shard_map/scatter | solution.py:334
  992.8 24.6 %conditional.9 = (f32[512,768]{1,0:T(8,128)}, f32[768,2304]{1,0:T(8,128)}, f32[768,768]{1,0:T(8,128)}, f32[768,3072]{1,0:T(8,128)}, f32[3072,768]{1,0:T(8,128)}, /*index=5*/f32[9984]{0:T(1024)}) conditional(s32[]{:T(128)} %convert_element_type.645, () %tuple.188, (f32[2,512,768]{1,0,2:T(2,128)}, s32[]{:T(128)}, pred[512,768]{1,0:T(8,128)(4,1)S(1)}, ...), branch_computations={%region_30.31_spmd, %region_31.46_spmd} | conditional | flops 16730281984 | bytes 448057792 | solution.py:407
  1021.0 170.8 %collective-permute-done.3 = bf16[512,768]{1,0:T(8,128)(2,1)} collective-permute-done((bf16[512,768]{1,0:T(8,128)(2,1)}, bf16[512,768]{1,0:T(8,128)(2,1)}, u32[]{:S(2)}, u32[]{:S(2)}) %collective-permute-start.3) | collective-permute-done | bytes 786464 | tf_op jit(solution)/shard_map/ppermute | solution.py:32
  1194.3 134.0 %conditional.10 = (f32[512,768]{1,0:T(8,128)}, f32[512,1536]{0,1:T(8,128)}, f32[768,2304]{1,0:T(8,128)}, f32[768,768]{1,0:T(8,128)}, f32[768,3072]{1,0:T(8,128)}, /*index=5*/f32[3072,768]{1,0:T(8,128)}, f32[9984]{0:T(1024)}) conditional(s32[]{:T(128)} %convert_element_type.647, f32[512,1536]{0,1:T(8,128)} %select_n.550, ...), branch_computations={%region_46.47_spmd, %region_47.62_spmd} | conditional | flops 16730281984 | bytes 444912096 | solution.py:407
  1202.9 20.3 convert_reduce_fusion.3
  1299.6 7.4 fusion.305
  1307.1 9.5 fusion.298
  1337.5 128.4 %conditional.11 = (f32[768,2304]{1,0:T(8,128)}, f32[768,768]{1,0:T(8,128)}, f32[768,3072]{1,0:T(8,128)}, f32[3072,768]{1,0:T(8,128)}, f32[9984]{0:T(1024)}, /*index=5*/f32[512,768]{0,1:T(8,128)}) conditional(s32[]{:T(128)} %convert_element_type.650, () %tuple.191, (f32[2,512,768]{1,0,2:T(2,128)}, s32[]{:T(128)}, ...), branch_computations={%region_62.63_spmd, %region_63.78_spmd.clone} | conditional | flops 16730281984 | bytes 465443520 | solution.py:407
  1351.3 20.3 convert_reduce_fusion.6
  1428.4 7.4 fusion.369
  1435.8 9.5 fusion.362
  1465.9 13.9 add_add_fusion.12
  1479.9 12.5 reshape.2090
  1492.3 8.5 copy.585
  1500.9 10.5 add_add_fusion.13
  1526.8 11.3 add_add_fusion.14
  1538.1 8.0 copy.581
  1546.1 9.7 reshape.2084
  1555.8 13.4 copy.582
  1575.4 18.6 maximum_bitcast_fusion.2
  1599.1 25.2 %dynamic_update_slice.27 = f32[2,512,768]{1,0,2:T(2,128)S(1)} dynamic-update-slice(f32[2,512,768]{1,0,2:T(2,128)S(1)} %broadcast.2577, f32[1,512,768]{1,0,2:T(1,128)} %broadcast_in_dim.490, s32[]{:T(128)} %select_n.548, s32[]{:T(128)} %constant.1633.clone.1, s32[]{:T(128)} %constant.1633.clone.1) | dynamic-update-slice | bytes 3145732 | tf_op jit(solution)/shard_map/dynamic_update_slice | solution.py:418
  1634.3 25.2 %dynamic_update_slice.28 = f32[2,512,768]{1,0,2:T(2,128)S(1)} dynamic-update-slice(f32[2,512,768]{1,0,2:T(2,128)S(1)} %dynamic_update_slice.27, f32[1,512,768]{1,0,2:T(1,128)} %broadcast_in_dim.491, s32[]{:T(128)} %select_n.551, s32[]{:T(128)} %constant.1633.clone.1, s32[]{:T(128)} %constant.1633.clone.1) | dynamic-update-slice | bytes 3145732 | tf_op jit(solution)/shard_map/dynamic_update_slice | solution.py:418
  1664.9 25.2 %dynamic_update_slice.29 = f32[2,512,768]{1,0,2:T(2,128)S(1)} dynamic-update-slice(f32[2,512,768]{1,0,2:T(2,128)S(1)} %dynamic_update_slice.28, f32[1,512,768]{1,0,2:T(1,128)} %broadcast_in_dim.492, s32[]{:T(128)} %select_n.552, s32[]{:T(128)} %constant.1633.clone.1, s32[]{:T(128)} %constant.1633.clone.1) | dynamic-update-slice | bytes 3145732 | tf_op jit(solution)/shard_map/dynamic_update_slice | solution.py:418
  1701.1 8.1 copy.593
  1710.2 103.6 %all-reduce.20 = f32[2304]{0:T(1024)S(1)} all-reduce(f32[2304]{0:T(1024)S(1)} %pad_maximum_fusion.10), channel_id=4, replica_groups=mesh['member'=4,'section'=2,'dp'=4] {'section','dp'}, use_global_device_ids=true, to_apply=%region_86.87.clone | all-reduce | flops 2304 | bytes 18432
  1818.8 32.9 %scatter_custom_fusion = f32[50304,96]{1,0:T(8,128)} fusion(s32[4096]{0:T(1024)S(1)} %bitcast.884, f32[4096,96]{1,0:T(8,128)} %bitcast.860, f32[]{:T(128)} %constant.1632.clone.1), kind=kCustom, calls=%fused_computation.702 | custom fusion | flops 393216 | bytes 19317248 | tf_op jit(solution)/shard_map/scatter-add | solution.py:427
  1851.8 23.2 copy.595
  1875.0 12.9 multiply_reduce_fusion.21
  1887.9 271.6 %reduce-scatter.5.cloned.1.call-done = f32[1,12,384,384]{3,2,1,0:T(8,128)} async-done(((f32[1,48,384,384]{3,2,1,0:T(8,128)}), f32[1,12,384,384]{3,2,1,0:T(8,128)}) %reduce-scatter.5.cloned.1.call-update) | async-done | bytes 7077904 | tf_op jit(solution)/shard_map/reduce_scatter | solution.py:432
  2167.5 24.8 %all-reduce.21 = (f32[1]{0:T(128)}, f32[]{:T(128)}) all-reduce(f32[1]{0:T(128)} %bitcast.134, f32[]{:T(128)S(6)} %add.1071), channel_id=1, replica_groups=mesh['member'=4,'section'=2,'dp'=4] {'section','dp'}, use_global_device_ids=true, to_apply=%region_25.26 | all-reduce | flops 2 | bytes 16 | tf_op jit(solution)/shard_map/psum | solution.py:441
  2199.8 17.2 fusion.407
  2217.0 17.9 bitcast_subtract_fusion.9
  2234.9 8.2 copy.596
  2243.1 21.3 bitcast_add_fusion.4
  2264.5 17.9 bitcast_add_fusion.3
  2283.8 46.9 %multiply_subtract_fusion = (f32[96,50304]{1,0:T(8,128)}, f32[96,50304]{1,0:T(8,128)}, f32[96,50304]{1,0:T(8,128)}) fusion(f32[96,50304]{1,0:T(8,128)} %param.68, f32[50304,96]{0,1:T(8,128)} %copy.595, f32[]{:T(128)S(6)} %div.358, f32[96,50304]{1,0:T(8,128)} %param.70, f32[96,50304]{1,0:T(8,128)} %param.69), kind=kLoop, calls=%fused_computation.701 | loop fusion | flops 77266944 | bytes 135217152 | tf_op jit(solution)/shard_map/sub | solution.py:245
  (649 shorter events, 641.8 us)
Async XLA Ops:
  7.2 271.4 %all-gather.2.cloned.1.call-start = ((), (), s32[]{:S(2)}) async-start(), calls=%async_computation.4 | async-start | bytes 17694720 | tf_op jit(solution)/shard_map/all_gather | solution.py:281
  24.2 15.0 copy-start.145
  54.7 18.1 copy-start.114
  72.1 19.3 copy-start.143
  72.2 19.4 copy-start.164
  72.2 75.0 %copy-start.172 = (u32[32]{0:T(128)S(1)}, u32[32]{0:T(128)}, u32[]{:S(2)}) copy-start(u32[32]{0:T(128)} %constant.1711) | copy-start | bytes 388
  72.2 76.2 %copy-start.122 = (f32[1,2496]{1,0:T(1,128)S(1)}, f32[1,2496]{1,0:T(1,128)}, u32[]{:S(2)}) copy-start(f32[1,2496]{1,0:T(1,128)} %param.76) | copy-start | bytes 29956
  72.2 108.4 %copy-start.167 = (s32[4]{0:T(128)S(1)}, s32[4]{0:T(128)}, u32[]{:S(2)}) copy-start(s32[4]{0:T(128)} %constant.1642.clone.1) | copy-start | bytes 52
  72.2 110.0 %copy-start.168 = (s32[3]{0:T(128)S(1)}, s32[3]{0:T(128)}, u32[]{:S(2)}) copy-start(s32[3]{0:T(128)} %constant.1640.clone.1) | copy-start | bytes 40
  73.7 105.5 %all-to-all-start = ((bf16[4,2,512,96]{2,3,1,0:T(8,128)(2,1)}), bf16[4,2,512,96]{2,3,1,0:T(8,128)(2,1)S(1)}, u32[]{:S(2)}, u32[]{:S(2)}) async-start(bf16[4,2,512,96]{2,3,1,0:T(8,128)(2,1)} %broadcast_select_fusion.5), calls=%async_computation | async-start | bytes 1572864 | tf_op jit(solution)/shard_map/all_to_all | solution.py:296
  90.2 1724.2 %reduce-scatter.7.cloned.1.call-start = ((), (), s32[]{:S(2)}) async-start(), calls=%async_computation.6 | async-start | bytes 6389760
  179.2 167.7 %copy-start.118 = (f32[1,3072]{1,0:T(1,128)}, f32[1,3072]{1,0:T(1,128)S(1)}, u32[]{:S(2)}) copy-start(f32[1,3072]{1,0:T(1,128)S(1)} %slice.716) | copy-start | bytes 36868
  179.3 5.0 collective-permute-start
  183.1 163.8 %copy-start.139 = (f32[2304]{0:T(1024)}, f32[2304]{0:T(1024)S(1)}, u32[]{:S(2)}) copy-start(f32[2304]{0:T(1024)S(1)} %slice_reduce_fusion) | copy-start | bytes 27652
  183.7 636.5 %copy-start.147 = (f32[768]{0:T(1024)}, f32[768]{0:T(1024)S(1)}, u32[]{:S(2)}) copy-start(f32[768]{0:T(1024)S(1)} %get-tuple-element.2070) | copy-start | bytes 9220
  183.7 636.5 %copy-start.149 = (f32[768]{0:T(1024)}, f32[768]{0:T(1024)S(1)}, u32[]{:S(2)}) copy-start(f32[768]{0:T(1024)S(1)} %get-tuple-element.2073) | copy-start | bytes 9220
  184.7 162.1 %copy-start.11 = (f32[2,512,768]{1,2,0:T(8,128)}, f32[2,512,768]{1,2,0:T(8,128)S(1)}, u32[]{:S(2)}) copy-start(f32[2,512,768]{1,2,0:T(8,128)S(1)} %maximum_convert_fusion) | copy-start | bytes 9437188
  354.1 24.3 %copy-start.33 = (f32[512,768]{1,0:T(8,128)}, f32[512,768]{1,0:T(8,128)S(1)}, u32[]{:S(2)}) copy-start(f32[512,768]{1,0:T(8,128)S(1)} %get-tuple-element.2082) | copy-start | bytes 4718596 | tf_op jit(solution)/shard_map/cond
  360.0 18.4 copy-start.73
  507.9 63.1 %collective-permute-start.1 = (bf16[512,768]{1,0:T(8,128)(2,1)}, bf16[512,768]{1,0:T(8,128)(2,1)}, u32[]{:S(2)}, u32[]{:S(2)}) collective-permute-start(bf16[512,768]{1,0:T(8,128)(2,1)} %convert_element_type.636), channel_id=1, source_target_pairs={{0,4},{1,5},{2,6},{3,7},{8,12},{9,13},{10,14},{11,15},{16,20},{17,... | collective-permute-start | bytes 2359304 | tf_op jit(solution)/shard_map/ppermute | solution.py:32
  578.7 21.3 copy-start.31
  582.6 17.5 copy-start.63
  582.6 17.4 copy-start.74
  766.4 12.0 copy-start.64
  766.4 12.0 copy-start.65
  776.3 41.5 %collective-permute-start.2 = (bf16[512,768]{1,0:T(8,128)(2,1)}, bf16[512,768]{1,0:T(8,128)(2,1)}, u32[]{:S(2)}, u32[]{:S(2)}) collective-permute-start(bf16[512,768]{1,0:T(8,128)(2,1)} %convert_element_type.639), channel_id=1, source_target_pairs={{0,4},{1,5},{2,6},{3,7},{8,12},{9,13},{10,14},{11,15},{16,20},{17,... | collective-permute-start | bytes 2359304 | tf_op jit(solution)/shard_map/ppermute | solution.py:32
  863.0 12.4 copy-start.161
  878.0 18.5 copy-start.125
  878.0 18.5 copy-start.121
  1019.7 172.1 %collective-permute-start.3 = (bf16[512,768]{1,0:T(8,128)(2,1)}, bf16[512,768]{1,0:T(8,128)(2,1)}, u32[]{:S(2)}, u32[]{:S(2)}) collective-permute-start(bf16[512,768]{1,0:T(8,128)(2,1)} %convert_element_type.648), channel_id=1, source_target_pairs={{4,0},{5,1},{6,2},{7,3},{12,8},{13,9},{14,10},{15,11},{20,16},{21,... | collective-permute-start | bytes 2359304 | tf_op jit(solution)/shard_map/ppermute | solution.py:32
  1200.0 23.2 slice-start.17
  1202.9 20.3 copy-start.52
  1202.9 20.3 slice-start.18
  1268.9 16.8 copy-start.84
  1307.1 12.1 copy-start.133
  1307.1 18.0 copy-start.127
  1330.6 4.5 collective-permute-start.4
  1348.8 22.7 slice-start.19
  1351.2 23.0 copy-start.54
  1351.3 20.3 slice-start.20
  1374.2 34.1 %copy-start.59 = (f32[512,768]{1,0:T(8,128)}, f32[512,768]{1,0:T(8,128)S(1)}, u32[]{:S(2)}) copy-start(f32[512,768]{1,0:T(8,128)S(1)} %fusion.464) | copy-start | bytes 4718596 | tf_op jit(solution)/shard_map/cond
  1403.0 12.7 copy-start.85
  1415.7 12.7 copy-start.130
  1445.3 11.6 copy-start.128
  1445.3 12.9 copy-start.138
  1445.3 14.1 copy-start.22
  1445.3 14.1 copy-start.24
  1445.3 14.1 copy-start.44
  1445.3 14.1 copy-start.60
  1445.3 14.1 copy-start.129
  1445.4 14.1 copy-start.131
  1575.4 584.1 %reduce-scatter.5.cloned.1.call-start = ((), (), s32[]{:S(2)}) async-start(), calls=%async_computation.5 | async-start | bytes 35389440 | tf_op jit(solution)/shard_map/reduce_scatter | solution.py:432
  1690.6 4.3 collective-permute-start.5
  1697.1 119.7 %all-to-all-start.1 = ((f32[1,2,512,384]{2,1,0,3:T(2,128)}), f32[1,2,512,384]{2,1,0,3:T(2,128)S(1)}, u32[]{:S(2)}, u32[]{:S(2)}) async-start(f32[1,2,512,384]{2,1,0,3:T(2,128)} %fusion.421), calls=%async_computation.2 | async-start | bytes 3145728 | tf_op jit(solution)/shard_map/all_to_all | solution.py:425
  2193.1 23.9 %slice-start.2 = ((s8[7077888]{0:T(1024)(128)(4,1)}), s8[4194304]{0:T(1024)(128)(4,1)S(1)}, s32[]{:S(2)}) async-start(s8[7077888]{0:T(1024)(128)(4,1)} %bitcast.738), calls=%async_computation.9 | async-start | bytes 8388608
  2199.8 17.2 slice-start.3
  2234.9 29.5 %slice-start = ((s8[7077888]{0:T(1024)(128)(4,1)}), s8[2883584]{0:T(1024)(128)(4,1)S(1)}, s32[]{:S(2)}) async-start(s8[7077888]{0:T(1024)(128)(4,1)} %bitcast.729), calls=%async_computation.7 | async-start | bytes 5767168
  2243.1 21.3 slice-start.1
  2264.4 18.0 copy-start.123
  2264.4 17.9 copy-start.141
  2264.4 17.9 copy-start.142
  2264.5 18.6 copy-start.144
  2264.5 18.6 copy-start.162
  2264.5 18.6 copy-start.163
  (98 other events, 455.6 us)
Sparse Core Ops, SparseCore 0:
  12.7 265.8 all-gather.1
  1575.5 89.7 reduce-scatter.6
  1667.7 491.7 reduce-scatter.4
where the time goes:
time: 2370 us; the launch traced here: 2340 us
  local copies, waits for them, and re-layouts  781 us (33%)
  waiting for transfers between devices  542 us (23%)
  other arithmetic  421 us (18%)
  matrix products  292 us (12%)
  blocking collectives  228 us (10%)
  starting transfers between devices  30.2 us (1%)
  between operations  24.6 us (1%)
    reduce_scatter x1, waiting for transfers between devices, local(): lax.psum_scatter(grad_blocks[None], 'dp', scatter_dimension=1, tiled=True)  272 us
    unnamed x3, blocking collectives  187 us
    ppermute x6, waiting for transfers between devices, passed_along(): return lax.ppermute(block, axis, route)  177 us
    scatter x6, local copies, waits for them, and re-layouts, local(): store.at[slot_index].set(item)  161 us
    all_gather x1, waiting for transfers between devices, local(): lax.all_gather(layer_blocks.astype(jnp.bfloat16), 'dp', axis=1, tiled=True)  93.8 us
    dynamic_update_slice x3, local copies, waits for them, and re-layouts, local(): lax.dynamic_update_slice(embed_grads, jnp.where(active, grad_in, previous...  75.7 us
    dynamic_update_slice x3, local copies, waits for them, and re-layouts, local(): lax.dynamic_update_slice(finals, jnp.where(active, output, previous_final...  75.6 us
    another operation x22, local copies, waits for them, and re-layouts  62.7 us
  transfers between devices with their start and end apart: 11, of which 5 were waited for; matrix products, arithmetic and copies ran while one was open for 15% of the time, Pallas kernels for 0%

commit v1 on v0

v1 whole, which is shorter than its diff:
```python
import functools
import math

import jax
import jax.numpy as jnp
from jax import lax
from jax.experimental import pallas as pl
from jax.experimental.pallas import tpu as pltpu
from jax.sharding import PartitionSpec as P

D = 768
HEADS = 12
HEAD = 64
ROT = 16
FF = 3072
STEP = 10
TILE = 384
PAIR = 2 * HEAD
QROWS = 256
CHUNK = 768

norm_eps = 1e-05
beta_first = 0.9
beta_second = 0.999
adam_eps = 1e-08
clip_limit = 1.0
embed_rate = 0.2
embed_decay = 0.01
vector_rate = 0.5
shampoo_rate = 0.1
stats_decay = 0.95
rope_base = 10000.0

f32 = jnp.float32
bf16 = jnp.bfloat16
VMEM_LIMIT = 60 * 2**20

COL_A, COL_O, COL_B, COL_H = 0, D, 2 * D, 3 * D
COL_QKV = 3 * D + FF
COL_GP = COL_QKV + 3 * D
COL_X = COL_GP + FF
KEPT = COL_X + D
COL_DP, COL_G, COL_DH = 0, 3 * D, 4 * D
GRADS = 4 * D + FF

V_G1, V_C1, V_G2, V_C2, V_QKV, V_O = 0, D, 2 * D, 3 * D, 4 * D, 7 * D
V_B1, V_B2, V_END = 8 * D, 8 * D + FF, 9 * D + FF


def block_places():
    places = []
    for matrix, (rows, cols) in enumerate(((D, 3 * D), (D, D), (D, FF), (FF, D))):
        for row in range(rows // TILE):
            for col in range(cols // TILE):
                places.append((matrix, row, col))
    return places


PLACES = block_places()


def nt(a, b):
    return lax.dot_general(a, b, (((1,), (1,)), ((), ())), preferred_element_type=f32)


def tn(a, b):
    return lax.dot_general(a, b, (((0,), (0,)), ((), ())), preferred_element_type=f32)


def nn(a, b):
    return lax.dot_general(a, b, (((1,), (0,)), ((), ())), preferred_element_type=f32)


def normalized(x):
    mean = jnp.mean(x, axis=-1, keepdims=True)
    centred = x - mean
    spread = jnp.mean(centred * centred, axis=-1, keepdims=True)
    scale = lax.rsqrt(spread + norm_eps)
    return centred * scale, scale


def norm_back(grad, gain, hat, scale):
    inner = grad * gain
    first = jnp.mean(inner, axis=-1, keepdims=True)
    second = jnp.mean(inner * hat, axis=-1, keepdims=True)
    return scale * (inner - first - hat * second)


def gelu_both(h):
    expo = jnp.exp(-0.5 * h * h)
    t = 1.0 / (1.0 + (0.3275911 * math.sqrt(0.5)) * jnp.abs(h))
    poly = 0.5 * 1.061405429
    for coef in (-1.453152027, 1.421413741, -0.284496736, 0.254829592):
        poly = poly * t + 0.5 * coef
    tail = poly * t * expo
    cdf = jnp.where(h >= 0.0, 1.0 - tail, tail)
    return h * cdf, cdf + h * expo * (1.0 / math.sqrt(2.0 * math.pi))


def head_masks(value):
    lane = lax.broadcasted_iota(jnp.int32, (1, PAIR), 1)
    return [
        jnp.where(lane < HEAD, value, 0.0).astype(bf16),
        jnp.where(lane < HEAD, 0.0, value).astype(bf16),
    ]


def weight_copies(shards, mats, sems):
    per = shards[0].shape[0]
    copies = []
    for index, (matrix, row, col) in enumerate(PLACES):
        copies.append(
            (
                matrix,
                pltpu.make_async_copy(
                    shards[index // per].at[index % per],
                    mats[matrix].at[pl.ds(row * TILE, TILE), pl.ds(col * TILE, TILE)],
                    sems.at[index],
                ),
            )
        )
    return copies


def wait_for(copies, matrix):
    for which, copy in copies:
        if which == matrix:
            copy.wait()


def forward_kernel(shard_count, first, *refs):
    slot_ref, x_ref, vec_ref, fin_ref, cos_ref, sa_ref, sb_ref = refs[:7]
    shards = refs[7 : 7 + shard_count]
    rest = refs[7 + shard_count + (0 if first else 3) :]
    xb_ref, red_ref, kept_out, xo_out, lse_out = rest[:5]
    wqkv, wo, w1, w2, kept, xo, lse, wsem, osem = rest[5:]
    mats = (wqkv, wo, w1, w2)
    length = x_ref.shape[0]
    slot = slot_ref[0]
    copies = weight_copies(shards, mats, wsem)
    for _, copy in copies:
        copy.start()

    stores = []

    def store(index, start, width):
        copy = pltpu.make_async_copy(
            kept.at[:, pl.ds(start, width)],
            kept_out.at[slot, :, pl.ds(start, width)],
            osem.at[index],
        )
        copy.start()
        stores.append(copy)

    hat, _ = normalized(x_ref[...].astype(f32))
    kept[:, COL_X : COL_X + D] = x_ref[...]
    kept[:, COL_A : COL_A + D] = (hat * vec_ref[:, V_G1 : V_G1 + D] + vec_ref[:, V_C1 : V_C1 + D]).astype(bf16)
    kept[:, COL_B : COL_B + D] = (hat * vec_ref[:, V_G2 : V_G2 + D] + vec_ref[:, V_C2 : V_C2 + D]).astype(bf16)
    wait_for(copies, 0)
    for part in range(3):
        at = part * D
        proj = nn(kept[:, COL_A : COL_A + D], wqkv[:, at : at + D])
        proj = proj + vec_ref[:, V_QKV + at : V_QKV + at + D]
        if part == 2:
            kept[:, COL_QKV + at : COL_QKV + at + D] = proj.astype(bf16)
        else:
            for p in range(D // PAIR):
                u = proj[:, p * PAIR : (p + 1) * PAIR]
                turned = (
                    u * cos_ref[...]
                    + pltpu.roll(u, PAIR - ROT // 2, 1) * sa_ref[...]
                    + pltpu.roll(u, ROT // 2, 1) * sb_ref[...]
                )
                kept[:, COL_QKV + at + p * PAIR : COL_QKV + at + (p + 1) * PAIR] = turned.astype(bf16)
    store(0, COL_QKV, 3 * D)
    store(1, COL_X, D)

    scales = head_masks(1.0 / math.sqrt(HEAD))
    lane = lax.broadcasted_iota(jnp.int32, (1, PAIR), 1)
    lse[...] = jnp.zeros_like(lse)
    q_at = lax.broadcasted_iota(jnp.int32, (QROWS, QROWS), 0)
    k_at = lax.broadcasted_iota(jnp.int32, (QROWS, QROWS), 1)

    def attend(p, carry):
        lanes = pl.multiple_of(p * PAIR, PAIR)
        for tile in range(length // QROWS):
            rows = pl.ds(tile * QROWS, QROWS)
            keys = (tile + 1) * QROWS
            q = kept[rows, pl.ds(COL_QKV + lanes, PAIR)]
            k = kept[pl.ds(0, keys), pl.ds(COL_QKV + D + lanes, PAIR)]
            v = kept[pl.ds(0, keys), pl.ds(COL_QKV + 2 * D + lanes, PAIR)]
            outs = []
            for side in range(2):
                s = nt(q * scales[side], k)
                near = jnp.where(k_at <= q_at, s[:, keys - QROWS :], -1e30)
                s = jnp.concatenate([s[:, : keys - QROWS], near], axis=1) if tile else near
                peak = jnp.max(s, axis=1, keepdims=True)
                expo = jnp.exp(s - peak)
                total = jnp.sum(expo, axis=1, keepdims=True)
                soft = (expo * (1.0 / total)).astype(bf16)
                outs.append(nn(soft, v))
                log_total = peak + jnp.log(total)
                lse[rows, :] = jnp.where(lane == 2 * p + side, log_total, lse[rows, :])
            mixed = jnp.where(lane < HEAD, outs[0], outs[1])
            kept[rows, pl.ds(COL_O + lanes, PAIR)] = mixed.astype(bf16)
        return carry

    lax.fori_loop(0, HEADS // 2, attend, 0)
    wait_for(copies, 1)
    out = x_ref[...].astype(f32) + (nn(kept[:, COL_O : COL_O + D], wo[...]) + vec_ref[:, V_O : V_O + D])
    store(2, COL_A, 3 * D)
    wait_for(copies, 2)
    wait_for(copies, 3)
    branch = jnp.zeros((length, D), f32) + vec_ref[:, V_B2 : V_B2 + D]
    for c in range(0, FF, CHUNK):
        h = nn(kept[:, COL_B : COL_B + D], w1[:, c : c + CHUNK]) + vec_ref[:, V_B1 + c : V_B1 + c + CHUNK]
        act, slope = gelu_both(h)
        kept[:, COL_H + c : COL_H + c + CHUNK] = act.astype(bf16)
        kept[:, COL_GP + c : COL_GP + c + CHUNK] = slope.astype(bf16)
        branch = branch + nn(kept[:, COL_H + c : COL_H + c + CHUNK], w2[c : c + CHUNK, :])
    store(3, COL_H, FF)
    store(4, COL_GP, FF)
    out = out + branch
    xo[...] = out
    xb_ref[...] = out.astype(bf16)
    tails = [
        pltpu.make_async_copy(xo, xo_out.at[slot], osem.at[5]),
        pltpu.make_async_copy(lse, lse_out.at[slot], osem.at[6]),
    ]
    for copy in tails:
        copy.start()
    hat, _ = normalized(out)
    final = (hat * fin_ref[:, :D] + fin_ref[:, D : 2 * D]).astype(bf16)
    red_ref[0:1, :] = jnp.sum(hat, axis=0, keepdims=True)
    red_ref[1:2, :] = jnp.sum(final.astype(f32), axis=0, keepdims=True)
    red_ref[2:8, :] = jnp.zeros((6, D), f32)
    for copy in stores + tails:
        copy.wait()


def forward(slot, x, vec, fin, tables, shards, state, slots):
    length = x.shape[0]
    count = len(shards)
    first = state is None
    whole = pl.BlockSpec(memory_space=pltpu.VMEM)
    anywhere = pl.BlockSpec(memory_space=pl.ANY)
    kept_shape = (
        jax.ShapeDtypeStruct((slots, length, KEPT), bf16),
        jax.ShapeDtypeStruct((slots, length, D), f32),
        jax.ShapeDtypeStruct((slots, length, PAIR), f32),
    )
    operands = [slot, x, vec, fin, *tables, *shards] + ([] if first else list(state))
    return pl.pallas_call(
        functools.partial(forward_kernel, count, first),
        out_shape=(
            jax.ShapeDtypeStruct((length, D), bf16),
            jax.ShapeDtypeStruct((8, D), f32),
            *kept_shape,
        ),
        in_specs=[pl.BlockSpec(memory_space=pltpu.SMEM)]
        + [whole] * 6
        + [anywhere] * (len(operands) - 7),
        out_specs=(whole, whole, anywhere, anywhere, anywhere),
        input_output_aliases={} if first else {7 + count + i: 2 + i for i in range(3)},
        scratch_shapes=[
            pltpu.VMEM((D, 3 * D), bf16),
            pltpu.VMEM((D, D), bf16),
            pltpu.VMEM((D, FF), bf16),
            pltpu.VMEM((FF, D), bf16),
            pltpu.VMEM((length, KEPT), bf16),
            pltpu.VMEM((length, D), f32),
            pltpu.VMEM((length, PAIR), f32),
            pltpu.SemaphoreType.DMA((len(PLACES),)),
            pltpu.SemaphoreType.DMA((7,)),
        ],
        compiler_params=pltpu.CompilerParams(vmem_limit_bytes=VMEM_LIMIT),
        cost_estimate=pl.CostEstimate(flops=10 * 10**9, bytes_accessed=30 * 10**6, transcendentals=5 * 10**6),
        name="layer_forward",
    )(*operands)


def backward_kernel(shard_count, *refs):
    slot_ref, flag_ref, recv_ref, vec_ref, fin_ref, cos_ref, sa_ref, sb_ref = refs[:8]
    shards = refs[8 : 8 + shard_count]
    kept_in, xo_in, lse_in = refs[8 + shard_count : 11 + shard_count]
    rest = refs[11 + shard_count :]
    dx_ref, vg_ref, kept_out = rest[:3]
    wqkv, wo, w1, w2, qkv, gp, x, xo, lse, grads, dmix, dq, dk, dv, wsem, isem, osem = rest[3:]
    mats = (wqkv, wo, w1, w2)
    length = recv_ref.shape[0]
    slot = slot_ref[0]
    copies = weight_copies(shards, mats, wsem)
    loads = [
        pltpu.make_async_copy(xo_in.at[slot], xo, isem.at[0]),
        pltpu.make_async_copy(kept_in.at[slot, :, pl.ds(COL_GP, FF)], gp, isem.at[1]),
        pltpu.make_async_copy(kept_in.at[slot, :, pl.ds(COL_X, D)], x, isem.at[2]),
        pltpu.make_async_copy(kept_in.at[slot, :, pl.ds(COL_QKV, 3 * D)], qkv, isem.at[3]),
        pltpu.make_async_copy(lse_in.at[slot], lse, isem.at[4]),
    ]
    loads[0].start()
    for which, copy in copies:
        if which == 3:
            copy.start()
    loads[1].start()
    loads[2].start()
    for which, copy in copies:
        if which == 2:
            copy.start()
    loads[3].start()
    loads[4].start()
    for which, copy in copies:
        if which < 2:
            copy.start()

    loads[0].wait()
    hat, scale = normalized(xo[...])
    weight = fin_ref[:, 2 * D : 3 * D] * fin_ref[:, :D]
    top = flag_ref[0] * norm_back(1.0, weight, hat, scale)
    use_top = flag_ref[1] > 0.5
    xo[...] = jnp.where(use_top, top, recv_ref[...].astype(f32))
    grads[:, COL_G : COL_G + D] = xo[...].astype(bf16)
    bias = jnp.sum(grads[:, COL_G : COL_G + D].astype(f32), axis=0, keepdims=True)
    vg_ref[:, V_O : V_O + D] = bias
    vg_ref[:, V_B2 : V_B2 + D] = bias

    wait_for(copies, 3)
    loads[1].wait()
    loads[2].wait()
    wait_for(copies, 2)
    second = jnp.zeros((length, D), f32)
    for c in range(0, FF, CHUNK):
        act = nt(grads[:, COL_G : COL_G + D], w2[c : c + CHUNK, :])
        pre = (act * gp[:, c : c + CHUNK].astype(f32)).astype(bf16)
        grads[:, COL_DH + c : COL_DH + c + CHUNK] = pre
        vg_ref[:, V_B1 + c : V_B1 + c + CHUNK] = jnp.sum(pre.astype(f32), axis=0, keepdims=True)
        second = second + nt(pre, w1[:, c : c + CHUNK])
    hat, scale = normalized(x[...].astype(f32))
    vg_ref[:, V_G2 : V_G2 + D] = jnp.sum(second * hat, axis=0, keepdims=True)
    vg_ref[:, V_C2 : V_C2 + D] = jnp.sum(second, axis=0, keepdims=True)
    xo[...] = xo[...] + norm_back(second, vec_ref[:, V_G2 : V_G2 + D], hat, scale)
    stores = [
        pltpu.make_async_copy(
            grads.at[:, pl.ds(COL_G, D)], kept_out.at[slot, :, pl.ds(COL_X, D)], osem.at[0]
        ),
        pltpu.make_async_copy(
            grads.at[:, pl.ds(COL_DH, FF)], kept_out.at[slot, :, pl.ds(COL_GP, FF)], osem.at[1]
        ),
    ]
    stores[0].start()
    stores[1].start()

    wait_for(copies, 1)
    dmix[...] = nt(grads[:, COL_G : COL_G + D], wo[...]).astype(bf16)
    loads[3].wait()
    loads[4].wait()
    lse_rows = jnp.transpose(lse[...])
    lse[0:PAIR, :] = lse_rows[:, 0:PAIR]
    for part in range(1, length // PAIR):
        lse[part * PAIR : (part + 1) * PAIR, :] = lse_rows[:, part * PAIR : (part + 1) * PAIR]
    scales = head_masks(1.0 / math.sqrt(HEAD))
    ones = head_masks(1.0)
    k_at = lax.broadcasted_iota(jnp.int32, (QROWS, QROWS), 0)
    q_at = lax.broadcasted_iota(jnp.int32, (QROWS, QROWS), 1)

    def attend(p, carry):
        lanes = pl.multiple_of(p * PAIR, PAIR)
        for tile in range(length // QROWS):
            rows = pl.ds(tile * QROWS, QROWS)
            keys = (tile + 1) * QROWS
            q = qkv[rows, pl.ds(lanes, PAIR)]
            k = qkv[pl.ds(0, keys), pl.ds(D + lanes, PAIR)]
            v = qkv[pl.ds(0, keys), pl.ds(2 * D + lanes, PAIR)]
            dm = dmix[rows, pl.ds(lanes, PAIR)]
            dq_sum = dk_sum = dv_sum = None
            for side in range(2):
                qs = q * scales[side]
                ks = k * scales[side]
                dms = dm * ones[side]
                s = nt(k, qs)
                row = jnp.concatenate(
                    [
                        lse[pl.ds(part * PAIR + 2 * p + side, 1), :]
                        for part in range(tile * QROWS // PAIR, (tile + 1) * QROWS // PAIR)
                    ],
                    axis=1,
                )
                soft = jnp.exp(s - row)
                near = jnp.where(k_at <= q_at, soft[keys - QROWS :, :], 0.0)
                soft = jnp.concatenate([soft[: keys - QROWS, :], near], axis=0) if tile else near
                dsoft = nt(v, dms)
                centre = jnp.sum(soft * dsoft, axis=0, keepdims=True)
                ds = (soft * (dsoft - centre)).astype(bf16)
                one_dv = nn(soft.astype(bf16), dms)
                one_dk = nn(ds, qs)
                one_dq = tn(ds, ks)
                if side:
                    dq_sum, dk_sum, dv_sum = dq_sum + one_dq, dk_sum + one_dk, dv_sum + one_dv
                else:
                    dq_sum, dk_sum, dv_sum = one_dq, one_dk, one_dv
            dq[rows, :] = dq_sum
            if tile:
                old = pl.ds(0, tile * QROWS)
                new = pl.ds(tile * QROWS, QROWS)
                dk[old, :] = dk[old, :] + dk_sum[: tile * QROWS]
                dk[new, :] = dk_sum[tile * QROWS :]
                dv[old, :] = dv[old, :] + dv_sum[: tile * QROWS]
                dv[new, :] = dv_sum[tile * QROWS :]
            else:
                dk[rows, :] = dk_sum
                dv[rows, :] = dv_sum
        for part, ref in ((0, dq), (1, dk)):
            g = ref[...]
            turned = (
                g * cos_ref[...]
                - pltpu.roll(g, PAIR - ROT // 2, 1) * sa_ref[...]
                - pltpu.roll(g, ROT // 2, 1) * sb_ref[...]
            )
            grads[:, pl.ds(COL_DP + part * D + lanes, PAIR)] = turned.astype(bf16)
        grads[:, pl.ds(COL_DP + 2 * D + lanes, PAIR)] = dv[...].astype(bf16)
        return carry

    lax.fori_loop(0, HEADS // 2, attend, 0)
    stores.append(
        pltpu.make_async_copy(
            grads.at[:, pl.ds(COL_DP, 3 * D)], kept_out.at[slot, :, pl.ds(COL_QKV, 3 * D)], osem.at[2]
        )
    )
    stores[2].start()
    vg_ref[:, V_QKV : V_QKV + 3 * D] = jnp.sum(
        grads[:, COL_DP : COL_DP + 3 * D].astype(f32), axis=0, keepdims=True
    )
    wait_for(copies, 0)
    one = nt(grads[:, COL_DP : COL_DP + 3 * D], wqkv[...])
    hat, scale = normalized(x[...].astype(f32))
    vg_ref[:, V_G1 : V_G1 + D] = jnp.sum(one * hat, axis=0, keepdims=True)
    vg_ref[:, V_C1 : V_C1 + D] = jnp.sum(one, axis=0, keepdims=True)
    total = xo[...] + norm_back(one, vec_ref[:, V_G1 : V_G1 + D], hat, scale)
    dx_ref[...] = total.astype(bf16)
    for copy in stores:
        copy.wait()


def backward(slot, flags, recv, vec, fin, tables, shards, state):
    length = recv.shape[0]
    count = len(shards)
    whole = pl.BlockSpec(memory_space=pltpu.VMEM)
    anywhere = pl.BlockSpec(memory_space=pl.ANY)
    small = pl.BlockSpec(memory_space=pltpu.SMEM)
    operands = [slot, flags, recv, vec, fin, *tables, *shards, *state]
    return pl.pallas_call(
        functools.partial(backward_kernel, count),
        out_shape=(
            jax.ShapeDtypeStruct((length, D), bf16),
            jax.ShapeDtypeStruct((1, V_END), f32),
            jax.ShapeDtypeStruct(state[0].shape, bf16),
        ),
        in_specs=[small, small] + [whole] * 6 + [anywhere] * (len(operands) - 8),
        out_specs=(whole, whole, anywhere),
        input_output_aliases={8 + count: 2},
        scratch_shapes=[
            pltpu.VMEM((D, 3 * D), bf16),
            pltpu.VMEM((D, D), bf16),
            pltpu.VMEM((D, FF), bf16),
            pltpu.VMEM((FF, D), bf16),
            pltpu.VMEM((length, 3 * D), bf16),
            pltpu.VMEM((length, FF), bf16),
            pltpu.VMEM((length, D), bf16),
            pltpu.VMEM((length, D), f32),
            pltpu.VMEM((length, PAIR), f32),
            pltpu.VMEM((length, GRADS), bf16),
            pltpu.VMEM((length, D), bf16),
            pltpu.VMEM((length, PAIR), f32),
            pltpu.VMEM((length, PAIR), f32),
            pltpu.VMEM((length, PAIR), f32),
            pltpu.SemaphoreType.DMA((len(PLACES),)),
            pltpu.SemaphoreType.DMA((5,)),
            pltpu.SemaphoreType.DMA((3,)),
        ],
        compiler_params=pltpu.CompilerParams(vmem_limit_bytes=VMEM_LIMIT),
        cost_estimate=pl.CostEstimate(flops=20 * 10**9, bytes_accessed=40 * 10**6, transcendentals=5 * 10**6),
        name="layer_backward",
    )(*operands)


def product_kernel(left_at, right_at, x_ref, y_ref, out_ref):
    units, rows, width = x_ref.shape
    x = x_ref[...].reshape(units * rows, width)
    y = y_ref[...].reshape(units * rows, width)
    out_ref[0] = tn(x, y)


def products(left_at, right_at, kept, units):
    count = left_at.shape[0]
    length = kept.shape[1]
    return pl.pallas_call(
        product_kernel,
        out_shape=jax.ShapeDtypeStruct((count, TILE, TILE), f32),
        grid_spec=pltpu.PrefetchScalarGridSpec(
            num_scalar_prefetch=2,
            grid=(count,),
            in_specs=[
                pl.BlockSpec((units, length, TILE), lambda i, a, b: (0, 0, a[i])),
                pl.BlockSpec((units, length, TILE), lambda i, a, b: (0, 0, b[i])),
            ],
            out_specs=pl.BlockSpec((1, TILE, TILE), lambda i, a, b: (i, 0, 0)),
        ),
        compiler_params=pltpu.CompilerParams(vmem_limit_bytes=VMEM_LIMIT),
        cost_estimate=pl.CostEstimate(
            flops=2 * count * TILE * TILE * units * length,
            bytes_accessed=count * TILE * (4 * units * length + 4 * TILE),
            transcendentals=0,
        ),
        name="weight_products",
    )(left_at, right_at, kept, kept)


def split(value):
    high = value.astype(bf16)
    return high, (value - high.astype(f32)).astype(bf16)


def shampoo_kernel(factor_ref, g_ref, w_ref, ls_ref, rs_ref, lr_ref, rr_ref, bg_ref, nw_ref, nl_ref, nr_ref):
    factor = factor_ref[0]
    g = g_ref[0]
    bg_ref[0] = g.astype(f32) * factor
    level = (1.0 - stats_decay) * factor * factor
    nl_ref[0] = stats_decay * ls_ref[0] + level * nt(g, g)
    nr_ref[0] = stats_decay * rs_ref[0] + level * tn(g, g)
    right_high, right_low = split(rr_ref[0])
    inner = nn(g, right_high) + nn(g, right_low)
    inner_high, inner_low = split(inner)
    left_high, left_low = split(lr_ref[0])
    direction = nn(left_high, inner_high) + (nn(left_high, inner_low) + nn(left_low, inner_high))
    nw_ref[0] = w_ref[0] - (shampoo_rate * factor) * direction


def shampoo(factor, grad, weights, left_stats, right_stats, left_root, right_root):
    count = grad.shape[0]
    block = pl.BlockSpec((1, TILE, TILE), lambda i: (i, 0, 0))
    shape = jax.ShapeDtypeStruct((count, TILE, TILE), f32)
    return pl.pallas_call(
        shampoo_kernel,
        out_shape=(shape,) * 4,
        grid=(count,),
        in_specs=[pl.BlockSpec(memory_space=pltpu.SMEM)] + [block] * 6,
        out_specs=(block,) * 4,
        compiler_params=pltpu.CompilerParams(vmem_limit_bytes=VMEM_LIMIT),
        cost_estimate=pl.CostEstimate(
            flops=14 * count * TILE**3, bytes_accessed=38 * count * TILE * TILE, transcendentals=0
        ),
        name="shampoo",
    )(factor, grad, weights, left_stats, right_stats, left_root, right_root)


def rope_columns(length):
    half_rot = ROT // 2
    lanes = jnp.arange(PAIR) % HEAD
    index = jnp.where(lanes < half_rot, lanes, lanes - half_rot).astype(f32)
    inverse = rope_base ** (-2.0 * index / ROT)
    angles = jnp.arange(length)[:, None].astype(f32) * inverse[None, :]
    cosine = jnp.where(lanes < ROT, jnp.cos(angles), 1.0)
    sine = jnp.where(lanes < ROT, jnp.sin(angles), 0.0)
    first = jnp.where(lanes < half_rot, -sine, 0.0)
    second = jnp.where(lanes < half_rot, 0.0, sine)
    return cosine, first, second


def adam_step(weight, moment, second, grad, rate, decay):
    moment_new = beta_first * moment + (1.0 - beta_first) * grad
    second_new = beta_second * second + (1.0 - beta_second) * grad * grad
    corrected = moment_new / (1.0 - beta_first**STEP)
    scaled = jnp.sqrt(second_new / (1.0 - beta_second**STEP)) + adam_eps
    return (moment_new, second_new, weight - rate * (corrected / scaled + decay * weight))


def rounded(values):
    return lax.reduce_precision(values, 8, 7)


def chosen(flags, values):
    total = values[-1]
    for flag, value in zip(flags[:-1], values[:-1]):
        total = jnp.where(flag, value, total)
    return total


def ordered(section, mine, other, axis):
    return jnp.concatenate(
        [jnp.where(section == 0, mine, other), jnp.where(section == 0, other, mine)], axis=axis
    )


def swapped(value):
    return lax.ppermute(value, "section", [(0, 1), (1, 0)])


def local(
    tokens,
    margins,
    tie_flags,
    embedding,
    embed_moment,
    embed_second,
    layer_blocks,
    left_stats,
    right_stats,
    left_root,
    right_root,
    layer_vectors,
    vector_moment,
    vector_second,
    closing_vectors,
    final_moment,
    final_second,
):
    both = ("section", "dp")
    count = lax.axis_size("dp")
    section = lax.axis_index("section")
    place = lax.axis_index("dp")
    low, high = count // 2 - 1, count // 2
    is_high = place >= high
    length = tokens.shape[2]
    units = tokens.shape[0] * count
    own_blocks = layer_blocks.shape[1]
    own_vector = layer_vectors.shape[1]
    own_final = closing_vectors.shape[0]
    features, vocab = embedding.shape

    own = layer_blocks[0].astype(bf16)
    shards = [None] * count
    order_low = list(range(count - 1, low, -1)) + list(range(low + 1))
    order_high = [count - 1 - k for k in order_low]
    for k in order_low:
        direct = lax.ppermute(own, both, [(k, low), (count + k, count + high)])
        relayed = lax.ppermute(direct, both, [(low, count + low), (count + high, high)])
        shards[k] = jnp.where((section == 1) == is_high, direct, relayed)

    pack = jnp.concatenate(
        [
            tokens.reshape(-1).astype(f32),
            margins.astype(f32),
            tie_flags.astype(f32),
            rounded(layer_vectors[0]),
            rounded(closing_vectors),
        ]
    )
    packs = lax.all_gather(pack, both, axis=0, tiled=False).reshape(2, count, -1)
    at = tokens.size
    ids = packs[0, :, :at].astype(jnp.int32).reshape(-1)
    pair_margins = packs[0, :, at : at + margins.size].reshape(-1)
    at = at + margins.size
    pair_ties = packs[0, :, at : at + margins.size].reshape(-1)
    at = at + margins.size
    layer_all = packs[:, :, at : at + own_vector].reshape(2, -1)
    vec = jnp.where(is_high, layer_all[1], layer_all[0])[None]
    fin = packs[:, :, at + own_vector :].reshape(1, -1)
    tables = rope_columns(length)

    looked = jnp.take(embedding.astype(bf16), ids, axis=1)
    half = jnp.concatenate([lax.ppermute(looked, "dp", [(k, low)]) for k in range(count)], axis=0)
    span = units * length
    mine = lax.dynamic_slice_in_dim(half, section * span, span, 1)
    other = swapped(lax.dynamic_slice_in_dim(half, (1 - section) * span, span, 1))
    embedded = ordered(section, mine, other, 0).reshape(D, units, length).transpose(1, 2, 0)

    slots = units + 1
    state = None
    arrived = []
    sums = []
    for tick in range(units + 2):
        slot = jnp.where(is_high, tick - 2 if tick >= 2 else units, min(tick, units))
        inputs = embedded[min(tick, units - 1)]
        if tick >= 2:
            inputs = jnp.where(is_high, arrived[tick - 2], inputs)
        result, tail, *state = forward(
            slot.astype(jnp.int32).reshape(1), inputs, vec, fin, tables, [*shards], state, slots
        )
        if tick < units:
            arrived.append(lax.ppermute(result, "dp", [(low, high)]))
        if tick >= 2:
            sums.append(tail[:2])
    sums = jnp.stack(sums)
    sum_hat, sum_final = sums[:, 0], sums[:, 1]
    final_gain, head = fin[0, :D], fin[0, 2 * D :]
    rewards = (jnp.sum(sum_final * head, axis=1) / length).reshape(-1, 2)
    pairs = units // 2
    gap = rewards[:, 0] - rewards[:, 1]
    half_margin = 0.5 * lax.dynamic_slice_in_dim(pair_margins, section * pairs, pairs, 0)
    tie = lax.dynamic_slice_in_dim(pair_ties, section * pairs, pairs, 0)
    pair_loss = (1.0 - tie) * jax.nn.softplus(half_margin - gap) + tie * 0.5 * (
        jax.nn.softplus(gap) + jax.nn.softplus(-gap)
    )
    gap_grad = -(1.0 - tie) * jax.nn.sigmoid(half_margin - gap) + tie * 0.5 * (
        jax.nn.sigmoid(gap) - jax.nn.sigmoid(-gap)
    )
    reward_grad = (jnp.stack([gap_grad, -gap_grad], axis=1) / length).reshape(-1)
    final_local = jnp.concatenate(
        [
            head * jnp.sum(reward_grad[:, None] * sum_hat, axis=0),
            head * (length * jnp.sum(reward_grad)),
            jnp.sum(reward_grad[:, None] * sum_final, axis=0),
        ]
    )

    arrived = []
    vector_sum = jnp.zeros((1, V_END), f32)
    embed_grads = []
    for tick in range(units + 2):
        slot = jnp.where(is_high, min(tick, units), tick - 2 if tick >= 2 else units)
        flags = jnp.stack([reward_grad[min(tick, units - 1)], is_high.astype(f32)])
        received = arrived[tick - 2] if tick >= 2 else jnp.zeros((length, D), bf16)
        grad_in, vector_part, state[0] = backward(
            slot.astype(jnp.int32).reshape(1), flags, received, vec, fin, tables, [*shards], state
        )
        if tick < units:
            arrived.append(lax.ppermute(grad_in, "dp", [(high, low)]))
        live = jnp.where(is_high, tick < units, tick >= 2)
        vector_sum = vector_sum + jnp.where(live, vector_part, 0.0)
        if tick >= 2:
            embed_grads.append(grad_in)

    embed_grads = jnp.stack(embed_grads).reshape(span, D).T
    half_width = D // 2
    mine = lax.dynamic_slice_in_dim(embed_grads, section * half_width, half_width, 0)
    other = swapped(lax.dynamic_slice_in_dim(embed_grads, (1 - section) * half_width, half_width, 0))
    half = ordered(section, mine, other, 1)
    token_grads = chosen(
        [place == k for k in range(count)],
        [
            lax.ppermute(half[k * features : (k + 1) * features], "dp", [(low, k)])
            for k in range(count)
        ],
    )

    left_at = jnp.array([(0, 2, 4, 6)[m] + row for m, row, _ in PLACES], jnp.int32)
    right_at = jnp.array([(14, 28, 20, 28)[m] + col for m, _, col in PLACES], jnp.int32)
    part = (own_blocks + 1) // 2
    rest = own_blocks - part
    kept = state[0]

    def part_of(start):
        return products(
            lax.dynamic_slice_in_dim(left_at, start, part, 0),
            lax.dynamic_slice_in_dim(right_at, start, part, 0),
            kept,
            units,
        )

    pieces = []
    for step in range(count):
        base = jnp.where(is_high, order_high[step], order_low[step]) * own_blocks
        sent = swapped(part_of(base + (1 - section) * rest))
        total = (part_of(base + section * rest) + sent).astype(bf16)
        route = [
            (core * count + source, core * count + target)
            for core in range(2)
            for source, target in ((low, order_low[step]), (high, order_high[step]))
        ]
        pieces.append(lax.ppermute(total, both, route))
    piece_low = chosen([place == k for k in order_low], pieces)
    piece_high = chosen([place == k for k in order_high], pieces)
    mine = jnp.where(section == 0, piece_low, piece_high)
    other = swapped(jnp.where(section == 0, piece_high, piece_low))
    grad_blocks = jnp.concatenate(
        [
            jnp.where(section == 0, mine, other),
            jnp.where(section == 0, other, mine)[2 * part - own_blocks :],
        ],
        axis=0,
    )

    zero = jnp.zeros((V_END,), f32)
    live_low, live_high = place == low, place == high
    vector_pack = jnp.concatenate(
        [
            jnp.where(live_low, vector_sum[0], zero),
            jnp.where(live_high, vector_sum[0], zero),
            jnp.where(live_high, final_local, 0.0),
            jnp.where(live_high, jnp.sum(pair_loss), 0.0).reshape(1),
        ]
    )
    vector_all = lax.psum(vector_pack, both)
    loss_total = vector_all[-1:]
    owned_vector = lax.dynamic_slice_in_dim(
        vector_all, section * V_END + place * own_vector, own_vector, 0
    )[None]
    owned_final = lax.dynamic_slice_in_dim(
        vector_all, 2 * V_END + (section * count + place) * own_final, own_final, 0
    )

    table_grad = jax.ops.segment_sum(token_grads.T.astype(f32), ids, num_segments=vocab).T
    block_values = grad_blocks.astype(f32)
    squares = (
        jnp.sum(block_values * block_values)
        + jnp.sum(owned_vector * owned_vector)
        + jnp.sum(owned_final * owned_final)
        + jnp.sum(table_grad * table_grad)
    )
    norm_value = jnp.sqrt(lax.psum(squares, both))
    factor = clip_limit / jnp.maximum(norm_value, clip_limit)

    block_grad, new_blocks, new_left, new_right = (
        out[None]
        for out in shampoo(
            factor.reshape(1),
            grad_blocks,
            layer_blocks[0],
            left_stats[0],
            right_stats[0],
            left_root[0],
            right_root[0],
        )
    )
    vector_m, vector_v, vector_w = adam_step(
        layer_vectors, vector_moment, vector_second, owned_vector * factor, vector_rate, 0.0
    )
    final_m, final_v, final_w = adam_step(
        closing_vectors, final_moment, final_second, owned_final * factor, vector_rate, 0.0
    )
    embed_m, embed_v, embed_w = adam_step(
        embedding, embed_moment, embed_second, table_grad * factor, embed_rate, embed_decay
    )
    return (
        loss_total,
        norm_value.reshape(1),
        block_grad,
        new_blocks,
        new_left,
        new_right,
        vector_m,
        vector_v,
        vector_w,
        final_m,
        final_v,
        final_w,
        embed_m,
        embed_v,
        embed_w,
    )


def solution(mesh):
    return jax.shard_map(
        local,
        mesh=mesh,
        in_specs=(
            P(("member", "dp"), None, None),
            P(("member", "dp")),
            P(("member", "dp")),
            P(("member", "section", "dp"), None),
            P(("member", "section", "dp"), None),
            P(("member", "section", "dp"), None),
            P(("member", "section"), "dp", None, None),
            P(("member", "section"), "dp", None, None),
            P(("member", "section"), "dp", None, None),
            P(("member", "section"), "dp", None, None),
            P(("member", "section"), "dp", None, None),
            P(("member", "section"), "dp"),
            P(("member", "section"), "dp"),
            P(("member", "section"), "dp"),
            P(("member", "section", "dp")),
            P(("member", "section", "dp")),
            P(("member", "section", "dp")),
        ),
        out_specs=(
            P("member"),
            P("member"),
            P(("member", "section"), "dp", None, None),
            P(("member", "section"), "dp", None, None),
            P(("member", "section"), "dp", None, None),
            P(("member", "section"), "dp", None, None),
            P(("member", "section"), "dp"),
            P(("member", "section"), "dp"),
            P(("member", "section"), "dp"),
            P(("member", "section", "dp")),
            P(("member", "section", "dp")),
            P(("member", "section", "dp")),
            P(("member", "section", "dp"), None),
            P(("member", "section", "dp"), None),
            P(("member", "section", "dp"), None),
        ),
        check_vma=False,
    )
```

time: 2370 us -> 1140 us (0.48)
  local copies, waits for them, and re-layouts: 781 us -> 89.4 us
  Pallas kernels: 0 us -> 488 us
  matrix products: 292 us -> 0 us
  waiting for transfers between devices: 542 us -> 256 us
  other arithmetic: 421 us -> 187 us
  blocking collectives: 228 us -> 18.8 us
  starting transfers between devices: 30.2 us -> 64.8 us
    pallas_call x0 -> x21, Pallas kernels: none -> 488 us  [the longest x6 189 us: forward(): pl.pallas_call(functools.partial(forward_kernel, count, first), out_shape...]
    dot_general x43 -> x0, matrix products: 292 us -> none  [the longest x2 40.6 us: layer_backward(): act_grad = jnp.dot(rounded, down_w.T, preferred_element_type=jnp.float32)]
    reduce_scatter x1 -> x0, waiting for transfers between devices: 272 us -> none  [local(): lax.psum_scatter(grad_blocks[None], 'dp', scatter_dimension=1, tiled=True)]
    unnamed x3 -> x0, blocking collectives: 187 us -> none
    scatter x6 -> x0, local copies, waits for them, and re-layouts: 161 us -> none  [local(): store.at[slot_index].set(item)]
    dynamic_update_slice x6 -> x0, local copies, waits for them, and re-layouts: 151 us -> none  [the longest x3 75.7 us: local(): lax.dynamic_update_slice(embed_grads, jnp.where(active, grad_in, previous...]
    all_gather x1 -> x0, waiting for transfers between devices: 93.8 us -> none  [local(): lax.all_gather(layer_blocks.astype(jnp.bfloat16), 'dp', axis=1, tiled=True)]
    reduce_sum x24 -> x7, other arithmetic: 74.6 us -> 7.22 us  [the longest x1 2.42 us: local(): jnp.sum(block_values * block_values) + jnp.sum(owned_vector * owned_vector)]
  transfers between devices with their start and end apart: 11 -> 37, of which waited for: 5 -> 5; matrix products, arithmetic and copies ran while one was open for 15% -> 18% of each run, Pallas kernels for 0% -> 26%
where the time goes in v1:
time: 1140 us; the launch traced here: 1130 us
  Pallas kernels  488 us (43%)
  waiting for transfers between devices  256 us (22%)
  other arithmetic  187 us (16%)
  local copies, waits for them, and re-layouts  89.4 us (8%)
  starting transfers between devices  64.8 us (6%)
  between operations  23 us (2%)
  blocking collectives  18.8 us (2%)
    pallas_call x6, Pallas kernels, forward(): pl.pallas_call(functools.partial(forward_kernel, count, first), out_shape...  189 us
    pallas_call x6, Pallas kernels, backward(): pl.pallas_call(functools.partial(backward_kernel, count), out_shape=(jax....  177 us
    ppermute x4, waiting for transfers between devices, local(): pieces.append(lax.ppermute(total, both, route))  170 us
    pallas_call x8, Pallas kernels, products(): pl.pallas_call(product_kernel, out_shape=jax.ShapeDtypeStruct((count, TIL...  93.3 us
    psum x1, waiting for transfers between devices, local(): vector_all = lax.psum(vector_pack, both)  55.3 us
    sub x3, other arithmetic, adam_step(): weight - rate * (corrected / scaled + decay * weight)  49 us
    scatter-add x1, other arithmetic, local(): jax.ops.segment_sum(token_grads.T.astype(f32), ids, num_segments=vocab)  32.9 us
    pallas_call x1, Pallas kernels, shampoo(): pl.pallas_call(shampoo_kernel, out_shape=(shape,) * 4, grid=(count,), in_...  29.7 us
  transfers between devices with their start and end apart: 37, of which 5 were waited for; matrix products, arithmetic and copies ran while one was open for 18% of the time, Pallas kernels for 26%

profile of v1, /device:TPU:0, one launch (start us, length us, event | category | flops | bytes accessed | tf_op | source)
XLA Modules:
  0.0 1126.2 jit_solution(16699959100427642285)
XLA Ops:
  13.8 5.3 bitcast_convert_fusion
  19.1 6.7 collective-permute-start.5
  25.7 2.4 collective-permute-start.7
  28.1 11.4 %convert_element_type.229 = bf16[96,50304]{1,0:T(8,128)(2,1)} convert(f32[96,50304]{1,0:T(8,128)} %param.22) | non-fusion elementwise | flops 4829184 | bytes 28975104 | tf_op jit(solution)/shard_map/convert_element_type | solution.py:659
  39.6 14.6 %copy.113 = bf16[96,50304]{0,1:T(8,128)(2,1)} copy(bf16[96,50304]{1,0:T(8,128)(2,1)} %convert_element_type.229) | data formatting | bytes 19316736 | tf_op jit(solution)/shard_map/convert_element_type | solution.py:659
  54.2 16.2 %all-reduce.6.cloned.1.call-done = f32[30480]{0:T(1024)} async-done(((f32[30480]{0:T(1024)}), f32[30480]{0:T(1024)}) %all-reduce.6.cloned.1.call-update) | async-done | bytes 121936
  71.5 17.4 %gather_fusion = bf16[4096,96]{1,0:T(8,128)(2,1)S(1)} fusion(bf16[96,50304]{0,1:T(8,128)(2,1)} %copy.113, s32[4096]{0:T(1024)S(1)} %broadcast_clamp_fusion), kind=kCustom, calls=%fused_computation | custom fusion | bytes 1589248 | tf_op jit(solution)/shard_map/jit(_take)/gather | solution.py:659
  88.9 2.1 select_bitcast_fusion
  92.3 10.0 collective-permute-start
  102.3 2.5 collective-permute-start.9
  106.3 13.7 %collective-permute-done = bf16[96,4096]{1,0:T(8,128)(2,1)} collective-permute-done((bf16[96,4096]{1,0:T(8,128)(2,1)}, bf16[96,4096]{1,0:T(8,128)(2,1)}, u32[]{:S(2)}, u32[]{:S(2)}) %collective-permute-start) | collective-permute-done | bytes 786464 | tf_op jit(solution)/shard_map/ppermute | solution.py:660
  120.1 2.5 collective-permute-start.11
  127.2 2.5 collective-permute-start.6
  130.9 2.5 collective-permute-start.8
  134.7 2.4 collective-permute-start.10
  137.2 2.7 collective-permute-start.12
  139.9 1.9 fusion.10
  143.4 2.2 broadcast_select_fusion.9
  145.6 2.1 pad_maximum_fusion.1
  147.7 3.2 copy.118
  152.1 4.2 broadcast_select_fusion.3.refs_7_.refs_8_
  156.3 4.2 broadcast_select_fusion.2.refs_8_.refs_9_
  160.5 4.2 broadcast_select_fusion.1.refs_9_.refs_10_
  164.7 4.2 broadcast_select_fusion.refs_10_.refs_11_
  168.9 31.8 %layer_forward.6 = (bf16[512,768]{1,0:T(8,128)(2,1)}, f32[8,768]{1,0:T(8,128)}, bf16[5,512,11520]{2,1,0:T(8,128)(2,1)}, f32[5,512,768]{2,1,0:T(8,128)}, f32[5,512,128]{2,1,0:T(8,128)}) custom-call(s32[1]{0:T(128)} %bitcast.3.refs_0_, bf16[512,768]{1,0:T(8,128)(2,1)} %get-tuple-element.206.refs_1_, f32[1,9984]{1,0:T(1,128)} %select_n.650.refs_2_.refs_3_, ...), custom_call_target="tpu_custom_call" | custom-call | flops 10000000000 | bytes 30000000 | tf_op jit(solution)/shard_map/layer_forward/pallas_call | solution.py:253
  202.2 31.5 %layer_forward.7 = (bf16[512,768]{1,0:T(8,128)(2,1)}, f32[8,768]{1,0:T(8,128)}, bf16[5,512,11520]{2,1,0:T(8,128)(2,1)}, f32[5,512,768]{2,1,0:T(8,128)}, f32[5,512,128]{2,1,0:T(8,128)}) custom-call(s32[1]{0:T(128)} %bitcast.12.refs_0_, bf16[512,768]{1,0:T(8,128)(2,1)} %get-tuple-element.207.refs_1_, ...), custom_call_target="tpu_custom_call", output_to_operand_aliasing={{2}: (11, {}), {3}: (12, {}), {4}: (13, {})} | custom-call | flops 10000000000 | bytes 30000000 | tf_op jit(solution)/shard_map/layer_forward/pallas_call | solution.py:253
  233.7 1.9 collective-permute-start.14
  236.6 31.3 %layer_forward.8 = (bf16[512,768]{1,0:T(8,128)(2,1)}, f32[8,768]{1,0:T(8,128)}, bf16[5,512,11520]{2,1,0:T(8,128)(2,1)}, f32[5,512,768]{2,1,0:T(8,128)}, f32[5,512,128]{2,1,0:T(8,128)}) custom-call(s32[1]{0:T(128)} %bitcast.2.refs_0_, bf16[512,768]{1,0:T(8,128)(2,1)} %fusion.7.refs_1_, ...), custom_call_target="tpu_custom_call", output_to_operand_aliasing={{2}: (11, {}), {3}: (12, {}), {4}: (13, {})} | custom-call | flops 10000000000 | bytes 30000000 | tf_op jit(solution)/shard_map/layer_forward/pallas_call | solution.py:253
  273.9 31.3 %layer_forward.9 = (bf16[512,768]{1,0:T(8,128)(2,1)}, f32[8,768]{1,0:T(8,128)}, bf16[5,512,11520]{2,1,0:T(8,128)(2,1)}, f32[5,512,768]{2,1,0:T(8,128)}, f32[5,512,128]{2,1,0:T(8,128)}) custom-call(s32[1]{0:T(128)} %bitcast.15.refs_0_, bf16[512,768]{1,0:T(8,128)(2,1)} %get-tuple-element.205.refs_1_, ...), custom_call_target="tpu_custom_call", output_to_operand_aliasing={{2}: (11, {}), {3}: (12, {}), {4}: (13, {})} | custom-call | flops 10000000000 | bytes 30000000 | tf_op jit(solution)/shard_map/layer_forward/pallas_call | solution.py:253
  305.2 1.9 collective-permute-start.16
  307.1 31.3 %layer_forward.10 = (bf16[512,768]{1,0:T(8,128)(2,1)}, f32[8,768]{1,0:T(8,128)}, bf16[5,512,11520]{2,1,0:T(8,128)(2,1)}, f32[5,512,768]{2,1,0:T(8,128)}, f32[5,512,128]{2,1,0:T(8,128)}) custom-call(s32[1]{0:T(128)} %bitcast.18.refs_0_, bf16[512,768]{1,0:T(8,128)(2,1)} %get-tuple-element.204.refs_1_, ...), custom_call_target="tpu_custom_call", output_to_operand_aliasing={{2}: (11, {}), {3}: (12, {}), {4}: (13, {})} | custom-call | flops 10000000000 | bytes 30000000 | tf_op jit(solution)/shard_map/layer_forward/pallas_call | solution.py:253
  340.9 31.5 %layer_forward.11 = (bf16[512,768]{1,0:T(8,128)(2,1)}, f32[8,768]{1,0:T(8,128)}, bf16[5,512,11520]{2,1,0:T(8,128)(2,1)}, f32[5,512,768]{2,1,0:T(8,128)}, f32[5,512,128]{2,1,0:T(8,128)}) custom-call(s32[1]{0:T(128)} %bitcast.20.refs_0_, ...), custom_call_target="tpu_custom_call", output_to_operand_aliasing={{2}: (11, {}), {3}: (12, {}), {4}: (13, {})} | custom-call | flops 10000000000 | bytes 30000000 | tf_op jit(solution)/shard_map/layer_forward/pallas_call | solution.py:253
  380.0 29.5 %layer_backward.6 = (bf16[512,768]{1,0:T(8,128)(2,1)}, f32[1,9984]{1,0:T(1,128)}, bf16[5,512,11520]{2,1,0:T(8,128)(2,1)}) custom-call(s32[1]{0:T(128)} %bitcast.refs_0_, f32[2]{0:T(128)} %pad_maximum_fusion.6.refs_1_, bf16[512,768]{1,0:T(8,128)(2,1)} %broadcast_11_refs_2_.2.refs_2_, ...), custom_call_target="tpu_custom_call", output_to_operand_aliasing={{2}: (12, {})} | custom-call | flops 20000000000 | bytes 40000000 | tf_op jit(solution)/shard_map/layer_backward/pallas_call | solution.py:450
  410.7 29.3 %layer_backward.7 = (bf16[512,768]{1,0:T(8,128)(2,1)}, f32[1,9984]{1,0:T(1,128)}, bf16[5,512,11520]{2,1,0:T(8,128)(2,1)}) custom-call(s32[1]{0:T(128)} %bitcast.24.refs_0_, f32[2]{0:T(128)} %pad_maximum_fusion.7.refs_1_, bf16[512,768]{1,0:T(8,128)(2,1)} %broadcast_11_refs_2_.2.refs_2_, ...), custom_call_target="tpu_custom_call", output_to_operand_aliasing={{2}: (12, {})} | custom-call | flops 20000000000 | bytes 40000000 | tf_op jit(solution)/shard_map/layer_backward/pallas_call | solution.py:450
  444.2 29.3 %layer_backward.8 = (bf16[512,768]{1,0:T(8,128)(2,1)}, f32[1,9984]{1,0:T(1,128)}, bf16[5,512,11520]{2,1,0:T(8,128)(2,1)}) custom-call(s32[1]{0:T(128)} %bitcast.25.refs_0_, f32[2]{0:T(128)} %pad_maximum_fusion.8.refs_1_, bf16[512,768]{1,0:T(8,128)(2,1)} %copy-done.9, f32[1,9984]{1,0:T(1,128)} %select_n.650.refs_2_.refs_3_, ...), custom_call_target="tpu_custom_call", output_to_operand_aliasing={{2}: (12, {})} | custom-call | flops 20000000000 | bytes 40000000 | tf_op jit(solution)/shard_map/layer_backward/pallas_call | solution.py:450
  475.4 29.4 %layer_backward.9 = (bf16[512,768]{1,0:T(8,128)(2,1)}, f32[1,9984]{1,0:T(1,128)}, bf16[5,512,11520]{2,1,0:T(8,128)(2,1)}) custom-call(s32[1]{0:T(128)} %bitcast.26.refs_0_, f32[2]{0:T(128)} %pad_maximum_fusion.9.refs_1_, bf16[512,768]{1,0:T(8,128)(2,1)} %copy-done.7, f32[1,9984]{1,0:T(1,128)} %select_n.650.refs_2_.refs_3_, ...), custom_call_target="tpu_custom_call", output_to_operand_aliasing={{2}: (12, {})} | custom-call | flops 20000000000 | bytes 40000000 | tf_op jit(solution)/shard_map/layer_backward/pallas_call | solution.py:450
  506.8 29.5 %layer_backward.10 = (bf16[512,768]{1,0:T(8,128)(2,1)}, f32[1,9984]{1,0:T(1,128)}, bf16[5,512,11520]{2,1,0:T(8,128)(2,1)}) custom-call(s32[1]{0:T(128)} %bitcast.27.refs_0_, f32[2]{0:T(128)} %pad_maximum_fusion.9.refs_1_, bf16[512,768]{1,0:T(8,128)(2,1)} %copy-done.10, f32[1,9984]{1,0:T(1,128)} %select_n.650.refs_2_.refs_3_, ...), custom_call_target="tpu_custom_call", output_to_operand_aliasing={{2}: (12, {})} | custom-call | flops 20000000000 | bytes 40000000 | tf_op jit(solution)/shard_map/layer_backward/pallas_call | solution.py:450
  537.1 29.5 %layer_backward.11 = (bf16[512,768]{1,0:T(8,128)(2,1)}, f32[1,9984]{1,0:T(1,128)}, bf16[5,512,11520]{2,1,0:T(8,128)(2,1)}) custom-call(s32[1]{0:T(128)} %bitcast.28.refs_0_, f32[2]{0:T(128)} %pad_maximum_fusion.9.refs_1_, bf16[512,768]{1,0:T(8,128)(2,1)} %copy-done.8, f32[1,9984]{1,0:T(1,128)} %select_n.650.refs_2_.refs_3_, ...), custom_call_target="tpu_custom_call", output_to_operand_aliasing={{2}: (12, {})} | custom-call | flops 20000000000 | bytes 40000000 | tf_op jit(solution)/shard_map/layer_backward/pallas_call | solution.py:450
  566.7 11.0 weight_products.9
  578.2 12.1 %weight_products.11 = f32[6,384,384]{2,1,0:T(8,128)} custom-call(s32[6]{0:T(128)} %get-tuple-element.252.left_at, s32[6]{0:T(128)} %get-tuple-element.228.right_at, bf16[5,512,11520]{2,1,0:T(8,128)(2,1)} %get-tuple-element.104.x_ref.y_ref, bf16[5,512,11520]{2,1,0:T(8,128)(2,1)} %get-tuple-element.104.x_ref.y_ref), custom_call_target="tpu_custom_call" | custom-call | flops 3623878656 | bytes 22413312 | tf_op jit(solution)/shard_map/weight_products/pallas_call | solution.py:495
  590.3 12.3 %weight_products.13 = f32[6,384,384]{2,1,0:T(8,128)} custom-call(s32[6]{0:T(128)} %get-tuple-element.254.left_at, s32[6]{0:T(128)} %get-tuple-element.226.right_at, bf16[5,512,11520]{2,1,0:T(8,128)(2,1)} %get-tuple-element.104.x_ref.y_ref, bf16[5,512,11520]{2,1,0:T(8,128)(2,1)} %get-tuple-element.104.x_ref.y_ref), custom_call_target="tpu_custom_call" | custom-call | flops 3623878656 | bytes 22413312 | tf_op jit(solution)/shard_map/weight_products/pallas_call | solution.py:495
  603.9 11.3 %weight_products.15 = f32[6,384,384]{2,1,0:T(8,128)} custom-call(s32[6]{0:T(128)} %get-tuple-element.255.left_at, s32[6]{0:T(128)} %get-tuple-element.225.right_at, bf16[5,512,11520]{2,1,0:T(8,128)(2,1)} %get-tuple-element.104.x_ref.y_ref, bf16[5,512,11520]{2,1,0:T(8,128)(2,1)} %get-tuple-element.104.x_ref.y_ref), custom_call_target="tpu_custom_call" | custom-call | flops 3623878656 | bytes 22413312 | tf_op jit(solution)/shard_map/weight_products/pallas_call | solution.py:495
  622.7 11.0 weight_products.8
  633.7 11.0 weight_products.10
  644.7 12.1 %weight_products.12 = f32[6,384,384]{2,1,0:T(8,128)} custom-call(s32[6]{0:T(128)} %get-tuple-element.253.left_at, s32[6]{0:T(128)} %get-tuple-element.227.right_at, bf16[5,512,11520]{2,1,0:T(8,128)(2,1)} %get-tuple-element.104.x_ref.y_ref, bf16[5,512,11520]{2,1,0:T(8,128)(2,1)} %get-tuple-element.104.x_ref.y_ref), custom_call_target="tpu_custom_call" | custom-call | flops 3623878656 | bytes 22413312 | tf_op jit(solution)/shard_map/weight_products/pallas_call | solution.py:495
  656.8 12.5 %weight_products.14 = f32[6,384,384]{2,1,0:T(8,128)} custom-call(s32[6]{0:T(128)} %get-tuple-element.248.left_at, s32[6]{0:T(128)} %get-tuple-element.232.right_at, bf16[5,512,11520]{2,1,0:T(8,128)(2,1)} %get-tuple-element.104.x_ref.y_ref, bf16[5,512,11520]{2,1,0:T(8,128)(2,1)} %get-tuple-element.104.x_ref.y_ref), custom_call_target="tpu_custom_call" | custom-call | flops 3623878656 | bytes 22413312 | tf_op jit(solution)/shard_map/weight_products/pallas_call | solution.py:495
  669.4 3.7 add_convert_fusion.3
  673.1 1.9 collective-permute-start.22
  675.1 3.7 add_convert_fusion.2
  678.8 2.0 collective-permute-start.24
  680.8 3.7 add_convert_fusion.1
  686.0 3.7 add_convert_fusion
  697.4 125.2 %collective-permute-done.22 = bf16[6,384,384]{2,1,0:T(8,128)(2,1)} collective-permute-done((bf16[6,384,384]{2,1,0:T(8,128)(2,1)}, bf16[6,384,384]{2,1,0:T(8,128)(2,1)}, u32[]{:S(2)}, u32[]{:S(2)}) %collective-permute-start.22) | collective-permute-done | bytes 1769504 | tf_op jit(solution)/shard_map/ppermute | solution.py:759
  825.5 45.0 %collective-permute-done.26 = bf16[6,384,384]{2,1,0:T(8,128)(2,1)} collective-permute-done((bf16[6,384,384]{2,1,0:T(8,128)(2,1)}, bf16[6,384,384]{2,1,0:T(8,128)(2,1)}, u32[]{:S(2)}, u32[]{:S(2)}) %collective-permute-start.26) | collective-permute-done | bytes 1769504 | tf_op jit(solution)/shard_map/ppermute | solution.py:759
  872.8 55.3 %all-reduce.4.cloned.1.call-done = f32[22273]{0:T(1024)} async-done(((f32[22273]{0:T(1024)}), f32[22273]{0:T(1024)}) %all-reduce.4.cloned.1.call-update) | async-done | bytes 89108 | tf_op jit(solution)/shard_map/psum | solution.py:782
  932.1 5.6 broadcast_select_fusion.6
  940.8 32.9 %scatter_custom_fusion = f32[50304,96]{1,0:T(8,128)} fusion(s32[4096]{0:T(1024)S(1)} %bitcast.159, f32[4096,96]{1,0:T(8,128)} %copy.125, f32[]{:T(128)} %constant.69.clone.1), kind=kCustom, calls=%fused_computation.8 | custom fusion | flops 393216 | bytes 19317248 | tf_op jit(solution)/shard_map/scatter-add | solution.py:791
  973.8 23.2 %copy.126 = f32[50304,96]{0,1:T(8,128)} copy(f32[50304,96]{1,0:T(8,128)} %scatter_custom_fusion) | data formatting | bytes 38633472 | tf_op jit(solution)/shard_map/scatter-add | solution.py:791
  996.9 13.0 %multiply_reduce_fusion = f32[]{:T(128)} fusion(f32[50304,96]{1,0:T(8,128)} %scatter_custom_fusion), kind=kLoop, calls=%fused_computation.3 | loop fusion | flops 9658367 | bytes 19316740 | tf_op jit(solution)/shard_map/reduce_sum | solution.py:797
  1011.8 2.4 multiply_reduce_fusion.1
  1016.8 2.2 pad_maximum_fusion.g_ref
  1019.0 18.8 %psum.15 = f32[]{:T(128)} all-reduce(f32[]{:T(128)S(6)} %add.365), channel_id=1, replica_groups=mesh['member'=4,'section'=2,'dp'=4] {'section','dp'}, use_global_device_ids=true, to_apply=%region_11.12 | all-reduce | flops 1 | bytes 8 | tf_op jit(solution)/shard_map/psum | solution.py:799
  1038.5 46.9 %multiply_subtract_fusion = (f32[96,50304]{1,0:T(8,128)}, f32[96,50304]{1,0:T(8,128)}, f32[96,50304]{1,0:T(8,128)}) fusion(f32[96,50304]{1,0:T(8,128)} %param.22, f32[50304,96]{0,1:T(8,128)} %copy.126, f32[]{:T(128)} %div.158, f32[96,50304]{1,0:T(8,128)} %param.24, f32[96,50304]{1,0:T(8,128)} %param.23), kind=kLoop, calls=%fused_computation.7 | loop fusion | flops 77266944 | bytes 135217152 | tf_op jit(solution)/shard_map/sub | solution.py:573
  1086.9 29.7 %shampoo.1 = (f32[12,384,384]{2,1,0:T(8,128)}, f32[12,384,384]{2,1,0:T(8,128)}, f32[12,384,384]{2,1,0:T(8,128)}, f32[12,384,384]{2,1,0:T(8,128)}) custom-call(f32[1]{0:T(128)} %bitcast.40.factor_ref, bf16[12,384,384]{2,1,0:T(8,128)(2,1)} %pad_maximum_fusion.g_ref, f32[12,384,384]{2,1,0:T(8,128)} %bitcast.142, f32[12,384,384]{2,1,0:T(8,128)} %bitcast.148, ...), custom_call_target="tpu_custom_call" | custom-call | flops 9512681472 | bytes 67239936 | tf_op jit(solution)/shard_map/shampoo/pallas_call | solution.py:541
  (239 shorter events, 80.9 us)
Async XLA Ops:
  7.2 63.2 %all-reduce.6.cloned.1.call-start = ((), (), s32[]{:S(2)}) async-start(), calls=%async_computation.1 | async-start | bytes 245760
  13.7 914.4 %all-reduce.4.cloned.1.call-start = ((), (), s32[]{:S(2)}) async-start(), calls=%async_computation | async-start | bytes 180224 | tf_op jit(solution)/shard_map/psum | solution.py:782
  19.1 108.2 %collective-permute-start.5 = (bf16[12,384,384]{2,1,0:T(8,128)(2,1)}, bf16[12,384,384]{2,1,0:T(8,128)(2,1)}, u32[]{:S(2)}, u32[]{:S(2)}) collective-permute-start(bf16[12,384,384]{2,1,0:T(8,128)(2,1)} %bitcast_convert_fusion), channel_id=1, source_target_pairs={{0,1},{4,6},{8,9},{12,14},{16,17},{20,22},{24,25},{28,30}} | collective-permute-start | bytes 10616840 | tf_op jit(solution)/shard_map/ppermute | solution.py:634
  25.7 105.2 %collective-permute-start.7 = (bf16[12,384,384]{2,1,0:T(8,128)(2,1)}, bf16[12,384,384]{2,1,0:T(8,128)(2,1)}, u32[]{:S(2)}, u32[]{:S(2)}) collective-permute-start(bf16[12,384,384]{2,1,0:T(8,128)(2,1)} %bitcast_convert_fusion), channel_id=1, source_target_pairs={{1,1},{5,6},{9,9},{13,14},{17,17},{21,22},{25,25},{29,30}} | collective-permute-start | bytes 10616840 | tf_op jit(solution)/shard_map/ppermute | solution.py:634
  71.4 17.4 %copy-start.16 = (s32[1,8,4,128]{3,2,1,0:T(4,128)}, s32[1,8,4,128]{3,2,1,0:T(4,128)S(1)}, u32[]{:S(2)}) copy-start(s32[1,8,4,128]{3,2,1,0:T(4,128)S(1)} %get-tuple-element.208) | copy-start | bytes 49156
  92.3 27.7 %collective-permute-start = (bf16[96,4096]{1,0:T(8,128)(2,1)}, bf16[96,4096]{1,0:T(8,128)(2,1)}, u32[]{:S(2)}, u32[]{:S(2)}) collective-permute-start(bf16[96,4096]{1,0:T(8,128)(2,1)} %copy.114), channel_id=1, source_target_pairs={{0,1},{4,5},{8,9},{12,13},{16,17},{20,21},{24,25},{28,29}} | collective-permute-start | bytes 2359304 | tf_op jit(solution)/shard_map/ppermute | solution.py:660
  102.3 32.5 %collective-permute-start.9 = (bf16[12,384,384]{2,1,0:T(8,128)(2,1)}, bf16[12,384,384]{2,1,0:T(8,128)(2,1)}, u32[]{:S(2)}, u32[]{:S(2)}) collective-permute-start(bf16[12,384,384]{2,1,0:T(8,128)(2,1)} %bitcast_convert_fusion), channel_id=1, source_target_pairs={{2,1},{6,6},{10,9},{14,14},{18,17},{22,22},{26,25},{30,30}} | collective-permute-start | bytes 10616840 | tf_op jit(solution)/shard_map/ppermute | solution.py:634
  104.8 17.8 %collective-permute-start.1 = (bf16[96,4096]{1,0:T(8,128)(2,1)}, bf16[96,4096]{1,0:T(8,128)(2,1)}, u32[]{:S(2)}, u32[]{:S(2)}) collective-permute-start(bf16[96,4096]{1,0:T(8,128)(2,1)} %copy.114), channel_id=1, source_target_pairs={{1,1},{5,5},{9,9},{13,13},{17,17},{21,21},{25,25},{29,29}} | collective-permute-start | bytes 2359304 | tf_op jit(solution)/shard_map/ppermute | solution.py:660
  120.1 17.1 %collective-permute-start.11 = (bf16[12,384,384]{2,1,0:T(8,128)(2,1)}, bf16[12,384,384]{2,1,0:T(8,128)(2,1)}, u32[]{:S(2)}, u32[]{:S(2)}) collective-permute-start(bf16[12,384,384]{2,1,0:T(8,128)(2,1)} %bitcast_convert_fusion), channel_id=1, source_target_pairs={{3,1},{7,6},{11,9},{15,14},{19,17},{23,22},{27,25},{31,30}} | collective-permute-start | bytes 10616840 | tf_op jit(solution)/shard_map/ppermute | solution.py:634
  122.6 2.7 collective-permute-start.2
  125.3 8.1 collective-permute-start.3
  127.2 24.9 %collective-permute-start.6 = (bf16[12,384,384]{2,1,0:T(8,128)(2,1)}, bf16[12,384,384]{2,1,0:T(8,128)(2,1)}, u32[]{:S(2)}, u32[]{:S(2)}) collective-permute-start(bf16[12,384,384]{2,1,0:T(8,128)(2,1)} %collective-permute-done.5), channel_id=1, source_target_pairs={{1,5},{6,2},{9,13},{14,10},{17,21},{22,18},{25,29},{30,26}} | collective-permute-start | bytes 10616840 | tf_op jit(solution)/shard_map/ppermute | solution.py:635
  130.9 25.4 %collective-permute-start.8 = (bf16[12,384,384]{2,1,0:T(8,128)(2,1)}, bf16[12,384,384]{2,1,0:T(8,128)(2,1)}, u32[]{:S(2)}, u32[]{:S(2)}) collective-permute-start(bf16[12,384,384]{2,1,0:T(8,128)(2,1)} %collective-permute-done.7), channel_id=1, source_target_pairs={{1,5},{6,2},{9,13},{14,10},{17,21},{22,18},{25,29},{30,26}} | collective-permute-start | bytes 10616840 | tf_op jit(solution)/shard_map/ppermute | solution.py:635
  134.7 8.7 collective-permute-start.4
  134.7 25.8 %collective-permute-start.10 = (bf16[12,384,384]{2,1,0:T(8,128)(2,1)}, bf16[12,384,384]{2,1,0:T(8,128)(2,1)}, u32[]{:S(2)}, u32[]{:S(2)}) collective-permute-start(bf16[12,384,384]{2,1,0:T(8,128)(2,1)} %collective-permute-done.9), channel_id=1, source_target_pairs={{1,5},{6,2},{9,13},{14,10},{17,21},{22,18},{25,29},{30,26}} | collective-permute-start | bytes 10616840 | tf_op jit(solution)/shard_map/ppermute | solution.py:635
  137.2 27.6 %collective-permute-start.12 = (bf16[12,384,384]{2,1,0:T(8,128)(2,1)}, bf16[12,384,384]{2,1,0:T(8,128)(2,1)}, u32[]{:S(2)}, u32[]{:S(2)}) collective-permute-start(bf16[12,384,384]{2,1,0:T(8,128)(2,1)} %collective-permute-done.11), channel_id=1, source_target_pairs={{1,5},{6,2},{9,13},{14,10},{17,21},{22,18},{25,29},{30,26}} | collective-permute-start | bytes 10616840 | tf_op jit(solution)/shard_map/ppermute | solution.py:635
  200.7 35.0 %collective-permute-start.13 = (bf16[512,768]{1,0:T(8,128)(2,1)}, bf16[512,768]{1,0:T(8,128)(2,1)}, u32[]{:S(2)}, u32[]{:S(2)}) collective-permute-start(bf16[512,768]{1,0:T(8,128)(2,1)} %get-tuple-element.63), channel_id=1, source_target_pairs={{1,2},{5,6},{9,10},{13,14},{17,18},{21,22},{25,26},{29,30}} | collective-permute-start | bytes 2359304 | tf_op jit(solution)/shard_map/ppermute | solution.py:679
  233.7 38.9 %collective-permute-start.14 = (bf16[512,768]{1,0:T(8,128)(2,1)}, bf16[512,768]{1,0:T(8,128)(2,1)}, u32[]{:S(2)}, u32[]{:S(2)}) collective-permute-start(bf16[512,768]{1,0:T(8,128)(2,1)} %get-tuple-element.71), channel_id=1, source_target_pairs={{1,2},{5,6},{9,10},{13,14},{17,18},{21,22},{25,26},{29,30}} | collective-permute-start | bytes 2359304 | tf_op jit(solution)/shard_map/ppermute | solution.py:679
  236.6 33.1 %copy-start.30 = (s32[48]{0:T(128)S(1)}, s32[48]{0:T(128)}, u32[]{:S(2)}) copy-start(s32[48]{0:T(128)} %constant.164.clone) | copy-start | bytes 580
  236.6 33.1 %copy-start.31 = (s32[48]{0:T(128)S(1)}, s32[48]{0:T(128)}, u32[]{:S(2)}) copy-start(s32[48]{0:T(128)} %constant.163.clone) | copy-start | bytes 580
  267.9 4.7 collective-permute-start.15
  271.2 103.6 %copy-start.40 = (f32[2]{0:T(128)}, f32[2]{0:T(128)S(1)}, u32[]{:S(2)}) copy-start(f32[2]{0:T(128)S(1)} %get-tuple-element.174) | copy-start | bytes 28
  271.2 103.6 %copy-start.42 = (f32[2]{0:T(128)}, f32[2]{0:T(128)S(1)}, u32[]{:S(2)}) copy-start(f32[2]{0:T(128)S(1)} %get-tuple-element.247) | copy-start | bytes 28
  271.9 101.8 %copy-start.28 = (f32[768]{0:T(1024)}, f32[768]{0:T(1024)S(1)}, u32[]{:S(2)}) copy-start(f32[768]{0:T(1024)S(1)} %slice_reduce_fusion) | copy-start | bytes 9220
  305.2 34.7 %collective-permute-start.16 = (bf16[512,768]{1,0:T(8,128)(2,1)}, bf16[512,768]{1,0:T(8,128)(2,1)}, u32[]{:S(2)}, u32[]{:S(2)}) collective-permute-start(bf16[512,768]{1,0:T(8,128)(2,1)} %get-tuple-element.81), channel_id=1, source_target_pairs={{1,2},{5,6},{9,10},{13,14},{17,18},{21,22},{25,26},{29,30}} | collective-permute-start | bytes 2359304 | tf_op jit(solution)/shard_map/ppermute | solution.py:679
  374.8 34.7 %copy-start.49 = (f32[2,1]{0,1:T(1,128)}, f32[2,1]{0,1:T(1,128)S(1)}, u32[]{:S(2)}) copy-start(f32[2,1]{0,1:T(1,128)S(1)} %copy.130) | copy-start | bytes 28
  376.0 33.5 %copy-start.35 = (f32[4]{0:T(128)}, f32[4]{0:T(128)S(1)}, u32[]{:S(2)}) copy-start(f32[4]{0:T(128)S(1)} %div.157) | copy-start | bytes 52
  409.5 33.8 %collective-permute-start.17 = (bf16[512,768]{1,0:T(8,128)(2,1)}, bf16[512,768]{1,0:T(8,128)(2,1)S(1)}, u32[]{:S(2)}, u32[]{:S(2)}) collective-permute-start(bf16[512,768]{1,0:T(8,128)(2,1)} %get-tuple-element.92), channel_id=1, source_target_pairs={{2,1},{6,5},{10,9},{14,13},{18,17},{22,21},{26,25},{30,29}} | collective-permute-start | bytes 2359304 | tf_op jit(solution)/shard_map/ppermute | solution.py:716
  440.0 34.4 %collective-permute-start.18 = (bf16[512,768]{1,0:T(8,128)(2,1)}, bf16[512,768]{1,0:T(8,128)(2,1)S(1)}, u32[]{:S(2)}, u32[]{:S(2)}) collective-permute-start(bf16[512,768]{1,0:T(8,128)(2,1)} %get-tuple-element.95), channel_id=1, source_target_pairs={{2,1},{6,5},{10,9},{14,13},{18,17},{22,21},{26,25},{30,29}} | collective-permute-start | bytes 2359304 | tf_op jit(solution)/shard_map/ppermute | solution.py:716
  473.5 32.4 %collective-permute-start.19 = (bf16[512,768]{1,0:T(8,128)(2,1)}, bf16[512,768]{1,0:T(8,128)(2,1)S(1)}, u32[]{:S(2)}, u32[]{:S(2)}) collective-permute-start(bf16[512,768]{1,0:T(8,128)(2,1)} %get-tuple-element.98), channel_id=1, source_target_pairs={{2,1},{6,5},{10,9},{14,13},{18,17},{22,21},{26,25},{30,29}} | collective-permute-start | bytes 2359304 | tf_op jit(solution)/shard_map/ppermute | solution.py:716
  504.8 31.5 %collective-permute-start.20 = (bf16[512,768]{1,0:T(8,128)(2,1)}, bf16[512,768]{1,0:T(8,128)(2,1)S(1)}, u32[]{:S(2)}, u32[]{:S(2)}) collective-permute-start(bf16[512,768]{1,0:T(8,128)(2,1)} %get-tuple-element.101), channel_id=1, source_target_pairs={{2,1},{6,5},{10,9},{14,13},{18,17},{22,21},{26,25},{30,29}} | collective-permute-start | bytes 2359304 | tf_op jit(solution)/shard_map/ppermute | solution.py:716
  577.7 91.7 %collective-permute-start.21 = (f32[6,384,384]{2,1,0:T(8,128)}, f32[6,384,384]{2,1,0:T(8,128)}, u32[]{:S(2)}, u32[]{:S(2)}) collective-permute-start(f32[6,384,384]{2,1,0:T(8,128)} %weight_products.9), channel_id=1, source_target_pairs={{0,4},{4,0},{1,5},{5,1},{2,6},{6,2},{3,7},{7,3},{8,12},{12,8},{9,1... | collective-permute-start | bytes 10616840 | tf_op jit(solution)/shard_map/ppermute | solution.py:594
  590.3 84.7 %collective-permute-start.23 = (f32[6,384,384]{2,1,0:T(8,128)}, f32[6,384,384]{2,1,0:T(8,128)}, u32[]{:S(2)}, u32[]{:S(2)}) collective-permute-start(f32[6,384,384]{2,1,0:T(8,128)} %weight_products.11), channel_id=1, source_target_pairs={{0,4},{4,0},{1,5},{5,1},{2,6},{6,2},{3,7},{7,3},{8,12},{12,8},{9,1... | collective-permute-start | bytes 10616840 | tf_op jit(solution)/shard_map/ppermute | solution.py:594
  590.3 12.8 %copy-start.19 = (f32[4,1,768]{2,1,0:T(1,128)S(1)}, f32[4,1,768]{2,1,0:T(1,128)}, u32[]{:S(2)}) copy-start(f32[4,1,768]{2,1,0:T(1,128)} %copy-done.18) | copy-start | bytes 36868
  590.3 12.8 %copy-start.20 = (f32[4,1,768]{2,1,0:T(1,128)S(1)}, f32[4,1,768]{2,1,0:T(1,128)}, u32[]{:S(2)}) copy-start(f32[4,1,768]{2,1,0:T(1,128)} %get-tuple-element.214) | copy-start | bytes 36868
  590.3 12.8 %copy-start.36 = (f32[4]{0:T(128)S(1)}, f32[4]{0:T(128)}, u32[]{:S(2)}) copy-start(f32[4]{0:T(128)} %copy-done.35) | copy-start | bytes 52
  602.7 78.1 %collective-permute-start.25 = (f32[6,384,384]{2,1,0:T(8,128)}, f32[6,384,384]{2,1,0:T(8,128)}, u32[]{:S(2)}, u32[]{:S(2)}) collective-permute-start(f32[6,384,384]{2,1,0:T(8,128)} %weight_products.13), channel_id=1, source_target_pairs={{0,4},{4,0},{1,5},{5,1},{2,6},{6,2},{3,7},{7,3},{8,12},{12,8},{9,1... | collective-permute-start | bytes 10616840 | tf_op jit(solution)/shard_map/ppermute | solution.py:594
  603.8 12.6 %copy-start.48 = (f32[2,1]{0,1:T(1,128)S(1)}, f32[2,1]{0,1:T(1,128)}, u32[]{:S(2)}) copy-start(f32[2,1]{0,1:T(1,128)} %copy-done.47) | copy-start | bytes 28
  603.8 12.6 %copy-start.50 = (f32[2,1]{0,1:T(1,128)S(1)}, f32[2,1]{0,1:T(1,128)}, u32[]{:S(2)}) copy-start(f32[2,1]{0,1:T(1,128)} %copy-done.49) | copy-start | bytes 28
  603.8 14.5 %copy-start.29 = (f32[768]{0:T(1024)S(1)}, f32[768]{0:T(1024)}, u32[]{:S(2)}) copy-start(f32[768]{0:T(1024)} %copy-done.28) | copy-start | bytes 9220
  603.8 15.1 %copy-start.11 = (bf16[512,768]{1,0:T(8,128)(2,1)S(1)}, bf16[512,768]{1,0:T(8,128)(2,1)}, u32[]{:S(2)}) copy-start(bf16[512,768]{1,0:T(8,128)(2,1)} %get-tuple-element.98) | copy-start | bytes 2359300
  603.8 15.1 %copy-start.12 = (bf16[512,768]{1,0:T(8,128)(2,1)S(1)}, bf16[512,768]{1,0:T(8,128)(2,1)}, u32[]{:S(2)}) copy-start(bf16[512,768]{1,0:T(8,128)(2,1)} %get-tuple-element.101) | copy-start | bytes 2359300
  603.8 15.1 %copy-start.13 = (bf16[512,768]{1,0:T(8,128)(2,1)S(1)}, bf16[512,768]{1,0:T(8,128)(2,1)}, u32[]{:S(2)}) copy-start(bf16[512,768]{1,0:T(8,128)(2,1)} %get-tuple-element.105) | copy-start | bytes 2359300
  603.8 15.1 %copy-start.14 = (bf16[512,768]{1,0:T(8,128)(2,1)S(1)}, bf16[512,768]{1,0:T(8,128)(2,1)}, u32[]{:S(2)}) copy-start(bf16[512,768]{1,0:T(8,128)(2,1)} %get-tuple-element.106) | copy-start | bytes 2359300
  615.1 70.9 %collective-permute-start.27 = (f32[6,384,384]{2,1,0:T(8,128)}, f32[6,384,384]{2,1,0:T(8,128)}, u32[]{:S(2)}, u32[]{:S(2)}) collective-permute-start(f32[6,384,384]{2,1,0:T(8,128)} %weight_products.15), channel_id=1, source_target_pairs={{0,4},{4,0},{1,5},{5,1},{2,6},{6,2},{3,7},{7,3},{8,12},{12,8},{9,1... | collective-permute-start | bytes 10616840 | tf_op jit(solution)/shard_map/ppermute | solution.py:594
  622.6 70.2 %collective-permute-start.30 = (bf16[384,2048]{1,0:T(8,128)(2,1)}, bf16[384,2048]{1,0:T(8,128)(2,1)}, u32[]{:S(2)}, u32[]{:S(2)}) collective-permute-start(bf16[384,2048]{1,0:T(8,128)(2,1)} %bitcast.37), channel_id=1, source_target_pairs={{0,4},{4,0},{1,5},{5,1},{2,6},{6,2},{3,7},{7,3},{8,12},{12,8},{9,1... | collective-permute-start | bytes 4718600 | tf_op jit(solution)/shard_map/ppermute | solution.py:594
  673.1 149.5 %collective-permute-start.22 = (bf16[6,384,384]{2,1,0:T(8,128)(2,1)}, bf16[6,384,384]{2,1,0:T(8,128)(2,1)}, u32[]{:S(2)}, u32[]{:S(2)}) collective-permute-start(bf16[6,384,384]{2,1,0:T(8,128)(2,1)} %add_convert_fusion.3), channel_id=1, source_target_pairs={{1,0},{2,3},{5,4},{6,7},{9,8},{10,11},{13,12},{14,15},{17,16},{18,... | collective-permute-start | bytes 5308424 | tf_op jit(solution)/shard_map/ppermute | solution.py:759
  678.8 145.5 %collective-permute-start.24 = (bf16[6,384,384]{2,1,0:T(8,128)(2,1)}, bf16[6,384,384]{2,1,0:T(8,128)(2,1)}, u32[]{:S(2)}, u32[]{:S(2)}) collective-permute-start(bf16[6,384,384]{2,1,0:T(8,128)(2,1)} %add_convert_fusion.2), channel_id=1, source_target_pairs={{1,2},{2,1},{5,6},{6,5},{9,10},{10,9},{13,14},{14,13},{17,18},{18,... | collective-permute-start | bytes 5308424 | tf_op jit(solution)/shard_map/ppermute | solution.py:759
  684.5 186.0 %collective-permute-start.26 = (bf16[6,384,384]{2,1,0:T(8,128)(2,1)}, bf16[6,384,384]{2,1,0:T(8,128)(2,1)}, u32[]{:S(2)}, u32[]{:S(2)}) collective-permute-start(bf16[6,384,384]{2,1,0:T(8,128)(2,1)} %add_convert_fusion.1), channel_id=1, source_target_pairs={{1,3},{2,0},{5,7},{6,4},{9,11},{10,8},{13,15},{14,12},{17,19},{18,... | collective-permute-start | bytes 5308424 | tf_op jit(solution)/shard_map/ppermute | solution.py:759
  689.7 242.4 %collective-permute-start.28 = (bf16[6,384,384]{2,1,0:T(8,128)(2,1)}, bf16[6,384,384]{2,1,0:T(8,128)(2,1)}, u32[]{:S(2)}, u32[]{:S(2)}) collective-permute-start(bf16[6,384,384]{2,1,0:T(8,128)(2,1)} %add_convert_fusion), channel_id=1, source_target_pairs={{1,1},{2,2},{5,5},{6,6},{9,9},{10,10},{13,13},{14,14},{17,17},{18,... | collective-permute-start | bytes 5308424 | tf_op jit(solution)/shard_map/ppermute | solution.py:759
  694.4 178.4 %copy-start.17 = (s32[1,8,4,128]{3,2,1,0:T(4,128)S(1)}, s32[1,8,4,128]{3,2,1,0:T(4,128)}, u32[]{:S(2)}) copy-start(s32[1,8,4,128]{3,2,1,0:T(4,128)} %copy-done.16) | copy-start | bytes 49156
  695.8 241.9 %collective-permute-start.31 = (bf16[96,4096]{1,0:T(8,128)(2,1)}, bf16[96,4096]{1,0:T(8,128)(2,1)}, u32[]{:S(2)}, u32[]{:S(2)}) collective-permute-start(bf16[96,4096]{1,0:T(8,128)(2,1)} %get-tuple-element.197), channel_id=1, source_target_pairs={{1,2},{5,6},{9,10},{13,14},{17,18},{21,22},{25,26},{29,30}} | collective-permute-start | bytes 2359304 | tf_op jit(solution)/shard_map/ppermute | solution.py:730
  822.6 115.1 %collective-permute-start.32 = (bf16[96,4096]{1,0:T(8,128)(2,1)}, bf16[96,4096]{1,0:T(8,128)(2,1)}, u32[]{:S(2)}, u32[]{:S(2)}) collective-permute-start(bf16[96,4096]{1,0:T(8,128)(2,1)} %get-tuple-element.198), channel_id=1, source_target_pairs={{1,1},{5,5},{9,9},{13,13},{17,17},{21,21},{25,25},{29,29}} | collective-permute-start | bytes 2359304 | tf_op jit(solution)/shard_map/ppermute | solution.py:730
  824.2 113.5 %collective-permute-start.33 = (bf16[96,4096]{1,0:T(8,128)(2,1)S(1)}, bf16[96,4096]{1,0:T(8,128)(2,1)}, u32[]{:S(2)}, u32[]{:S(2)}) collective-permute-start(bf16[96,4096]{1,0:T(8,128)(2,1)S(1)} %get-tuple-element.199), channel_id=1, source_target_pairs={{1,0},{5,4},{9,8},{13,12},{17,16},{21,20},{25,24},{29,28}} | collective-permute-start | bytes 2359304 | tf_op jit(solution)/shard_map/ppermute | solution.py:730
  870.5 67.2 %collective-permute-start.34 = (bf16[96,4096]{1,0:T(8,128)(2,1)S(1)}, bf16[96,4096]{1,0:T(8,128)(2,1)}, u32[]{:S(2)}, u32[]{:S(2)}) collective-permute-start(bf16[96,4096]{1,0:T(8,128)(2,1)S(1)} %get-tuple-element.196), channel_id=1, source_target_pairs={{1,3},{5,7},{9,11},{13,15},{17,19},{21,23},{25,27},{29,31}} | collective-permute-start | bytes 2359304 | tf_op jit(solution)/shard_map/ppermute | solution.py:730
  937.7 72.3 %collective-permute-start.29 = (bf16[6,384,384]{2,1,0:T(8,128)(2,1)S(1)}, bf16[6,384,384]{2,1,0:T(8,128)(2,1)}, u32[]{:S(2)}, u32[]{:S(2)}) collective-permute-start(bf16[6,384,384]{2,1,0:T(8,128)(2,1)S(1)} %get-tuple-element.187), channel_id=1, source_target_pairs={{0,4},{4,0},{1,5},{5,1},{2,6},{6,2},{3,7},{7,3},{8,12},{12,8},{9,1... | collective-permute-start | bytes 5308424 | tf_op jit(solution)/shard_map/ppermute | solution.py:594
  996.9 13.0 %copy-start.4 = (bf16[6,384,384]{2,1,0:T(8,128)(2,1)S(1)}, bf16[6,384,384]{2,1,0:T(8,128)(2,1)}, u32[]{:S(2)}) copy-start(bf16[6,384,384]{2,1,0:T(8,128)(2,1)} %get-tuple-element.188) | copy-start | bytes 5308420
  996.9 13.0 %copy-start.5 = (bf16[6,384,384]{2,1,0:T(8,128)(2,1)S(1)}, bf16[6,384,384]{2,1,0:T(8,128)(2,1)}, u32[]{:S(2)}) copy-start(bf16[6,384,384]{2,1,0:T(8,128)(2,1)} %get-tuple-element.189) | copy-start | bytes 5308420
  1038.5 47.7 %copy-start.21 = (f32[1,2496]{1,0:T(1,128)S(1)}, f32[1,2496]{1,0:T(1,128)}, u32[]{:S(2)}) copy-start(f32[1,2496]{1,0:T(1,128)} %param.30) | copy-start | bytes 29956
  1038.5 47.7 %copy-start.37 = (f32[1,2496]{1,0:T(1,128)S(1)}, f32[1,2496]{1,0:T(1,128)}, u32[]{:S(2)}) copy-start(f32[1,2496]{1,0:T(1,128)} %param.32) | copy-start | bytes 29956
  1038.5 47.7 %copy-start.38 = (f32[1,2496]{1,0:T(1,128)S(1)}, f32[1,2496]{1,0:T(1,128)}, u32[]{:S(2)}) copy-start(f32[1,2496]{1,0:T(1,128)} %param.31) | copy-start | bytes 29956
  1086.9 29.7 %copy-start.39 = (f32[288]{0:T(512)S(1)}, f32[288]{0:T(512)}, u32[]{:S(2)}) copy-start(f32[288]{0:T(512)} %param.33) | copy-start | bytes 3460
  1086.9 29.7 %copy-start.44 = (f32[288]{0:T(512)S(1)}, f32[288]{0:T(512)}, u32[]{:S(2)}) copy-start(f32[288]{0:T(512)} %param.35) | copy-start | bytes 3460
  1086.9 29.7 %copy-start.45 = (f32[288]{0:T(512)S(1)}, f32[288]{0:T(512)}, u32[]{:S(2)}) copy-start(f32[288]{0:T(512)} %param.34) | copy-start | bytes 3460
  (24 other events, 151.8 us)
Sparse Core Ops, SparseCore 0:
  13.9 56.4 all-reduce.5
  872.9 55.1 all-reduce.3

commit v2 on v1

v2 whole, which is shorter than its diff:
```python
import functools
import math

import jax
import jax.numpy as jnp
from jax import lax
from jax.experimental import pallas as pl
from jax.experimental.pallas import tpu as pltpu
from jax.sharding import PartitionSpec as P

D = 768
HEADS = 12
HEAD = 64
ROT = 16
FF = 3072
STEP = 10
TILE = 384
PAIR = 2 * HEAD
QROWS = 256
CHUNK = 768
LSE_ROWS = 16

norm_eps = 1e-05
beta_first = 0.9
beta_second = 0.999
adam_eps = 1e-08
clip_limit = 1.0
embed_rate = 0.2
embed_decay = 0.01
vector_rate = 0.5
shampoo_rate = 0.1
stats_decay = 0.95
rope_base = 10000.0

f32 = jnp.float32
bf16 = jnp.bfloat16
VMEM_LIMIT = 60 * 2**20
LIGHT = pl.CostEstimate(flops=1, bytes_accessed=1, transcendentals=0)

COL_A, COL_O, COL_B, COL_H = 0, D, 2 * D, 3 * D
COL_QKV = 3 * D + FF
COL_GP = COL_QKV + 3 * D
COL_X = COL_GP + FF
KEPT = COL_X + D
COL_DP, COL_G, COL_DH = 0, 3 * D, 4 * D
GRADS = 4 * D + FF

V_G1, V_C1, V_G2, V_C2, V_QKV, V_O = 0, D, 2 * D, 3 * D, 4 * D, 7 * D
V_B1, V_B2, V_END = 8 * D, 8 * D + FF, 9 * D + FF


def block_places():
    places = []
    for matrix, (rows, cols) in enumerate(((D, 3 * D), (D, D), (D, FF), (FF, D))):
        for row in range(rows // TILE):
            for col in range(cols // TILE):
                places.append((matrix, row, col))
    return places


PLACES = block_places()


def nt(a, b):
    return lax.dot_general(a, b, (((1,), (1,)), ((), ())), preferred_element_type=f32)


def tn(a, b):
    return lax.dot_general(a, b, (((0,), (0,)), ((), ())), preferred_element_type=f32)


def nn(a, b):
    return lax.dot_general(a, b, (((1,), (0,)), ((), ())), preferred_element_type=f32)


def normalized(x):
    mean = jnp.mean(x, axis=-1, keepdims=True)
    centred = x - mean
    spread = jnp.mean(centred * centred, axis=-1, keepdims=True)
    scale = lax.rsqrt(spread + norm_eps)
    return centred * scale, scale


def norm_back(grad, gain, hat, scale):
    inner = grad * gain
    first = jnp.mean(inner, axis=-1, keepdims=True)
    second = jnp.mean(inner * hat, axis=-1, keepdims=True)
    return scale * (inner - first - hat * second)


def gelu_both(h):
    expo = jnp.exp(-0.5 * h * h)
    t = 1.0 / (1.0 + (0.3275911 * math.sqrt(0.5)) * jnp.abs(h))
    poly = 0.5 * 1.061405429
    for coef in (-1.453152027, 1.421413741, -0.284496736, 0.254829592):
        poly = poly * t + 0.5 * coef
    tail = poly * t * expo
    cdf = jnp.where(h >= 0.0, 1.0 - tail, tail)
    return h * cdf, cdf + h * expo * (1.0 / math.sqrt(2.0 * math.pi))


def head_masks(value):
    lane = lax.broadcasted_iota(jnp.int32, (1, PAIR), 1)
    return [
        jnp.where(lane < HEAD, value, 0.0).astype(bf16),
        jnp.where(lane < HEAD, 0.0, value).astype(bf16),
    ]


def arrivals(count):
    low = count // 2 - 1
    order = list(range(count - 1, low, -1)) + list(range(low))
    return [order[i : i + 2] for i in range(0, count - 1, 2)]


def shard_sources(count, is_high, direct):
    rounds = arrivals(count)
    own = count // 2 - 1
    sources = [None] * count
    for index, pair in enumerate(rounds):
        for side, shard in enumerate(pair):
            sources[shard] = index + (0 if direct == (side == 0) else len(rounds))
    sources[own] = 2 * len(rounds) + (0 if direct else 1)
    return sources[::-1] if is_high else sources


class Weights:
    def __init__(self, role, arrays, mats, sems):
        self.role = role
        count = len(PLACES) // arrays[0].shape[0]
        per = arrays[0].shape[0]
        self.copies = []
        for is_high in (False, True):
            for direct in (False, True):
                sources = shard_sources(count, is_high, direct)
                self.copies.append(
                    [
                        pltpu.make_async_copy(
                            arrays[sources[index // per]].at[index % per],
                            mats[matrix].at[pl.ds(row * TILE, TILE), pl.ds(col * TILE, TILE)],
                            sems.at[index],
                        )
                        for index, (matrix, row, col) in enumerate(PLACES)
                    ]
                )

    def start(self, *matrices):
        for role, copies in enumerate(self.copies):

            @pl.when(self.role == role)
            def _(copies=copies):
                for matrix in matrices:
                    for place, copy in zip(PLACES, copies):
                        if place[0] == matrix:
                            copy.start()

    def wait(self, matrix):
        for place, copy in zip(PLACES, self.copies[0]):
            if place[0] == matrix:
                copy.wait()


def forward_kernel(tick, unit, part_count, shard_count, first, handed, *refs):
    meta_ref, order_ref, vec_ref, fin_ref, cos_ref, sa_ref, sb_ref = refs[:7]
    if handed:
        recv_ref, *refs = refs[7:]
    else:
        refs = refs[7:]
    parts, refs = refs[:part_count], refs[part_count:]
    shards = refs[:shard_count]
    rest = refs[shard_count + (0 if first else 3) :]
    xb_ref, red_ref, kept_out, xo_out, lse_out = rest[:5]
    wqkv, wo, w1, w2, kept, xo, lse, looked, wsem, isem, osem = rest[5:]
    mats = (wqkv, wo, w1, w2)
    length = xb_ref.shape[0]
    slot = meta_ref[1 + tick]
    weights = Weights(meta_ref[0], shards, mats, wsem)
    width = looked.shape[2]

    def assemble():
        copies = [
            pltpu.make_async_copy(part.at[pl.ds(unit * length, length)], looked.at[k], isem.at[k])
            for k, part in enumerate(parts)
        ]
        for copy in copies:
            copy.start()
        for copy in copies:
            copy.wait()
        found = jnp.zeros((length, D), f32)
        for k in range(part_count):
            found = found + nn(looked[k], order_ref[k * width : (k + 1) * width, :])
        kept[:, COL_X : COL_X + D] = found.astype(bf16)

    weights.start(0)
    if handed:
        is_high = meta_ref[0] >= 2

        @pl.when(is_high)
        def _():
            copy = pltpu.make_async_copy(recv_ref, kept.at[:, pl.ds(COL_X, D)], isem.at[0])
            copy.start()
            copy.wait()

        pl.when(jnp.logical_not(is_high))(assemble)
    else:
        assemble()
    inputs = kept[:, COL_X : COL_X + D]
    stores = []

    def store(index, start, width):
        copy = pltpu.make_async_copy(
            kept.at[:, pl.ds(start, width)],
            kept_out.at[slot, :, pl.ds(start, width)],
            osem.at[index],
        )
        copy.start()
        stores.append(copy)

    hat, _ = normalized(inputs.astype(f32))
    kept[:, COL_A : COL_A + D] = (hat * vec_ref[:, V_G1 : V_G1 + D] + vec_ref[:, V_C1 : V_C1 + D]).astype(bf16)
    kept[:, COL_B : COL_B + D] = (hat * vec_ref[:, V_G2 : V_G2 + D] + vec_ref[:, V_C2 : V_C2 + D]).astype(bf16)
    weights.wait(0)
    weights.start(1, 2, 3)
    for part in range(3):
        at = part * D
        proj = nn(kept[:, COL_A : COL_A + D], wqkv[:, at : at + D])
        proj = proj + vec_ref[:, V_QKV + at : V_QKV + at + D]
        if part == 2:
            kept[:, COL_QKV + at : COL_QKV + at + D] = proj.astype(bf16)
        else:
            for p in range(D // PAIR):
                u = proj[:, p * PAIR : (p + 1) * PAIR]
                turned = (
                    u * cos_ref[...]
                    + pltpu.roll(u, PAIR - ROT // 2, 1) * sa_ref[...]
                    + pltpu.roll(u, ROT // 2, 1) * sb_ref[...]
                )
                kept[:, COL_QKV + at + p * PAIR : COL_QKV + at + (p + 1) * PAIR] = turned.astype(bf16)
    store(0, COL_QKV, 3 * D)
    store(1, COL_X, D)
    lse[HEADS:LSE_ROWS, :] = jnp.zeros((LSE_ROWS - HEADS, length), f32)

    scales = head_masks(1.0 / math.sqrt(HEAD))
    lane = lax.broadcasted_iota(jnp.int32, (1, PAIR), 1)
    k_at = lax.broadcasted_iota(jnp.int32, (QROWS, QROWS), 0)
    q_at = lax.broadcasted_iota(jnp.int32, (QROWS, QROWS), 1)

    def attend(p, carry):
        lanes = pl.multiple_of(p * PAIR, PAIR)
        for tile in range(length // QROWS):
            rows = pl.ds(tile * QROWS, QROWS)
            keys = (tile + 1) * QROWS
            q = kept[rows, pl.ds(COL_QKV + lanes, PAIR)]
            k = kept[pl.ds(0, keys), pl.ds(COL_QKV + D + lanes, PAIR)]
            v = kept[pl.ds(0, keys), pl.ds(COL_QKV + 2 * D + lanes, PAIR)]
            outs = []
            for side in range(2):
                s = nt(k, q * scales[side])
                near = jnp.where(k_at <= q_at, s[keys - QROWS :, :], -1e30)
                s = jnp.concatenate([s[: keys - QROWS, :], near], axis=0) if tile else near
                peak = jnp.max(s, axis=0, keepdims=True)
                expo = jnp.exp(s - peak)
                total = jnp.sum(expo, axis=0, keepdims=True)
                soft = (expo * (1.0 / total)).astype(bf16)
                outs.append(tn(soft, v))
                lse[pl.ds(2 * p + side, 1), rows] = peak + jnp.log(total)
            mixed = jnp.where(lane < HEAD, outs[0], outs[1])
            kept[rows, pl.ds(COL_O + lanes, PAIR)] = mixed.astype(bf16)
        return carry

    lax.fori_loop(0, HEADS // 2, attend, 0)
    weights.wait(1)
    out = kept[:, COL_X : COL_X + D].astype(f32) + (nn(kept[:, COL_O : COL_O + D], wo[...]) + vec_ref[:, V_O : V_O + D])
    store(2, COL_A, 3 * D)
    weights.wait(2)
    weights.wait(3)
    branch = jnp.zeros((length, D), f32) + vec_ref[:, V_B2 : V_B2 + D]
    for c in range(0, FF, CHUNK):
        h = nn(kept[:, COL_B : COL_B + D], w1[:, c : c + CHUNK]) + vec_ref[:, V_B1 + c : V_B1 + c + CHUNK]
        act, slope = gelu_both(h)
        kept[:, COL_H + c : COL_H + c + CHUNK] = act.astype(bf16)
        kept[:, COL_GP + c : COL_GP + c + CHUNK] = slope.astype(bf16)
        branch = branch + nn(kept[:, COL_H + c : COL_H + c + CHUNK], w2[c : c + CHUNK, :])
        store(5 + 2 * (c // CHUNK), COL_H + c, CHUNK)
        store(6 + 2 * (c // CHUNK), COL_GP + c, CHUNK)
    out = out + branch
    xo[...] = out
    xb_ref[...] = out.astype(bf16)
    tails = [
        pltpu.make_async_copy(xo, xo_out.at[slot], osem.at[3]),
        pltpu.make_async_copy(lse, lse_out.at[slot], osem.at[4]),
    ]
    for copy in tails:
        copy.start()
    hat, _ = normalized(out)
    final = (hat * fin_ref[:, :D] + fin_ref[:, D : 2 * D]).astype(bf16)
    red_ref[0:1, :] = jnp.sum(hat, axis=0, keepdims=True)
    red_ref[1:2, :] = jnp.sum(final.astype(f32), axis=0, keepdims=True)
    red_ref[2:8, :] = jnp.zeros((6, D), f32)
    for copy in stores + tails:
        copy.wait()


def forward(tick, meta, order, parts, unit, recv, vec, fin, tables, shards, state, slots):
    length = tables[0].shape[0]
    count = len(shards)
    first, handed = state is None, recv is not None
    whole = pl.BlockSpec(memory_space=pltpu.VMEM)
    anywhere = pl.BlockSpec(memory_space=pl.ANY)
    kept_shape = (
        jax.ShapeDtypeStruct((slots, length, KEPT), bf16),
        jax.ShapeDtypeStruct((slots, length, D), f32),
        jax.ShapeDtypeStruct((slots, LSE_ROWS, length), f32),
    )
    operands = [meta, order, vec, fin, *tables]
    if handed:
        operands.append(recv)
    operands += parts
    before = len(operands)
    operands = operands + [*shards] + ([] if first else list(state))
    return pl.pallas_call(
        functools.partial(forward_kernel, tick, unit, len(parts), count, first, handed),
        out_shape=(
            jax.ShapeDtypeStruct((length, D), bf16),
            jax.ShapeDtypeStruct((8, D), f32),
            *kept_shape,
        ),
        in_specs=[pl.BlockSpec(memory_space=pltpu.SMEM)]
        + [whole] * 6
        + [anywhere] * (len(operands) - 7),
        out_specs=(whole, whole, anywhere, anywhere, anywhere),
        input_output_aliases={} if first else {before + count + i: 2 + i for i in range(3)},
        scratch_shapes=[
            pltpu.VMEM((D, 3 * D), bf16),
            pltpu.VMEM((D, D), bf16),
            pltpu.VMEM((D, FF), bf16),
            pltpu.VMEM((FF, D), bf16),
            pltpu.VMEM((length, KEPT), bf16),
            pltpu.VMEM((length, D), f32),
            pltpu.VMEM((LSE_ROWS, length), f32),
            pltpu.VMEM((len(parts), length, parts[0].shape[1]), bf16),
            pltpu.SemaphoreType.DMA((len(PLACES),)),
            pltpu.SemaphoreType.DMA((len(parts),)),
            pltpu.SemaphoreType.DMA((5 + 2 * (FF // CHUNK),)),
        ],
        compiler_params=pltpu.CompilerParams(vmem_limit_bytes=VMEM_LIMIT),
        cost_estimate=pl.CostEstimate(flops=10 * 10**9, bytes_accessed=30 * 10**6, transcendentals=5 * 10**6),
        name="layer_forward",
    )(*operands)


def backward_kernel(tick, units, shard_count, handed, back_in, back_out, *refs):
    meta_ref, flag_ref, order_ref, vec_ref, fin_ref, cos_ref, sa_ref, sb_ref = refs[:8]
    if handed:
        recv_ref, *refs = refs[8:]
    else:
        refs = refs[8:]
    shards = refs[:shard_count]
    kept_in, xo_in, lse_in = refs[shard_count : 3 + shard_count]
    rest = refs[3 + shard_count + back_in :]
    dx_ref, vg_ref, kept_out = rest[:3]
    backs, rest = rest[3 : 3 + back_out], rest[3 + back_out :]
    wqkv, wo, w1, w2, qkv, gp, x, xo, lse, grads, dmix, dq, dk, dv, turned, wsem, isem, osem, bsem = rest
    mats = (wqkv, wo, w1, w2)
    length = cos_ref.shape[0]
    slot = meta_ref[1 + units + 2 + tick]
    weights = Weights(meta_ref[0], shards, mats, wsem)
    loads = [
        pltpu.make_async_copy(xo_in.at[slot], xo, isem.at[0]),
        pltpu.make_async_copy(kept_in.at[slot, :, pl.ds(COL_GP, FF)], gp, isem.at[1]),
        pltpu.make_async_copy(kept_in.at[slot, :, pl.ds(COL_X, D)], x, isem.at[2]),
        pltpu.make_async_copy(kept_in.at[slot, :, pl.ds(COL_QKV, 3 * D)], qkv, isem.at[3]),
        pltpu.make_async_copy(lse_in.at[slot], lse, isem.at[4]),
    ]
    loads[0].start()
    weights.start(1)
    loads[3].start()
    loads[4].start()
    loads[0].wait()
    hat, scale = normalized(xo[...])
    headed = fin_ref[:, 2 * D : 3 * D] * fin_ref[:, :D]
    top = flag_ref[min(tick, units - 1)] * norm_back(1.0, headed, hat, scale)
    if handed:
        top = jnp.where(meta_ref[0] >= 2, top, recv_ref[...].astype(f32))
    xo[...] = top
    grads[:, COL_G : COL_G + D] = xo[...].astype(bf16)
    bias = jnp.sum(grads[:, COL_G : COL_G + D].astype(f32), axis=0, keepdims=True)
    vg_ref[:, V_O : V_O + D] = bias
    vg_ref[:, V_B2 : V_B2 + D] = bias

    weights.wait(1)
    dmix[...] = nt(grads[:, COL_G : COL_G + D], wo[...]).astype(bf16)
    loads[3].wait()
    loads[4].wait()
    weights.start(3)
    loads[1].start()
    weights.start(2)
    loads[2].start()
    weights.start(0)
    scales = head_masks(1.0 / math.sqrt(HEAD))
    ones = head_masks(1.0)
    k_at = lax.broadcasted_iota(jnp.int32, (QROWS, QROWS), 0)
    q_at = lax.broadcasted_iota(jnp.int32, (QROWS, QROWS), 1)

    def attend(p, carry):
        lanes = pl.multiple_of(p * PAIR, PAIR)
        for tile in range(length // QROWS):
            rows = pl.ds(tile * QROWS, QROWS)
            keys = (tile + 1) * QROWS
            q = qkv[rows, pl.ds(lanes, PAIR)]
            k = qkv[pl.ds(0, keys), pl.ds(D + lanes, PAIR)]
            v = qkv[pl.ds(0, keys), pl.ds(2 * D + lanes, PAIR)]
            dm = dmix[rows, pl.ds(lanes, PAIR)]
            dq_sum = dk_sum = dv_sum = None
            for side in range(2):
                qs = q * scales[side]
                ks = k * scales[side]
                dms = dm * ones[side]
                s = nt(k, qs)
                soft = jnp.exp(s - lse[pl.ds(2 * p + side, 1), rows])
                near = jnp.where(k_at <= q_at, soft[keys - QROWS :, :], 0.0)
                soft = jnp.concatenate([soft[: keys - QROWS, :], near], axis=0) if tile else near
                dsoft = nt(v, dms)
                centre = jnp.sum(soft * dsoft, axis=0, keepdims=True)
                ds = (soft * (dsoft - centre)).astype(bf16)
                one_dv = nn(soft.astype(bf16), dms)
                one_dk = nn(ds, qs)
                one_dq = tn(ds, ks)
                if side:
                    dq_sum, dk_sum, dv_sum = dq_sum + one_dq, dk_sum + one_dk, dv_sum + one_dv
                else:
                    dq_sum, dk_sum, dv_sum = one_dq, one_dk, one_dv
            dq[rows, :] = dq_sum
            if tile:
                old = pl.ds(0, tile * QROWS)
                new = pl.ds(tile * QROWS, QROWS)
                dk[old, :] = dk[old, :] + dk_sum[: tile * QROWS]
                dk[new, :] = dk_sum[tile * QROWS :]
                dv[old, :] = dv[old, :] + dv_sum[: tile * QROWS]
                dv[new, :] = dv_sum[tile * QROWS :]
            else:
                dk[rows, :] = dk_sum
                dv[rows, :] = dv_sum
        for part, ref in ((0, dq), (1, dk)):
            g = ref[...]
            turned = (
                g * cos_ref[...]
                - pltpu.roll(g, PAIR - ROT // 2, 1) * sa_ref[...]
                - pltpu.roll(g, ROT // 2, 1) * sb_ref[...]
            )
            grads[:, pl.ds(COL_DP + part * D + lanes, PAIR)] = turned.astype(bf16)
        grads[:, pl.ds(COL_DP + 2 * D + lanes, PAIR)] = dv[...].astype(bf16)
        return carry

    lax.fori_loop(0, HEADS // 2, attend, 0)
    stores = [
        pltpu.make_async_copy(
            grads.at[:, pl.ds(COL_DP, 3 * D)], kept_out.at[slot, :, pl.ds(COL_QKV, 3 * D)], osem.at[2]
        )
    ]
    stores[0].start()
    weights.wait(3)
    loads[1].wait()
    loads[2].wait()
    weights.wait(2)
    second = jnp.zeros((length, D), f32)
    for c in range(0, FF, CHUNK):
        act = nt(grads[:, COL_G : COL_G + D], w2[c : c + CHUNK, :])
        pre = (act * gp[:, c : c + CHUNK].astype(f32)).astype(bf16)
        grads[:, COL_DH + c : COL_DH + c + CHUNK] = pre
        vg_ref[:, V_B1 + c : V_B1 + c + CHUNK] = jnp.sum(pre.astype(f32), axis=0, keepdims=True)
        second = second + nt(pre, w1[:, c : c + CHUNK])
    hat, scale = normalized(x[...].astype(f32))
    vg_ref[:, V_G2 : V_G2 + D] = jnp.sum(second * hat, axis=0, keepdims=True)
    vg_ref[:, V_C2 : V_C2 + D] = jnp.sum(second, axis=0, keepdims=True)
    xo[...] = xo[...] + norm_back(second, vec_ref[:, V_G2 : V_G2 + D], hat, scale)
    stores += [
        pltpu.make_async_copy(
            grads.at[:, pl.ds(COL_G, D)], kept_out.at[slot, :, pl.ds(COL_X, D)], osem.at[0]
        ),
        pltpu.make_async_copy(
            grads.at[:, pl.ds(COL_DH, FF)], kept_out.at[slot, :, pl.ds(COL_GP, FF)], osem.at[1]
        ),
    ]
    stores[1].start()
    stores[2].start()

    vg_ref[:, V_QKV : V_QKV + 3 * D] = jnp.sum(
        grads[:, COL_DP : COL_DP + 3 * D].astype(f32), axis=0, keepdims=True
    )
    weights.wait(0)
    one = nt(grads[:, COL_DP : COL_DP + 3 * D], wqkv[...])
    hat, scale = normalized(x[...].astype(f32))
    vg_ref[:, V_G1 : V_G1 + D] = jnp.sum(one * hat, axis=0, keepdims=True)
    vg_ref[:, V_C1 : V_C1 + D] = jnp.sum(one, axis=0, keepdims=True)
    total = xo[...] + norm_back(one, vec_ref[:, V_G1 : V_G1 + D], hat, scale)
    dx_ref[...] = total.astype(bf16)
    if back_out:
        turned[...] = nt(order_ref[...], dx_ref[...]).astype(bf16)
        start = (tick - 2) * length if tick <= units else 0
        width = backs[0].shape[0]
        for k, back in enumerate(backs):
            copy = pltpu.make_async_copy(
                turned.at[pl.ds(k * width, width)], back.at[:, pl.ds(start, length)], bsem.at[k]
            )
            copy.start()
            stores.append(copy)
    for copy in stores:
        copy.wait()


def backward(tick, units, meta, flags, order, recv, vec, fin, tables, shards, state, backs):
    length = tables[0].shape[0]
    count = len(shards)
    handed = recv is not None
    chips = len(PLACES) // shards[0].shape[0]
    spans = 0 if tick < 2 else (units - 1 if tick <= units else 1)
    back_shapes = [jax.ShapeDtypeStruct((D // chips, spans * length), bf16)] * (chips if spans else 0)
    whole = pl.BlockSpec(memory_space=pltpu.VMEM)
    anywhere = pl.BlockSpec(memory_space=pl.ANY)
    small = pl.BlockSpec(memory_space=pltpu.SMEM)
    operands = [meta, flags, order, vec, fin, *tables]
    if handed:
        operands.append(recv)
    dense = len(operands)
    operands = operands + [*shards, *state, *backs]
    aliases = {dense + count: 2} | {dense + count + 3 + i: 3 + i for i in range(len(backs))}
    return pl.pallas_call(
        functools.partial(backward_kernel, tick, units, count, handed, len(backs), len(back_shapes)),
        out_shape=(
            jax.ShapeDtypeStruct((length, D), bf16),
            jax.ShapeDtypeStruct((1, V_END), f32),
            jax.ShapeDtypeStruct(state[0].shape, bf16),
            *back_shapes,
        ),
        in_specs=[small, small] + [whole] * (dense - 2) + [anywhere] * (len(operands) - dense),
        out_specs=(whole, whole, anywhere) + (anywhere,) * len(back_shapes),
        input_output_aliases=aliases,
        scratch_shapes=[
            pltpu.VMEM((D, 3 * D), bf16),
            pltpu.VMEM((D, D), bf16),
            pltpu.VMEM((D, FF), bf16),
            pltpu.VMEM((FF, D), bf16),
            pltpu.VMEM((length, 3 * D), bf16),
            pltpu.VMEM((length, FF), bf16),
            pltpu.VMEM((length, D), bf16),
            pltpu.VMEM((length, D), f32),
            pltpu.VMEM((LSE_ROWS, length), f32),
            pltpu.VMEM((length, GRADS), bf16),
            pltpu.VMEM((length, D), bf16),
            pltpu.VMEM((length, PAIR), f32),
            pltpu.VMEM((length, PAIR), f32),
            pltpu.VMEM((length, PAIR), f32),
            pltpu.VMEM((D, length), bf16),
            pltpu.SemaphoreType.DMA((len(PLACES),)),
            pltpu.SemaphoreType.DMA((5,)),
            pltpu.SemaphoreType.DMA((3,)),
            pltpu.SemaphoreType.DMA((chips,)),
        ],
        compiler_params=pltpu.CompilerParams(vmem_limit_bytes=VMEM_LIMIT),
        cost_estimate=pl.CostEstimate(flops=20 * 10**9, bytes_accessed=40 * 10**6, transcendentals=5 * 10**6),
        name="layer_backward",
    )(*operands)


def product_kernel(left_at, right_at, count_ref, x_ref, y_ref, *refs):
    sent_ref = refs[0] if len(refs) == 4 else None
    out_ref, square_ref, turned = refs[-3:] if sent_ref is not None else (refs[0], None, refs[1])
    units, rows, width = x_ref.shape
    step = pl.program_id(0)
    before = left_at[jnp.maximum(step - 1, 0)]

    @pl.when(jnp.logical_or(step == 0, left_at[step] != before))
    def _():
        for unit in range(units):
            turned[:, unit * rows : (unit + 1) * rows] = jnp.transpose(x_ref[unit])

    found = nn(turned[...], y_ref[...].reshape(units * rows, -1))
    if sent_ref is None:
        for i in range(out_ref.shape[0]):
            out_ref[i] = found[:, i * TILE : (i + 1) * TILE]
        return

    @pl.when(step == 0)
    def _():
        square_ref[...] = jnp.zeros_like(square_ref)

    for i in range(out_ref.shape[0]):
        whole = found[:, i * TILE : (i + 1) * TILE] + sent_ref[i]
        out_ref[i] = whole.astype(bf16)
        weight = count_ref[step * out_ref.shape[0] + i].astype(f32)
        square_ref[...] += weight * jnp.sum(whole * whole, axis=0, keepdims=True)


def products(left_at, right_at, counted, kept, units, each, sent=None):
    steps = left_at.shape[0]
    length = kept.shape[1]
    block = pl.BlockSpec((each, TILE, TILE), lambda i, a, b, c: (i, 0, 0))
    shape = (steps * each, TILE, TILE)
    if sent is None:
        out_shape, out_specs, more = jax.ShapeDtypeStruct(shape, f32), block, []
    else:
        out_shape = (jax.ShapeDtypeStruct(shape, bf16), jax.ShapeDtypeStruct((1, TILE), f32))
        out_specs, more = (block, pl.BlockSpec((1, TILE), lambda i, a, b, c: (0, 0))), [sent]
    return pl.pallas_call(
        product_kernel,
        out_shape=out_shape,
        grid_spec=pltpu.PrefetchScalarGridSpec(
            num_scalar_prefetch=3,
            grid=(steps,),
            in_specs=[
                pl.BlockSpec((units, length, TILE), lambda i, a, b, c: (0, 0, a[i])),
                pl.BlockSpec((units, length, each * TILE), lambda i, a, b, c: (0, 0, b[i])),
            ]
            + [block] * len(more),
            out_specs=out_specs,
            scratch_shapes=[pltpu.VMEM((TILE, units * length), bf16)],
        ),
        compiler_params=pltpu.CompilerParams(vmem_limit_bytes=VMEM_LIMIT),
        cost_estimate=LIGHT,
        name="weight_products",
    )(left_at, right_at, counted, kept, kept, *more)


def lookup_kernel(ids_ref, embedding_ref, first_ref, rest_ref, table, wide):
    step = pl.program_id(0)
    features = embedding_ref.shape[0]
    lanes = table.shape[1]
    tiles = embedding_ref.shape[1] // lanes
    tokens = wide.shape[0]

    def turn(i):
        tile = embedding_ref[:, pl.ds(pl.multiple_of(i * lanes, lanes), lanes)]
        table[pl.ds(pl.multiple_of((step * tiles + i) * lanes, lanes), lanes), :features] = jnp.transpose(tile)

    def several(i, carry):
        for j in range(8):
            turn(i * 8 + j)
        return carry

    lax.fori_loop(0, tiles // 8, several, 0)
    for i in range(tiles // 8 * 8, tiles):
        turn(i)

    @pl.when(step == pl.num_programs(0) - 1)
    def _():
        def fetch(i, carry):
            for j in range(16):
                wide[pl.ds(i * 16 + j, 1), :] = table[pl.ds(ids_ref[i * 16 + j], 1), :]
            return carry

        lax.fori_loop(0, tokens // 16, fetch, 0)
        first = first_ref.shape[0]
        first_ref[...] = wide[:first, :features].astype(bf16)
        rest_ref[...] = wide[first:, :features].astype(bf16)


def lookup(ids, embedding, first):
    features, vocab = embedding.shape
    tokens = ids.shape[0]
    lanes = 128
    steps = 3 if vocab % (3 * lanes) == 0 else 1
    whole = lambda i: (0, 0)
    return pl.pallas_call(
        lookup_kernel,
        out_shape=(
            jax.ShapeDtypeStruct((first, features), bf16),
            jax.ShapeDtypeStruct((tokens - first, features), bf16),
        ),
        grid=(steps,),
        in_specs=[
            pl.BlockSpec(memory_space=pltpu.SMEM),
            pl.BlockSpec((features, vocab // steps), lambda i: (0, i)),
        ],
        out_specs=(
            pl.BlockSpec((first, features), whole),
            pl.BlockSpec((tokens - first, features), whole),
        ),
        scratch_shapes=[pltpu.VMEM((vocab, lanes), f32), pltpu.VMEM((tokens, lanes), f32)],
        compiler_params=pltpu.CompilerParams(vmem_limit_bytes=VMEM_LIMIT),
        cost_estimate=LIGHT,
        name="table_lookup",
    )(ids, embedding)


def table_kernel(ids_ref, *refs):
    parts = refs[:-5]
    out_ref, square_ref, table, wide, total = refs[-5:]
    step = pl.program_id(0)
    features = out_ref.shape[0]
    tokens = wide.shape[0]
    vocab, lanes = table.shape
    tiles = out_ref.shape[1] // lanes

    @pl.when(step == 0)
    def _():
        def clear(i, carry):
            table[pl.ds(pl.multiple_of(i * 3 * lanes, lanes), 3 * lanes), :] = jnp.zeros((3 * lanes, lanes), f32)
            return carry

        lax.fori_loop(0, vocab // (3 * lanes), clear, 0)
        total[...] = jnp.zeros_like(total)
        if features < lanes:
            wide[:, features:] = jnp.zeros((tokens, lanes - features), f32)
        start = 0
        for part in parts:

            def upright(i, carry, part=part, start=start):
                tile = part[:, pl.ds(pl.multiple_of(i * lanes, lanes), lanes)].astype(f32)
                wide[pl.ds(pl.multiple_of(start + i * lanes, lanes), lanes), :features] = jnp.transpose(tile)
                return carry

            lax.fori_loop(0, part.shape[1] // lanes, upright, 0)
            start += part.shape[1]

        def add(i, carry):
            for j in range(16):
                row = pl.ds(ids_ref[i * 16 + j], 1)
                table[row, :] = table[row, :] + wide[pl.ds(i * 16 + j, 1), :]
            return carry

        lax.fori_loop(0, tokens // 16, add, 0)

    def turn(i):
        tile = table[pl.ds(pl.multiple_of((step * tiles + i) * lanes, lanes), lanes), :]
        total[...] += tile * tile
        out_ref[:, pl.ds(pl.multiple_of(i * lanes, lanes), lanes)] = jnp.transpose(tile)[:features]

    def several(i, carry):
        for j in range(8):
            turn(i * 8 + j)
        return carry

    lax.fori_loop(0, tiles // 8, several, 0)
    for i in range(tiles // 8 * 8, tiles):
        turn(i)

    @pl.when(step == pl.num_programs(0) - 1)
    def _():
        square_ref[...] = jnp.sum(total[...], axis=0, keepdims=True)


def table_gradient(ids, parts, vocab):
    tokens, features = ids.shape[0], parts[0].shape[0]
    lanes = 128
    steps = 3 if vocab % (3 * lanes) == 0 else 1
    return pl.pallas_call(
        table_kernel,
        out_shape=(jax.ShapeDtypeStruct((features, vocab), f32), jax.ShapeDtypeStruct((1, lanes), f32)),
        grid=(steps,),
        in_specs=[
            pl.BlockSpec(memory_space=pltpu.SMEM),
        ]
        + [pl.BlockSpec(part.shape, lambda i: (0, 0), pipeline_mode=pl.Buffered(1)) for part in parts],
        out_specs=(
            pl.BlockSpec((features, vocab // steps), lambda i: (0, i)),
            pl.BlockSpec((1, lanes), lambda i: (0, 0)),
        ),
        scratch_shapes=[
            pltpu.VMEM((vocab, lanes), f32),
            pltpu.VMEM((tokens, lanes), f32),
            pltpu.VMEM((lanes, lanes), f32),
        ],
        compiler_params=pltpu.CompilerParams(vmem_limit_bytes=VMEM_LIMIT),
        cost_estimate=LIGHT,
        name="table_gradient",
    )(ids, *parts)


def split(value):
    high = value.astype(bf16)
    return high, (value - high.astype(f32)).astype(bf16)


def shampoo_kernel(factor_ref, g_ref, w_ref, ls_ref, rs_ref, lr_ref, rr_ref, bg_ref, nw_ref, nl_ref, nr_ref):
    factor = factor_ref[0]
    level = (1.0 - stats_decay) * factor * factor
    for i in range(g_ref.shape[0]):
        g = g_ref[i]
        bg_ref[i] = g.astype(f32) * factor
        nl_ref[i] = stats_decay * ls_ref[i] + level * nt(g, g)
        nr_ref[i] = stats_decay * rs_ref[i] + level * tn(g, g)
        right_high, right_low = split(rr_ref[i])
        inner = nn(g, right_high) + nn(g, right_low)
        inner_high, inner_low = split(inner)
        left_high, left_low = split(lr_ref[i])
        direction = nn(left_high, inner_high) + (nn(left_high, inner_low) + nn(left_low, inner_high))
        nw_ref[i] = w_ref[i] - (shampoo_rate * factor) * direction


def shampoo(factor, grad, weights, left_stats, right_stats, left_root, right_root):
    count = grad.shape[0]
    each = max(i for i in (1, 2, 3) if count % i == 0)
    block = pl.BlockSpec((each, TILE, TILE), lambda i: (i, 0, 0))
    shape = jax.ShapeDtypeStruct((count, TILE, TILE), f32)
    return pl.pallas_call(
        shampoo_kernel,
        out_shape=(shape,) * 4,
        grid=(count // each,),
        in_specs=[pl.BlockSpec(memory_space=pltpu.SMEM)] + [block] * 6,
        out_specs=(block,) * 4,
        compiler_params=pltpu.CompilerParams(vmem_limit_bytes=VMEM_LIMIT),
        cost_estimate=LIGHT,
        name="shampoo",
    )(factor, grad, weights, left_stats, right_stats, left_root, right_root)


def rope_columns(length):
    half_rot = ROT // 2
    lanes = jnp.arange(PAIR) % HEAD
    index = jnp.where(lanes < half_rot, lanes, lanes - half_rot).astype(f32)
    inverse = rope_base ** (-2.0 * index / ROT)
    angles = jnp.arange(length)[:, None].astype(f32) * inverse[None, :]
    cosine = jnp.where(lanes < ROT, jnp.cos(angles), 1.0)
    sine = jnp.where(lanes < ROT, jnp.sin(angles), 0.0)
    first = jnp.where(lanes < half_rot, -sine, 0.0)
    second = jnp.where(lanes < half_rot, 0.0, sine)
    return cosine, first, second


def adam_step(weight, moment, second, grad, rate, decay):
    moment_new = beta_first * moment + (1.0 - beta_first) * grad
    second_new = beta_second * second + (1.0 - beta_second) * grad * grad
    corrected = moment_new / (1.0 - beta_first**STEP)
    scaled = jnp.sqrt(second_new / (1.0 - beta_second**STEP)) + adam_eps
    return (moment_new, second_new, weight - rate * (corrected / scaled + decay * weight))


def rounded(values):
    return lax.reduce_precision(values, 8, 7)


def chosen(flags, values):
    total = values[-1]
    for flag, value in zip(flags[:-1], values[:-1]):
        total = jnp.where(flag, value, total)
    return total


def ordered(section, mine, other, axis):
    return jnp.concatenate(
        [jnp.where(section == 0, mine, other), jnp.where(section == 0, other, mine)], axis=axis
    )


def swapped(value):
    return lax.ppermute(value, "section", [(0, 1), (1, 0)])


def local(
    tokens,
    margins,
    tie_flags,
    embedding,
    embed_moment,
    embed_second,
    layer_blocks,
    left_stats,
    right_stats,
    left_root,
    right_root,
    layer_vectors,
    vector_moment,
    vector_second,
    closing_vectors,
    final_moment,
    final_second,
):
    both = ("section", "dp")
    count = lax.axis_size("dp")
    section = lax.axis_index("section")
    place = lax.axis_index("dp")
    low, high = count // 2 - 1, count // 2
    is_high = place >= high
    order_low = list(range(count - 1, low, -1)) + list(range(low + 1))
    order_high = [count - 1 - k for k in order_low]
    length = tokens.shape[2]
    units = tokens.shape[0] * count
    own_blocks = layer_blocks.shape[1]
    own_vector = layer_vectors.shape[1]
    own_final = closing_vectors.shape[0]
    features, vocab = embedding.shape

    own_closing = rounded(closing_vectors)
    pack = jnp.concatenate(
        [
            tokens.reshape(-1).astype(f32),
            margins.astype(f32),
            tie_flags.astype(f32),
            rounded(layer_vectors[0]),
            own_closing,
        ]
    )
    passed = [pack] + [
        lax.ppermute(pack, "dp", [(i, (i + d) % count) for i in range(count)]) for d in range(1, count)
    ]
    packs = jnp.stack(passed)

    own, packs = lax.optimization_barrier((layer_blocks[0].astype(bf16), packs))
    rounds = arrivals(count)
    received = []
    for pair in rounds:
        route = []
        for side, shard in enumerate(pair):
            route.append((shard, side * count + low))
            route.append((count + count - 1 - shard, (1 - side) * count + high))
        received.append(lax.ppermute(own, both, route))

    packs = packs[(place - jnp.arange(count)) % count]
    at = tokens.size
    ids = packs[:, :at].astype(jnp.int32).reshape(2, units, length)
    pair_margins = packs[:, at : at + margins.size].reshape(-1)
    at = at + margins.size
    pair_ties = packs[:, at : at + margins.size].reshape(-1)
    at = at + margins.size
    other_packs = swapped(packs[:, at:])
    layer_packs = jnp.where((section == 1) == is_high, packs[:, at:], other_packs)
    vec = layer_packs[:, :own_vector].reshape(1, -1)
    fin = ordered(section, packs[:, at + own_vector :], other_packs[:, own_vector:], 0).reshape(1, -1)
    tables = rope_columns(length)

    ids_here = jnp.where(section == 0, ids, ids[::-1])
    looked = lookup(
        jnp.concatenate([ids_here[:, :1].reshape(-1), ids_here[:, 1:].reshape(-1)]), embedding, 2 * length
    )

    def joined(rows):
        half = rows.shape[0] // 2
        return ordered(section, rows[:half], swapped(rows[half:]), 1)

    def sent_on(rows):
        return [rows if k == low else lax.ppermute(rows, "dp", [(k, low)]) for k in range(count)]

    looked = [joined(rows) for rows in looked]
    first = sent_on(looked[0])
    slot_at = jnp.arange(D)
    chip, within = slot_at // (2 * features), slot_at % (2 * features)
    feature_at = within // features * (D // 2) + chip * features + within % features
    order = (feature_at[:, None] == jnp.arange(D)[None, :]).astype(bf16)
    first, later, received, vec, fin, tables, order = lax.optimization_barrier(
        (first, looked[1], received, vec, fin, tables, order)
    )
    relays = [
        lax.ppermute(
            array, both, [(low, count + low), (count + low, low), (high, count + high), (count + high, high)]
        )
        for array in [own, *received]
    ]
    later, relays[-1] = lax.optimization_barrier((later, relays[-1]))
    later = sent_on(later)
    shards = [*received, *relays[1:], own, relays[0]]
    role = is_high * 2 + ((section == 1) == is_high) * 1

    slots = units + 1
    early = [*range(units), units, units]
    late = [units, units, *range(units)]
    meta = jnp.where(is_high, jnp.array([0, *late, *early]), jnp.array([0, *early, *late])).at[0].set(role)
    meta = meta.astype(jnp.int32)
    state = None
    arrived = []
    sums = []
    for tick in range(units + 2):
        unit = min(tick, units - 1)
        result, tail, *state = forward(
            tick,
            meta,
            order,
            later if unit else first,
            max(unit - 1, 0),
            arrived[tick - 2] if tick >= 2 else None,
            vec,
            fin,
            tables,
            shards,
            state,
            slots,
        )
        if tick < units:
            arrived.append(lax.ppermute(result, "dp", [(low, high)]))
        if tick >= 2:
            sums.append(tail[:2])
    sums = jnp.stack(sums)
    sum_hat, sum_final = sums[:, 0], sums[:, 1]
    final_gain, head = fin[0, :D], fin[0, 2 * D :]
    rewards = (jnp.sum(sum_final * head, axis=1) / length).reshape(-1, 2)
    pairs = units // 2
    gap = rewards[:, 0] - rewards[:, 1]
    half_margin = 0.5 * lax.dynamic_slice_in_dim(pair_margins, section * pairs, pairs, 0)
    tie = lax.dynamic_slice_in_dim(pair_ties, section * pairs, pairs, 0)
    pair_loss = (1.0 - tie) * jax.nn.softplus(half_margin - gap) + tie * 0.5 * (
        jax.nn.softplus(gap) + jax.nn.softplus(-gap)
    )
    gap_grad = -(1.0 - tie) * jax.nn.sigmoid(half_margin - gap) + tie * 0.5 * (
        jax.nn.sigmoid(gap) - jax.nn.sigmoid(-gap)
    )
    reward_grad = (jnp.stack([gap_grad, -gap_grad], axis=1) / length).reshape(-1)
    final_local = jnp.concatenate(
        [
            head * jnp.sum(reward_grad[:, None] * sum_hat, axis=0),
            head * (length * jnp.sum(reward_grad)),
            jnp.sum(reward_grad[:, None] * sum_final, axis=0),
        ]
    )

    def returned(parts):
        return chosen(
            [place == k for k in range(count)],
            [part if k == low else lax.ppermute(part, "dp", [(low, k)]) for k, part in enumerate(parts)],
        )

    def own_features(both_cores):
        mine, other = both_cores[:features], both_cores[features:]
        return [jnp.where(section == 0, mine, other), swapped(jnp.where(section == 0, other, mine))]

    arrived = []
    vector_sum = jnp.zeros((1, V_END), f32)
    backs = []
    token_grads = []
    for tick in range(units + 2):
        if tick == units + 1:
            token_grads.append(returned(backs))
            backs = []
        grad_in, vector_part, state[0], *backs = backward(
            tick,
            units,
            meta,
            reward_grad,
            order,
            arrived[tick - 2] if tick >= 2 else None,
            vec,
            fin,
            tables,
            shards,
            state,
            backs,
        )
        if tick < units:
            arrived.append(lax.ppermute(grad_in, "dp", [(high, low)]))
        live = jnp.where(is_high, tick < units, tick >= 2)
        vector_sum = vector_sum + jnp.where(live, vector_part, 0.0)
    token_grads.append(returned(backs))

    vector_pack = jnp.concatenate([vector_sum[0], jnp.where(place == high, final_local, 0.0)])
    vector_pack = vector_pack + swapped(vector_pack)
    own_rows = own_vector + own_final
    extra = -(-2 * own_rows // (16 * TILE)) * 16

    def vector_rows(k):
        values = jnp.concatenate(
            [
                lax.dynamic_slice_in_dim(vector_pack, k * own_vector, own_vector, 0),
                lax.dynamic_slice_in_dim(vector_pack, V_END + (section * count + k) * own_final, own_final, 0),
            ]
        )
        top = rounded(values)
        halves = jnp.concatenate([top.astype(bf16), (values - top).astype(bf16)])
        return jnp.pad(halves, (0, extra * TILE - 2 * own_rows)).reshape(extra, TILE)

    left_at = jnp.array([(0, 2, 4, 6)[m] + row for m, row, _ in PLACES], jnp.int32)
    right_at = jnp.array([(14, 28, 20, 28)[m] + col for m, _, col in PLACES], jnp.int32)
    part = (own_blocks + 1) // 2
    rest = own_blocks - part
    kept = state[0]
    each = 2 if own_blocks % 4 == 0 else 1

    def tiles_of(shards, half):
        places = jnp.concatenate([shard * own_blocks + half * rest + jnp.arange(0, part, each) for shard in shards])
        return left_at[places], right_at[places] // each

    live = (place == low) | (place == high)
    token_grads[0], left_at = lax.optimization_barrier((token_grads[0], left_at))
    squares = jnp.where(live & (section == 0), jnp.sum(vector_pack * vector_pack), 0.0)
    counted = jnp.where((jnp.arange(part) < part - rest) & (section == 1), 0, 1).astype(jnp.int32)
    group = max(count // 2, 1)
    counted = jnp.concatenate([counted] * group)
    sent, keeping, groups = [], [], []
    for start in range(0, count, group):
        steps = range(start, start + group)
        groups.append([jnp.where(is_high, order_high[step], order_low[step]) for step in steps])
        keeping.append(tiles_of(groups[-1], section))
        sums = products(*tiles_of(groups[-1], 1 - section), counted, kept, units, each)
        left_at, sums = lax.optimization_barrier((left_at, sums))
        sent.append(swapped(sums))
    pieces = []
    for start, shards_here, tiles, others in zip(range(0, count, group), groups, keeping, sent):
        if pieces:
            tiles, pieces = lax.optimization_barrier((tiles, pieces))
        total, block_squares = products(*tiles, counted, kept, units, each, others)
        squares = squares + jnp.where(live, jnp.sum(block_squares), 0.0)
        total = total.reshape(group, part * TILE, TILE)
        pieces += [
            jnp.concatenate([total[i], vector_rows(shard)], axis=0) for i, shard in enumerate(shards_here)
        ]
    for step in range(count - 1):
        route = [
            (core * count + source, core * count + target)
            for core in range(2)
            for source, target in ((low, order_low[step]), (high, order_high[step]))
        ]
        pieces[step] = lax.ppermute(pieces[step], both, route)
    token_grads[1], pieces[-1] = lax.optimization_barrier((token_grads[1], pieces[-1]))
    ids_ordered = jnp.concatenate(
        [ids_here[0, :-1], ids_here[1, :-1], ids_here[0, -1:], ids_here[1, -1:]], axis=0
    ).reshape(-1)
    table_grad, table_squares = table_gradient(
        ids_ordered, own_features(token_grads[0]) + own_features(token_grads[1]), vocab
    )

    loss = jnp.where(place == high, jnp.sum(pair_loss), 0.0)
    square_total, loss_total = lax.psum((squares + jnp.sum(table_squares), loss), both)
    norm_value = jnp.sqrt(square_total)
    factor = clip_limit / jnp.maximum(norm_value, clip_limit)
    embed_m, embed_v, embed_w = adam_step(
        embedding, embed_moment, embed_second, table_grad * factor, embed_rate, embed_decay
    )
    pieces, embed_w = lax.optimization_barrier((pieces, embed_w))
    piece_low = chosen([place == k for k in order_low], pieces)
    piece_high = chosen([place == k for k in order_high], pieces)
    mine = jnp.where(section == 0, piece_low, piece_high)
    other = swapped(jnp.where(section == 0, piece_high, piece_low)[: part * TILE])
    block_part, other = (value.reshape(part, TILE, TILE) for value in (mine[: part * TILE], other))
    grad_blocks = jnp.concatenate(
        [
            jnp.where(section == 0, block_part, other),
            jnp.where(section == 0, other, block_part)[2 * part - own_blocks :],
        ],
        axis=0,
    )

    def vectors_of(piece, start, width):
        rows = piece[part * TILE :].reshape(-1)
        return rows[start : start + width].astype(f32) + rows[own_rows + start : own_rows + start + width].astype(f32)

    owned_vector = vectors_of(mine, 0, own_vector)[None]
    owned_final = vectors_of(piece_high, own_vector, own_final)

    block_grad, new_blocks, new_left, new_right = (
        out[None]
        for out in shampoo(
            factor.reshape(1),
            grad_blocks,
            layer_blocks[0],
            left_stats[0],
            right_stats[0],
            left_root[0],
            right_root[0],
        )
    )
    vector_m, vector_v, vector_w = adam_step(
        layer_vectors, vector_moment, vector_second, owned_vector * factor, vector_rate, 0.0
    )
    final_m, final_v, final_w = adam_step(
        closing_vectors, final_moment, final_second, owned_final * factor, vector_rate, 0.0
    )
    return (
        loss_total.reshape(1),
        norm_value.reshape(1),
        block_grad,
        new_blocks,
        new_left,
        new_right,
        vector_m,
        vector_v,
        vector_w,
        final_m,
        final_v,
        final_w,
        embed_m,
        embed_v,
        embed_w,
    )


def solution(mesh):
    return jax.shard_map(
        local,
        mesh=mesh,
        in_specs=(
            P(("member", "dp"), None, None),
            P(("member", "dp")),
            P(("member", "dp")),
            P(("member", "section", "dp"), None),
            P(("member", "section", "dp"), None),
            P(("member", "section", "dp"), None),
            P(("member", "section"), "dp", None, None),
            P(("member", "section"), "dp", None, None),
            P(("member", "section"), "dp", None, None),
            P(("member", "section"), "dp", None, None),
            P(("member", "section"), "dp", None, None),
            P(("member", "section"), "dp"),
            P(("member", "section"), "dp"),
            P(("member", "section"), "dp"),
            P(("member", "section", "dp")),
            P(("member", "section", "dp")),
            P(("member", "section", "dp")),
        ),
        out_specs=(
            P("member"),
            P("member"),
            P(("member", "section"), "dp", None, None),
            P(("member", "section"), "dp", None, None),
            P(("member", "section"), "dp", None, None),
            P(("member", "section"), "dp", None, None),
            P(("member", "section"), "dp"),
            P(("member", "section"), "dp"),
            P(("member", "section"), "dp"),
            P(("member", "section", "dp")),
            P(("member", "section", "dp")),
            P(("member", "section", "dp")),
            P(("member", "section", "dp"), None),
            P(("member", "section", "dp"), None),
            P(("member", "section", "dp"), None),
        ),
        check_vma=False,
    )
```

time: 1140 us -> 837 us (0.73)
  waiting for transfers between devices: 256 us -> 47.4 us
  other arithmetic: 187 us -> 97.8 us
  local copies, waits for them, and re-layouts: 89.4 us -> 58.7 us
  blocking collectives: 18.8 us -> 48.2 us
  Pallas kernels: 488 us -> 509 us
  between operations: 23 us -> 9.18 us
    ppermute x20 -> x23, waiting for transfers between devices: 184 us -> 43.9 us  [the longest x6 31.5 us: sent_on(): lax.ppermute(rows, 'dp', [(k, low)])]
    psum x1 -> x0, waiting for transfers between devices: 55.3 us -> none  [local(): vector_all = lax.psum(vector_pack, both)]
    scatter-add x1 -> x0, other arithmetic: 32.9 us -> none  [local(): jax.ops.segment_sum(token_grads.T.astype(f32), ids, num_segments=vocab)]
    psum x1, blocking collectives: 18.8 us -> 48.2 us  [local(): lax.psum((squares + jnp.sum(table_squares), loss), both)]
    convert_element_type x7, other arithmetic: 32.9 us -> 6.39 us  [the longest x1 3.47 us: local(): own, packs = lax.optimization_barrier((layer_blocks[0].astype(bf16), packs))]
    scatter-add x1 -> x0, local copies, waits for them, and re-layouts: 23.2 us -> none  [local(): jax.ops.segment_sum(token_grads.T.astype(f32), ids, num_segments=vocab)]
    select_n x15 -> x18, other arithmetic: 31.7 us -> 11 us  [the longest x1 3.83 us: local(): mine = jnp.where(section == 0, piece_low, piece_high)]
    pallas_call x21 -> x19, Pallas kernels: 488 us -> 509 us  [the longest x6 194 us: forward(): pl.pallas_call(functools.partial(forward_kernel, tick, unit, len(parts),...]
  transfers between devices with their start and end apart: 37 -> 40, of which waited for: 5 -> 3; matrix products, arithmetic and copies ran while one was open for 18% -> 16% of each run, Pallas kernels for 26% -> 49%
where the time goes in v2:
time: 837 us; the launch traced here: 827 us
  Pallas kernels  509 us (61%)
  other arithmetic  97.8 us (12%)
  local copies, waits for them, and re-layouts  58.7 us (7%)
  starting transfers between devices  57.3 us (7%)
  blocking collectives  48.2 us (6%)
  waiting for transfers between devices  47.4 us (6%)
  between operations  9.18 us (1%)
    pallas_call x6, Pallas kernels, forward(): pl.pallas_call(functools.partial(forward_kernel, tick, unit, len(parts),...  194 us
    pallas_call x6, Pallas kernels, backward(): pl.pallas_call(functools.partial(backward_kernel, tick, units, count, han...  166 us
    pallas_call x4, Pallas kernels, products(): pl.pallas_call(product_kernel, out_shape=out_shape, grid_spec=pltpu.Prefe...  68.8 us
    sub x3, other arithmetic, adam_step(): weight - rate * (corrected / scaled + decay * weight)  49.7 us
    psum x1, blocking collectives, local(): lax.psum((squares + jnp.sum(table_squares), loss), both)  48.2 us
    pallas_call x1, Pallas kernels, table_gradient(): pl.pallas_call(table_kernel, out_shape=(jax.ShapeDtypeStruct((features, v...  35 us
    ppermute x6, waiting for transfers between devices, sent_on(): lax.ppermute(rows, 'dp', [(k, low)])  31.5 us
    pallas_call x1, Pallas kernels, shampoo(): pl.pallas_call(shampoo_kernel, out_shape=(shape,) * 4, grid=(count // eac...  26.3 us
  transfers between devices with their start and end apart: 40, of which 3 were waited for; matrix products, arithmetic and copies ran while one was open for 16% of the time, Pallas kernels for 49%

profile of v2, /device:TPU:0, one launch (start us, length us, event | category | flops | bytes accessed | tf_op | source)
XLA Modules:
  0.0 827.1 jit_solution(6173640595253336694)
XLA Ops:
  4.1 5.1 collective-permute-start.2
  10.8 3.5 bitcast_convert_fusion.refs_15_.refs_16_.refs_12_.refs_13_
  18.1 1.4 pad_maximum_fusion.7
  19.5 6.1 collective-permute-start.9
  25.7 2.5 collective-permute-start.8
  28.2 2.6 fusion.4
  32.1 2.0 gather_fusion
  34.1 1.3 slice_convert_fusion
  36.8 1.5 slice.206
  38.9 1.3 pad_add_fusion.ids_ref
  40.3 18.4 %table_lookup.1 = (bf16[1024,96]{1,0:T(8,128)(2,1)}, bf16[3072,96]{1,0:T(8,128)(2,1)}) custom-call(s32[4096]{0:T(1024)} %pad_add_fusion.ids_ref, f32[96,50304]{1,0:T(8,128)} %embedding_ref.1), custom_call_target="tpu_custom_call" | custom-call | flops 1 | bytes 1 | tf_op jit(solution)/shard_map/table_lookup/pallas_call | solution.py:664
  58.7 1.6 slice.147
  60.8 1.8 slice.149
  63.8 1.5 reshape.465.refs_2_.refs_3_
  70.1 1.4 collective-permute-start.4
  73.9 31.5 %collective-permute-done.4.refs_7_ = bf16[512,192]{1,0:T(8,128)(2,1)S(1)} collective-permute-done((bf16[512,192]{1,0:T(8,128)(2,1)S(1)}, bf16[512,192]{1,0:T(8,128)(2,1)S(1)}, u32[]{:S(2)}, u32[]{:S(2)}) %collective-permute-start.4) | collective-permute-done | bytes 196640 | tf_op jit(solution)/shard_map/ppermute | solution.py:932
  105.5 2.4 collective-permute-start.12
  107.9 2.5 collective-permute-start.13
  110.4 2.4 collective-permute-start.11
  119.3 1.4 fusion.76
  121.3 2.2 copy.67
  123.5 1.5 collective-permute-start.17
  125.0 1.5 collective-permute-start.16
  126.5 11.4 %collective-permute-start.15 = (bf16[1536,192]{0,1:T(8,128)(2,1)}, bf16[1536,192]{0,1:T(8,128)(2,1)}, u32[]{:S(2)}, u32[]{:S(2)}) collective-permute-start(bf16[1536,192]{0,1:T(8,128)(2,1)} %copy.67), channel_id=1, source_target_pairs={{0,1},{4,5},{8,9},{12,13},{16,17},{20,21},{24,25},{28,29}} | collective-permute-start | bytes 1769480 | tf_op jit(solution)/shard_map/ppermute | solution.py:932
  138.0 30.7 %layer_forward.6 = (bf16[512,768]{1,0:T(8,128)(2,1)}, f32[8,768]{1,0:T(8,128)}, bf16[5,512,11520]{2,1,0:T(8,128)(2,1)}, f32[5,512,768]{2,1,0:T(8,128)}, f32[5,16,512]{2,1,0:T(8,128)}) custom-call(s32[13]{0:T(128)} %copy-done.24, bf16[768,768]{1,0:T(8,128)(2,1)} %fusion.1.refs_1_.refs_2_, f32[1,9984]{1,0:T(1,128)} %reshape.465.refs_2_.refs_3_, ...), custom_call_target="tpu_custom_call" | custom-call | flops 10000000000 | bytes 30000000 | tf_op jit(solution)/shard_map/layer_forward/pallas_call | solution.py:321
  169.4 2.2 copy.75.refs_10_.refs_11_
  171.6 2.2 copy.74.refs_9_.refs_10_
  173.8 2.2 copy.73.refs_7_.refs_8_
  176.1 41.0 %layer_forward.7 = (bf16[512,768]{1,0:T(8,128)(2,1)}, f32[8,768]{1,0:T(8,128)}, bf16[5,512,11520]{2,1,0:T(8,128)(2,1)}, f32[5,512,768]{2,1,0:T(8,128)}, f32[5,16,512]{2,1,0:T(8,128)}) custom-call(s32[13]{0:T(128)} %copy-done.24, bf16[768,768]{1,0:T(8,128)(2,1)} %fusion.1.refs_1_.refs_2_, ...), custom_call_target="tpu_custom_call", output_to_operand_aliasing={{2}: (17, {}), {3}: (18, {}), {4}: (19, {})} | custom-call | flops 10000000000 | bytes 30000000 | tf_op jit(solution)/shard_map/layer_forward/pallas_call | solution.py:321
  218.7 30.6 %layer_forward.8 = (bf16[512,768]{1,0:T(8,128)(2,1)}, f32[8,768]{1,0:T(8,128)}, bf16[5,512,11520]{2,1,0:T(8,128)(2,1)}, f32[5,512,768]{2,1,0:T(8,128)}, f32[5,16,512]{2,1,0:T(8,128)}) custom-call(s32[13]{0:T(128)} %copy-done.24, bf16[768,768]{1,0:T(8,128)(2,1)} %fusion.1.refs_1_.refs_2_, ...), custom_call_target="tpu_custom_call", output_to_operand_aliasing={{2}: (18, {}), {3}: (19, {}), {4}: (20, {})} | custom-call | flops 10000000000 | bytes 30000000 | tf_op jit(solution)/shard_map/layer_forward/pallas_call | solution.py:321
  251.7 30.4 %layer_forward.9 = (bf16[512,768]{1,0:T(8,128)(2,1)}, f32[8,768]{1,0:T(8,128)}, bf16[5,512,11520]{2,1,0:T(8,128)(2,1)}, f32[5,512,768]{2,1,0:T(8,128)}, f32[5,16,512]{2,1,0:T(8,128)}) custom-call(s32[13]{0:T(128)} %copy-done.24, bf16[768,768]{1,0:T(8,128)(2,1)} %fusion.1.refs_1_.refs_2_, ...), custom_call_target="tpu_custom_call", output_to_operand_aliasing={{2}: (18, {}), {3}: (19, {}), {4}: (20, {})} | custom-call | flops 10000000000 | bytes 30000000 | tf_op jit(solution)/shard_map/layer_forward/pallas_call | solution.py:321
  284.5 30.6 %layer_forward.10 = (bf16[512,768]{1,0:T(8,128)(2,1)}, f32[8,768]{1,0:T(8,128)}, bf16[5,512,11520]{2,1,0:T(8,128)(2,1)}, f32[5,512,768]{2,1,0:T(8,128)}, f32[5,16,512]{2,1,0:T(8,128)}) custom-call(s32[13]{0:T(128)} %copy-done.24, bf16[768,768]{1,0:T(8,128)(2,1)} %fusion.1.refs_1_.refs_2_, ...), custom_call_target="tpu_custom_call", output_to_operand_aliasing={{2}: (18, {}), {3}: (19, {}), {4}: (20, {})} | custom-call | flops 10000000000 | bytes 30000000 | tf_op jit(solution)/shard_map/layer_forward/pallas_call | solution.py:321
  316.8 30.4 %layer_forward.11 = (bf16[512,768]{1,0:T(8,128)(2,1)}, f32[8,768]{1,0:T(8,128)}, bf16[5,512,11520]{2,1,0:T(8,128)(2,1)}, f32[5,512,768]{2,1,0:T(8,128)}, f32[5,16,512]{2,1,0:T(8,128)}) custom-call(s32[13]{0:T(128)} %copy-done.24, bf16[768,768]{1,0:T(8,128)(2,1)} %fusion.1.refs_1_.refs_2_, ...), custom_call_target="tpu_custom_call", output_to_operand_aliasing={{2}: (18, {}), {3}: (19, {}), {4}: (20, {})} | custom-call | flops 10000000000 | bytes 30000000 | tf_op jit(solution)/shard_map/layer_forward/pallas_call | solution.py:321
  351.4 26.6 %layer_backward.6 = (bf16[512,768]{1,0:T(8,128)(2,1)}, f32[1,9984]{1,0:T(1,128)}, bf16[5,512,11520]{2,1,0:T(8,128)(2,1)}) custom-call(s32[13]{0:T(128)} %copy-done.24, f32[4]{0:T(128)} %div.145.refs_1_, bf16[768,768]{1,0:T(8,128)(2,1)} %fusion.1.refs_1_.refs_2_, f32[1,9984]{1,0:T(1,128)} %reshape.465.refs_2_.refs_3_, ...), custom_call_target="tpu_custom_call", output_to_operand_aliasing={{2}: (14, {})} | custom-call | flops 20000000000 | bytes 40000000 | tf_op jit(solution)/shard_map/layer_backward/pallas_call | solution.py:528
  378.8 26.4 %layer_backward.7 = (bf16[512,768]{1,0:T(8,128)(2,1)}, f32[1,9984]{1,0:T(1,128)}, bf16[5,512,11520]{2,1,0:T(8,128)(2,1)}) custom-call(s32[13]{0:T(128)} %copy-done.24, f32[4]{0:T(128)} %div.145.refs_1_, bf16[768,768]{1,0:T(8,128)(2,1)} %fusion.1.refs_1_.refs_2_, f32[1,9984]{1,0:T(1,128)} %reshape.465.refs_2_.refs_3_, ...), custom_call_target="tpu_custom_call", output_to_operand_aliasing={{2}: (14, {})} | custom-call | flops 20000000000 | bytes 40000000 | tf_op jit(solution)/shard_map/layer_backward/pallas_call | solution.py:528
  406.8 28.4 %layer_backward.8 = (bf16[512,768]{1,0:T(8,128)(2,1)}, f32[1,9984]{1,0:T(1,128)}, bf16[5,512,11520]{2,1,0:T(8,128)(2,1)}, bf16[192,1536]{1,0:T(8,128)(2,1)}, bf1...) custom-call(s32[13]{0:T(128)} %copy-done.24, ...), custom_call_target="tpu_custom_call", output_to_operand_aliasing={{2}: (15, {})} | custom-call | flops 20000000000 | bytes 40000000 | tf_op jit(solution)/shard_map/layer_backward/pallas_call | solution.py:528
  436.9 28.2 %layer_backward.9 = (bf16[512,768]{1,0:T(8,128)(2,1)}, f32[1,9984]{1,0:T(1,128)}, bf16[5,512,11520]{2,1,0:T(8,128)(2,1)}, bf16[192,1536]{1,0:T(8,128)(2,1)}, bf1...) custom-call(s32[13]{0:T(128)} %copy-done.24, ...), custom_call_target="tpu_custom_call", output_to_operand_aliasing={{2}: (15, {}), {3}: (18, {}), {4}: (19, {}), {5}: (20, {}),... | custom-call | flops 20000000000 | bytes 40000000 | tf_op jit(solution)/shard_map/layer_backward/pallas_call | solution.py:528
  466.7 28.4 %layer_backward.10 = (bf16[512,768]{1,0:T(8,128)(2,1)}, f32[1,9984]{1,0:T(1,128)}, bf16[5,512,11520]{2,1,0:T(8,128)(2,1)}, bf16[192,1536]{1,0:T(8,128)(2,1)}, bf...) custom-call(s32[13]{0:T(128)} %copy-done.24, ...), custom_call_target="tpu_custom_call", output_to_operand_aliasing={{2}: (15, {}), {3}: (18, {}), {4}: (19, {}), {5}: (20, {}),... | custom-call | flops 20000000000 | bytes 40000000 | tf_op jit(solution)/shard_map/layer_backward/pallas_call | solution.py:528
  498.7 28.2 %layer_backward.11 = (bf16[512,768]{1,0:T(8,128)(2,1)}, f32[1,9984]{1,0:T(1,128)}, bf16[5,512,11520]{2,1,0:T(8,128)(2,1)}, bf16[192,512]{1,0:T(8,128)(2,1)}, bf1...) custom-call(s32[13]{0:T(128)} %copy-done.24, ...), custom_call_target="tpu_custom_call", output_to_operand_aliasing={{2}: (15, {})} | custom-call | flops 20000000000 | bytes 40000000 | tf_op jit(solution)/shard_map/layer_backward/pallas_call | solution.py:528
  528.4 16.8 %weight_products.4 = f32[12,384,384]{2,1,0:T(8,128)} custom-call(s32[6]{0:T(128)} %gather_fusion.3, s32[6]{0:T(128)} %get-tuple-element.309.right_at, s32[12]{0:T(128)} %concatenate.182.count_ref, bf16[5,512,11520]{2,1,0:T(8,128)(2,1)} %get-tuple-element.203.x_ref.y_ref, bf16[5,512,11520]{2,1,0:T(8,128)(2,1)} %get-tuple-element.203.x_ref.y_ref), custom_call_target="tpu_custom_call" | custom-call | flops 1 | bytes 1 | tf_op jit(solution)/shard_map/weight_products/pallas_call | solution.py:605
  546.8 16.1 %weight_products.6 = f32[12,384,384]{2,1,0:T(8,128)} custom-call(s32[6]{0:T(128)} %gather_fusion.7, s32[6]{0:T(128)} %get-tuple-element.308.right_at, s32[12]{0:T(128)} %concatenate.182.count_ref, bf16[5,512,11520]{2,1,0:T(8,128)(2,1)} %get-tuple-element.203.x_ref.y_ref, bf16[5,512,11520]{2,1,0:T(8,128)(2,1)} %get-tuple-element.203.x_ref.y_ref), custom_call_target="tpu_custom_call" | custom-call | flops 1 | bytes 1 | tf_op jit(solution)/shard_map/weight_products/pallas_call | solution.py:605
  562.9 1.5 collective-permute-start.30
  571.9 3.4 collective-permute-done.25
  578.2 12.3 %collective-permute-done.33 = bf16[192,512]{1,0:T(8,128)(2,1)S(1)} collective-permute-done((bf16[192,512]{1,0:T(8,128)(2,1)S(1)}, bf16[192,512]{1,0:T(8,128)(2,1)S(1)}, u32[]{:S(2)}, u32[]{:S(2)}) %collective-permute-start.33) | collective-permute-done | bytes 196640 | tf_op jit(solution)/shard_map/ppermute | solution.py:1008
  593.6 17.6 %weight_products.5 = (bf16[12,384,384]{2,1,0:T(8,128)(2,1)}, f32[1,384]{1,0:T(1,128)}) custom-call(s32[6]{0:T(128)} %gather_fusion.1, s32[6]{0:T(128)} %and_select_fusion.3.right_at, s32[12]{0:T(128)} %concatenate.182.count_ref, bf16[5,512,11520]{2,1,0:T(8,128)(2,1)} %get-tuple-element.203.x_ref.y_ref, ...), custom_call_target="tpu_custom_call" | custom-call | flops 1 | bytes 1 | tf_op jit(solution)/shard_map/weight_products/pallas_call | solution.py:605
  613.2 2.4 fusion.75
  615.5 1.4 pad_maximum_fusion.2
  616.9 1.4 pad_maximum_fusion.1
  618.3 18.3 %weight_products.7 = (bf16[12,384,384]{2,1,0:T(8,128)(2,1)}, f32[1,384]{1,0:T(1,128)}) custom-call(s32[6]{0:T(128)} %gather_fusion.5, s32[6]{0:T(128)} %and_select_fusion.1.right_at, s32[12]{0:T(128)} %concatenate.182.count_ref, bf16[5,512,11520]{2,1,0:T(8,128)(2,1)} %get-tuple-element.203.x_ref.y_ref, ...), custom_call_target="tpu_custom_call" | custom-call | flops 1 | bytes 1 | tf_op jit(solution)/shard_map/weight_products/pallas_call | solution.py:605
  639.8 1.9 collective-permute-start.37
  641.7 2.4 fusion.74
  644.1 1.5 pad_maximum_fusion.3
  646.2 1.4 pad_maximum_fusion.4
  649.7 35.0 %table_gradient.1 = (f32[96,50304]{1,0:T(8,128)}, f32[1,128]{1,0:T(1,128)}) custom-call(s32[4096]{0:T(1024)} %bitcast.90, bf16[96,1536]{1,0:T(8,128)(2,1)} %get-tuple-element.266.refs_0_, bf16[96,1536]{1,0:T(8,128)(2,1)} %copy-done.15, bf16[96,512]{1,0:T(8,128)(2,1)} %get-tuple-element.270.refs_2_, bf16[96,512]{1,0:T(8,128)(2,1)} %copy-done.23), custom_call_target="tpu_custom_call" | custom-call | flops 1 | bytes 1 | tf_op jit(solution)/shard_map/table_gradient/pallas_call | solution.py:747
  686.6 48.2 %all-reduce.5 = (f32[1]{0:T(128)}, f32[]{:T(128)}) all-reduce(f32[1]{0:T(128)} %bitcast.9, f32[]{:T(128)S(6)} %add.559), channel_id=1, replica_groups=mesh['member'=4,'section'=2,'dp'=4] {'section','dp'}, use_global_device_ids=true, to_apply=%region_2.3 | all-reduce | flops 2 | bytes 16 | tf_op jit(solution)/shard_map/psum | solution.py:1110
  735.5 46.9 %multiply_subtract_fusion = (f32[96,50304]{1,0:T(8,128)}, f32[96,50304]{1,0:T(8,128)}, f32[96,50304]{1,0:T(8,128)}) fusion(f32[96,50304]{1,0:T(8,128)} %embedding_ref.1, f32[96,50304]{1,0:T(8,128)} %get-tuple-element.223, f32[]{:T(128)} %div.158, f32[96,50304]{1,0:T(8,128)} %param.27, f32[96,50304]{1,0:T(8,128)} %param.28), kind=kLoop, calls=%fused_computation.11 | loop fusion | flops 77266944 | bytes 135217152 | tf_op jit(solution)/shard_map/sub | solution.py:826
  783.6 3.8 broadcast_select_fusion
  787.5 1.4 slice_select_fusion
  789.9 1.3 reshape.476
  791.8 1.3 reshape.475
  793.1 1.4 multiply_subtract_fusion.2
  795.4 1.4 multiply_subtract_fusion.1
  797.1 2.2 pad_maximum_fusion.g_ref
  799.3 26.3 %shampoo.1 = (f32[12,384,384]{2,1,0:T(8,128)}, f32[12,384,384]{2,1,0:T(8,128)}, f32[12,384,384]{2,1,0:T(8,128)}, f32[12,384,384]{2,1,0:T(8,128)}) custom-call(f32[1]{0:T(128)} %bitcast.30.factor_ref, bf16[12,384,384]{2,1,0:T(8,128)(2,1)} %pad_maximum_fusion.g_ref, f32[12,384,384]{2,1,0:T(8,128)} %bitcast.79, f32[12,384,384]{2,1,0:T(8,128)} %bitcast.86, ...), custom_call_target="tpu_custom_call" | custom-call | flops 1 | bytes 1 | tf_op jit(solution)/shard_map/shampoo/pallas_call | solution.py:796
  (271 shorter events, 74.7 us)
Async XLA Ops:
  4.1 11.7 %collective-permute-start.2 = (f32[3810]{0:T(1024)S(1)}, f32[3810]{0:T(1024)}, u32[]{:S(2)}, u32[]{:S(2)}) collective-permute-start(f32[3810]{0:T(1024)S(1)} %concatenate.172), channel_id=1, source_target_pairs={{0,3},{1,0},{2,1},{3,2},{4,7},{5,4},{6,5},{7,6},{8,11},{9,8},{10,9... | collective-permute-start | bytes 45728 | tf_op jit(solution)/shard_map/ppermute | solution.py:895
  9.2 7.4 collective-permute-start.1
  9.2 8.1 collective-permute-start
  14.3 93.6 %copy-start.3 = (bf16[12,384,384]{2,1,0:T(8,128)(2,1)}, bf16[12,384,384]{2,1,0:T(8,128)(2,1)S(1)}, u32[]{:S(2)}) copy-start(bf16[12,384,384]{2,1,0:T(8,128)(2,1)S(1)} %bitcast_convert_fusion.refs_15_.refs_16_.refs_12_.refs_13_) | copy-start | bytes 10616836
  19.5 85.9 %collective-permute-start.9 = (bf16[12,384,384]{2,1,0:T(8,128)(2,1)S(1)}, bf16[12,384,384]{2,1,0:T(8,128)(2,1)}, u32[]{:S(2)}, u32[]{:S(2)}) collective-permute-start(bf16[12,384,384]{2,1,0:T(8,128)(2,1)S(1)} %bitcast_convert_fusion.refs_15_.refs_16_.refs_12_.refs_13_), channel_id=1, source_target_pairs={{0,1},{7,6},{8,9},{15,14},{16,17},{23,22},{24,25},{31,30}} | collective-permute-start | bytes 10616840 | tf_op jit(solution)/shard_map/ppermute | solution.py:907
  25.7 79.8 %collective-permute-start.8 = (bf16[12,384,384]{2,1,0:T(8,128)(2,1)S(1)}, bf16[12,384,384]{2,1,0:T(8,128)(2,1)}, u32[]{:S(2)}, u32[]{:S(2)}) collective-permute-start(bf16[12,384,384]{2,1,0:T(8,128)(2,1)S(1)} %bitcast_convert_fusion.refs_15_.refs_16_.refs_12_.refs_13_), channel_id=1, source_target_pairs={{3,1},{4,6},{2,5},{5,2},{11,9},{12,14},{10,13},{13,10},{19,17},{20... | collective-permute-start | bytes 10616840 | tf_op jit(solution)/shard_map/ppermute | solution.py:907
  38.9 23.6 %collective-permute-start.10 = (f32[4,2784]{1,0:T(4,128)}, f32[4,2784]{1,0:T(4,128)S(1)}, u32[]{:S(2)}, u32[]{:S(2)}) collective-permute-start(f32[4,2784]{1,0:T(4,128)} %slice.206), channel_id=1, source_target_pairs={{0,4},{4,0},{1,5},{5,1},{2,6},{6,2},{3,7},{7,3},{8,12},{12,8},{9,1... | collective-permute-start | bytes 133640 | tf_op jit(solution)/shard_map/ppermute | solution.py:847
  40.3 22.9 %copy-start.20 = (f32[4,2784]{1,0:T(4,128)S(1)}, f32[4,2784]{1,0:T(4,128)}, u32[]{:S(2)}) copy-start(f32[4,2784]{1,0:T(4,128)} %slice.206) | copy-start | bytes 133636
  58.7 55.4 %copy-start.1 = (s32[48]{0:T(128)S(1)}, s32[48]{0:T(128)}, u32[]{:S(2)}) copy-start(s32[48]{0:T(128)} %constant.249.clone) | copy-start | bytes 580
  60.3 7.2 collective-permute-start.3
  62.6 7.5 collective-permute-start.7
  67.5 70.5 %copy-start.6 = (f32[1,2304]{1,0:T(1,128)}, f32[1,2304]{1,0:T(1,128)S(1)}, u32[]{:S(2)}) copy-start(f32[1,2304]{1,0:T(1,128)S(1)} %reshape.466.refs_3_.refs_4_) | copy-start | bytes 27652
  68.7 41.7 %copy-start.16 = (bf16[512,192]{1,0:T(8,128)(2,1)}, bf16[512,192]{1,0:T(8,128)(2,1)S(1)}, u32[]{:S(2)}) copy-start(bf16[512,192]{1,0:T(8,128)(2,1)S(1)} %pad_maximum_fusion.6.refs_8_) | copy-start | bytes 589828
  68.7 5.2 collective-permute-start.6
  69.4 4.6 collective-permute-start.5
  70.1 35.4 %collective-permute-start.4 = (bf16[512,192]{1,0:T(8,128)(2,1)S(1)}, bf16[512,192]{1,0:T(8,128)(2,1)S(1)}, u32[]{:S(2)}, u32[]{:S(2)}) collective-permute-start(bf16[512,192]{1,0:T(8,128)(2,1)S(1)} %pad_maximum_fusion.6.refs_8_), channel_id=1, source_target_pairs={{0,1},{4,5},{8,9},{12,13},{16,17},{20,21},{24,25},{28,29}} | collective-permute-start | bytes 589832 | tf_op jit(solution)/shard_map/ppermute | solution.py:932
  73.9 36.5 %copy-start.43 = (bf16[512,192]{1,0:T(8,128)(2,1)}, bf16[512,192]{1,0:T(8,128)(2,1)S(1)}, u32[]{:S(2)}) copy-start(bf16[512,192]{1,0:T(8,128)(2,1)S(1)} %collective-permute-done.6.refs_10_) | copy-start | bytes 589828
  73.9 36.5 %copy-start.44 = (bf16[512,192]{1,0:T(8,128)(2,1)}, bf16[512,192]{1,0:T(8,128)(2,1)S(1)}, u32[]{:S(2)}) copy-start(bf16[512,192]{1,0:T(8,128)(2,1)S(1)} %collective-permute-done.5.refs_9_) | copy-start | bytes 589828
  105.5 15.8 %collective-permute-start.12 = (bf16[12,384,384]{2,1,0:T(8,128)(2,1)}, bf16[12,384,384]{2,1,0:T(8,128)(2,1)}, u32[]{:S(2)}, u32[]{:S(2)}) collective-permute-start(bf16[12,384,384]{2,1,0:T(8,128)(2,1)} %collective-permute-done.9.refs_12_.refs_13_.refs_9_.refs_10_), channel_id=1, source_target_pairs={{1,5},{5,1},{2,6},{6,2},{9,13},{13,9},{10,14},{14,10},{17,21},{21,... | collective-permute-start | bytes 10616840 | tf_op jit(solution)/shard_map/ppermute | solution.py:944
  107.9 30.1 %collective-permute-start.13 = (bf16[12,384,384]{2,1,0:T(8,128)(2,1)S(1)}, bf16[12,384,384]{2,1,0:T(8,128)(2,1)}, u32[]{:S(2)}, u32[]{:S(2)}) collective-permute-start(bf16[12,384,384]{2,1,0:T(8,128)(2,1)S(1)} %bitcast_convert_fusion.refs_15_.refs_16_.refs_12_.refs_13_), channel_id=1, source_target_pairs={{1,5},{5,1},{2,6},{6,2},{9,13},{13,9},{10,14},{14,10},{17,21},{21,... | collective-permute-start | bytes 10616840 | tf_op jit(solution)/shard_map/ppermute | solution.py:944
  110.4 27.6 %collective-permute-start.11 = (bf16[12,384,384]{2,1,0:T(8,128)(2,1)}, bf16[12,384,384]{2,1,0:T(8,128)(2,1)}, u32[]{:S(2)}, u32[]{:S(2)}) collective-permute-start(bf16[12,384,384]{2,1,0:T(8,128)(2,1)} %collective-permute-done.8.refs_11_.refs_12_.refs_8_.refs_9_), channel_id=1, source_target_pairs={{1,5},{5,1},{2,6},{6,2},{9,13},{13,9},{10,14},{14,10},{17,21},{21,... | collective-permute-start | bytes 10616840 | tf_op jit(solution)/shard_map/ppermute | solution.py:944
  123.5 45.9 %collective-permute-start.17 = (bf16[1536,192]{0,1:T(8,128)(2,1)}, bf16[1536,192]{0,1:T(8,128)(2,1)}, u32[]{:S(2)}, u32[]{:S(2)}) collective-permute-start(bf16[1536,192]{0,1:T(8,128)(2,1)} %copy.67), channel_id=1, source_target_pairs={{3,1},{7,5},{11,9},{15,13},{19,17},{23,21},{27,25},{31,29}} | collective-permute-start | bytes 1769480 | tf_op jit(solution)/shard_map/ppermute | solution.py:932
  125.0 46.6 %collective-permute-start.16 = (bf16[1536,192]{0,1:T(8,128)(2,1)}, bf16[1536,192]{0,1:T(8,128)(2,1)}, u32[]{:S(2)}, u32[]{:S(2)}) collective-permute-start(bf16[1536,192]{0,1:T(8,128)(2,1)} %copy.67), channel_id=1, source_target_pairs={{2,1},{6,5},{10,9},{14,13},{18,17},{22,21},{26,25},{30,29}} | collective-permute-start | bytes 1769480 | tf_op jit(solution)/shard_map/ppermute | solution.py:932
  126.5 47.3 %collective-permute-start.15 = (bf16[1536,192]{0,1:T(8,128)(2,1)}, bf16[1536,192]{0,1:T(8,128)(2,1)}, u32[]{:S(2)}, u32[]{:S(2)}) collective-permute-start(bf16[1536,192]{0,1:T(8,128)(2,1)} %copy.67), channel_id=1, source_target_pairs={{0,1},{4,5},{8,9},{12,13},{16,17},{20,21},{24,25},{28,29}} | collective-permute-start | bytes 1769480 | tf_op jit(solution)/shard_map/ppermute | solution.py:932
  168.7 49.2 %collective-permute-start.14 = (bf16[512,768]{1,0:T(8,128)(2,1)}, bf16[512,768]{1,0:T(8,128)(2,1)S(1)}, u32[]{:S(2)}, u32[]{:S(2)}) collective-permute-start(bf16[512,768]{1,0:T(8,128)(2,1)} %get-tuple-element.148), channel_id=1, source_target_pairs={{1,2},{5,6},{9,10},{13,14},{17,18},{21,22},{25,26},{29,30}} | collective-permute-start | bytes 2359304 | tf_op jit(solution)/shard_map/ppermute | solution.py:979
  217.1 33.7 %collective-permute-start.18 = (bf16[512,768]{1,0:T(8,128)(2,1)}, bf16[512,768]{1,0:T(8,128)(2,1)S(1)}, u32[]{:S(2)}, u32[]{:S(2)}) collective-permute-start(bf16[512,768]{1,0:T(8,128)(2,1)} %get-tuple-element.157), channel_id=1, source_target_pairs={{1,2},{5,6},{9,10},{13,14},{17,18},{21,22},{25,26},{29,30}} | collective-permute-start | bytes 2359304 | tf_op jit(solution)/shard_map/ppermute | solution.py:979
  249.3 34.2 %collective-permute-start.19 = (bf16[512,768]{1,0:T(8,128)(2,1)}, bf16[512,768]{1,0:T(8,128)(2,1)S(1)}, u32[]{:S(2)}, u32[]{:S(2)}) collective-permute-start(bf16[512,768]{1,0:T(8,128)(2,1)} %get-tuple-element.162), channel_id=1, source_target_pairs={{1,2},{5,6},{9,10},{13,14},{17,18},{21,22},{25,26},{29,30}} | collective-permute-start | bytes 2359304 | tf_op jit(solution)/shard_map/ppermute | solution.py:979
  282.1 33.7 %collective-permute-start.20 = (bf16[512,768]{1,0:T(8,128)(2,1)}, bf16[512,768]{1,0:T(8,128)(2,1)S(1)}, u32[]{:S(2)}, u32[]{:S(2)}) collective-permute-start(bf16[512,768]{1,0:T(8,128)(2,1)} %get-tuple-element.167), channel_id=1, source_target_pairs={{1,2},{5,6},{9,10},{13,14},{17,18},{21,22},{25,26},{29,30}} | collective-permute-start | bytes 2359304 | tf_op jit(solution)/shard_map/ppermute | solution.py:979
  316.8 32.4 %copy-start.33 = (f32[768]{0:T(1024)S(1)}, f32[768]{0:T(1024)}, u32[]{:S(2)}) copy-start(f32[768]{0:T(1024)} %slice_reduce_fusion) | copy-start | bytes 9220
  316.8 32.6 %copy-start.37 = (f32[4,1]{1,0:T(4,128)S(1)}, f32[4,1]{1,0:T(4,128)}, u32[]{:S(2)}) copy-start(f32[4,1]{1,0:T(4,128)} %get-tuple-element.273) | copy-start | bytes 52
  316.8 32.6 %copy-start.38 = (f32[4,1]{1,0:T(4,128)S(1)}, f32[4,1]{1,0:T(4,128)}, u32[]{:S(2)}) copy-start(f32[4,1]{1,0:T(4,128)} %get-tuple-element.274) | copy-start | bytes 52
  378.1 27.9 %collective-permute-start.21 = (bf16[512,768]{1,0:T(8,128)(2,1)}, bf16[512,768]{1,0:T(8,128)(2,1)S(1)}, u32[]{:S(2)}, u32[]{:S(2)}) collective-permute-start(bf16[512,768]{1,0:T(8,128)(2,1)} %get-tuple-element.178), channel_id=1, source_target_pairs={{2,1},{6,5},{10,9},{14,13},{18,17},{22,21},{26,25},{30,29}} | collective-permute-start | bytes 2359304 | tf_op jit(solution)/shard_map/ppermute | solution.py:1038
  405.2 30.8 %collective-permute-start.22 = (bf16[512,768]{1,0:T(8,128)(2,1)}, bf16[512,768]{1,0:T(8,128)(2,1)S(1)}, u32[]{:S(2)}, u32[]{:S(2)}) collective-permute-start(bf16[512,768]{1,0:T(8,128)(2,1)} %get-tuple-element.181), channel_id=1, source_target_pairs={{2,1},{6,5},{10,9},{14,13},{18,17},{22,21},{26,25},{30,29}} | collective-permute-start | bytes 2359304 | tf_op jit(solution)/shard_map/ppermute | solution.py:1038
  435.3 30.6 %collective-permute-start.23 = (bf16[512,768]{1,0:T(8,128)(2,1)}, bf16[512,768]{1,0:T(8,128)(2,1)S(1)}, u32[]{:S(2)}, u32[]{:S(2)}) collective-permute-start(bf16[512,768]{1,0:T(8,128)(2,1)} %get-tuple-element.188), channel_id=1, source_target_pairs={{2,1},{6,5},{10,9},{14,13},{18,17},{22,21},{26,25},{30,29}} | collective-permute-start | bytes 2359304 | tf_op jit(solution)/shard_map/ppermute | solution.py:1038
  465.1 32.8 %collective-permute-start.24 = (bf16[512,768]{1,0:T(8,128)(2,1)}, bf16[512,768]{1,0:T(8,128)(2,1)S(1)}, u32[]{:S(2)}, u32[]{:S(2)}) collective-permute-start(bf16[512,768]{1,0:T(8,128)(2,1)} %get-tuple-element.195), channel_id=1, source_target_pairs={{2,1},{6,5},{10,9},{14,13},{18,17},{22,21},{26,25},{30,29}} | collective-permute-start | bytes 2359304 | tf_op jit(solution)/shard_map/ppermute | solution.py:1038
  495.1 31.9 %collective-permute-start.26 = (bf16[192,1536]{1,0:T(8,128)(2,1)}, bf16[192,1536]{1,0:T(8,128)(2,1)S(1)}, u32[]{:S(2)}, u32[]{:S(2)}) collective-permute-start(bf16[192,1536]{1,0:T(8,128)(2,1)} %get-tuple-element.198), channel_id=1, source_target_pairs={{1,2},{5,6},{9,10},{13,14},{17,18},{21,22},{25,26},{29,30}} | collective-permute-start | bytes 1769480 | tf_op jit(solution)/shard_map/ppermute | solution.py:1008
  495.8 31.2 %collective-permute-start.27 = (bf16[192,1536]{1,0:T(8,128)(2,1)}, bf16[192,1536]{1,0:T(8,128)(2,1)S(1)}, u32[]{:S(2)}, u32[]{:S(2)}) collective-permute-start(bf16[192,1536]{1,0:T(8,128)(2,1)} %get-tuple-element.200), channel_id=1, source_target_pairs={{1,0},{5,4},{9,8},{13,12},{17,16},{21,20},{25,24},{29,28}} | collective-permute-start | bytes 1769480 | tf_op jit(solution)/shard_map/ppermute | solution.py:1008
  497.1 29.9 %collective-permute-start.28 = (bf16[192,1536]{1,0:T(8,128)(2,1)}, bf16[192,1536]{1,0:T(8,128)(2,1)S(1)}, u32[]{:S(2)}, u32[]{:S(2)}) collective-permute-start(bf16[192,1536]{1,0:T(8,128)(2,1)} %get-tuple-element.201), channel_id=1, source_target_pairs={{1,3},{5,7},{9,11},{13,15},{17,19},{21,23},{25,27},{29,31}} | collective-permute-start | bytes 1769480 | tf_op jit(solution)/shard_map/ppermute | solution.py:1008
  498.7 28.3 %copy-start.4 = (bf16[192,1536]{1,0:T(8,128)(2,1)S(1)}, bf16[192,1536]{1,0:T(8,128)(2,1)}, u32[]{:S(2)}) copy-start(bf16[192,1536]{1,0:T(8,128)(2,1)} %get-tuple-element.199) | copy-start | bytes 1769476
  498.7 28.4 %copy-start = (s32[48]{0:T(128)S(1)}, s32[48]{0:T(128)}, u32[]{:S(2)}) copy-start(s32[48]{0:T(128)} %constant.248.clone) | copy-start | bytes 580
  545.2 48.4 %collective-permute-start.29 = (f32[12,384,384]{2,1,0:T(8,128)}, f32[12,384,384]{2,1,0:T(8,128)}, u32[]{:S(2)}, u32[]{:S(2)}) collective-permute-start(f32[12,384,384]{2,1,0:T(8,128)} %weight_products.4), channel_id=1, source_target_pairs={{0,4},{4,0},{1,5},{5,1},{2,6},{6,2},{3,7},{7,3},{8,12},{12,8},{9,1... | collective-permute-start | bytes 21233672 | tf_op jit(solution)/shard_map/ppermute | solution.py:847
  546.6 21.6 %copy-start.27 = (f32[1,9984]{1,0:T(1,128)S(1)}, f32[1,9984]{1,0:T(1,128)}, u32[]{:S(2)}) copy-start(f32[1,9984]{1,0:T(1,128)} %get-tuple-element.175) | copy-start | bytes 119812
  546.6 21.6 %copy-start.28 = (f32[1,9984]{1,0:T(1,128)S(1)}, f32[1,9984]{1,0:T(1,128)}, u32[]{:S(2)}) copy-start(f32[1,9984]{1,0:T(1,128)} %get-tuple-element.177) | copy-start | bytes 119812
  546.6 21.6 %copy-start.29 = (f32[1,9984]{1,0:T(1,128)S(1)}, f32[1,9984]{1,0:T(1,128)}, u32[]{:S(2)}) copy-start(f32[1,9984]{1,0:T(1,128)} %get-tuple-element.180) | copy-start | bytes 119812
  546.6 21.6 %copy-start.30 = (f32[1,9984]{1,0:T(1,128)S(1)}, f32[1,9984]{1,0:T(1,128)}, u32[]{:S(2)}) copy-start(f32[1,9984]{1,0:T(1,128)} %get-tuple-element.187) | copy-start | bytes 119812
  546.7 21.9 %copy-start.39 = (f32[2]{0:T(128)S(1)}, f32[2]{0:T(128)}, u32[]{:S(2)}) copy-start(f32[2]{0:T(128)} %get-tuple-element.304) | copy-start | bytes 28
  546.7 21.9 %copy-start.40 = (f32[2]{0:T(128)S(1)}, f32[2]{0:T(128)}, u32[]{:S(2)}) copy-start(f32[2]{0:T(128)} %get-tuple-element.305) | copy-start | bytes 28
  546.7 21.9 %copy-start.41 = (f32[2]{0:T(128)S(1)}, f32[2]{0:T(128)}, u32[]{:S(2)}) copy-start(f32[2]{0:T(128)} %get-tuple-element.306) | copy-start | bytes 28
  546.7 21.9 %copy-start.42 = (f32[2]{0:T(128)S(1)}, f32[2]{0:T(128)}, u32[]{:S(2)}) copy-start(f32[2]{0:T(128)} %get-tuple-element.307) | copy-start | bytes 28
  546.7 23.2 %copy-start.48 = (bf16[192,512]{1,0:T(8,128)(2,1)S(1)}, bf16[192,512]{1,0:T(8,128)(2,1)}, u32[]{:S(2)}) copy-start(bf16[192,512]{1,0:T(8,128)(2,1)} %get-tuple-element.213) | copy-start | bytes 589828
  546.7 23.9 %copy-start.47 = (bf16[192,512]{1,0:T(8,128)(2,1)S(1)}, bf16[192,512]{1,0:T(8,128)(2,1)}, u32[]{:S(2)}) copy-start(bf16[192,512]{1,0:T(8,128)(2,1)} %get-tuple-element.215) | copy-start | bytes 589828
  546.7 28.6 %copy-start.46 = (bf16[192,512]{1,0:T(8,128)(2,1)S(1)}, bf16[192,512]{1,0:T(8,128)(2,1)}, u32[]{:S(2)}) copy-start(bf16[192,512]{1,0:T(8,128)(2,1)} %get-tuple-element.216) | copy-start | bytes 589828
  546.7 43.8 %copy-start.19 = (bf16[192,512]{1,0:T(8,128)(2,1)S(1)}, bf16[192,512]{1,0:T(8,128)(2,1)}, u32[]{:S(2)}) copy-start(bf16[192,512]{1,0:T(8,128)(2,1)} %get-tuple-element.214) | copy-start | bytes 589828
  562.9 55.4 %collective-permute-start.30 = (f32[12,384,384]{2,1,0:T(8,128)}, f32[12,384,384]{2,1,0:T(8,128)}, u32[]{:S(2)}, u32[]{:S(2)}) collective-permute-start(f32[12,384,384]{2,1,0:T(8,128)} %weight_products.6), channel_id=1, source_target_pairs={{0,4},{4,0},{1,5},{5,1},{2,6},{6,2},{3,7},{7,3},{8,12},{12,8},{9,1... | collective-permute-start | bytes 21233672 | tf_op jit(solution)/shard_map/ppermute | solution.py:847
  568.5 6.8 collective-permute-start.25
  569.9 8.3 %collective-permute-start.32 = (bf16[192,512]{1,0:T(8,128)(2,1)S(1)}, bf16[192,512]{1,0:T(8,128)(2,1)S(1)}, u32[]{:S(2)}, u32[]{:S(2)}) collective-permute-start(bf16[192,512]{1,0:T(8,128)(2,1)S(1)} %copy-done.48), channel_id=1, source_target_pairs={{1,2},{5,6},{9,10},{13,14},{17,18},{21,22},{25,26},{29,30}} | collective-permute-start | bytes 589832 | tf_op jit(solution)/shard_map/ppermute | solution.py:1008
  570.6 19.9 %collective-permute-start.33 = (bf16[192,512]{1,0:T(8,128)(2,1)S(1)}, bf16[192,512]{1,0:T(8,128)(2,1)S(1)}, u32[]{:S(2)}, u32[]{:S(2)}) collective-permute-start(bf16[192,512]{1,0:T(8,128)(2,1)S(1)} %copy-done.47), channel_id=1, source_target_pairs={{1,0},{5,4},{9,8},{13,12},{17,16},{21,20},{25,24},{29,28}} | collective-permute-start | bytes 589832 | tf_op jit(solution)/shard_map/ppermute | solution.py:1008
  575.3 15.2 %collective-permute-start.34 = (bf16[192,512]{1,0:T(8,128)(2,1)S(1)}, bf16[192,512]{1,0:T(8,128)(2,1)S(1)}, u32[]{:S(2)}, u32[]{:S(2)}) collective-permute-start(bf16[192,512]{1,0:T(8,128)(2,1)S(1)} %copy-done.46), channel_id=1, source_target_pairs={{1,3},{5,7},{9,11},{13,15},{17,19},{21,23},{25,27},{29,31}} | collective-permute-start | bytes 589832 | tf_op jit(solution)/shard_map/ppermute | solution.py:1008
  593.6 55.3 %collective-permute-start.31 = (bf16[96,1536]{1,0:T(8,128)(2,1)S(1)}, bf16[96,1536]{1,0:T(8,128)(2,1)S(1)}, u32[]{:S(2)}, u32[]{:S(2)}) collective-permute-start(bf16[96,1536]{1,0:T(8,128)(2,1)S(1)} %get-tuple-element.265), channel_id=1, source_target_pairs={{0,4},{4,0},{1,5},{5,1},{2,6},{6,2},{3,7},{7,3},{8,12},{12,8},{9,1... | collective-permute-start | bytes 884744 | tf_op jit(solution)/shard_map/ppermute | solution.py:847
  638.5 143.9 %collective-permute-start.36 = (bf16[2320,384]{1,0:T(8,128)(2,1)}, bf16[2320,384]{1,0:T(8,128)(2,1)S(1)}, u32[]{:S(2)}, u32[]{:S(2)}) collective-permute-start(bf16[2320,384]{1,0:T(8,128)(2,1)} %pad_maximum_fusion.1), channel_id=1, source_target_pairs={{1,3},{2,0},{5,7},{6,4},{9,11},{10,8},{13,15},{14,12},{17,19},{18,... | collective-permute-start | bytes 5345288 | tf_op jit(solution)/shard_map/ppermute | solution.py:1100
  639.8 142.6 %collective-permute-start.37 = (bf16[2320,384]{1,0:T(8,128)(2,1)}, bf16[2320,384]{1,0:T(8,128)(2,1)}, u32[]{:S(2)}, u32[]{:S(2)}) collective-permute-start(bf16[2320,384]{1,0:T(8,128)(2,1)} %pad_maximum_fusion.2), channel_id=1, source_target_pairs={{1,2},{2,1},{5,6},{6,5},{9,10},{10,9},{13,14},{14,13},{17,18},{18,... | collective-permute-start | bytes 5345288 | tf_op jit(solution)/shard_map/ppermute | solution.py:1100
  646.2 2.7 collective-permute-start.35
  647.6 134.8 %collective-permute-start.38 = (bf16[2320,384]{1,0:T(8,128)(2,1)}, bf16[2320,384]{1,0:T(8,128)(2,1)}, u32[]{:S(2)}, u32[]{:S(2)}) collective-permute-start(bf16[2320,384]{1,0:T(8,128)(2,1)} %pad_maximum_fusion.4), channel_id=1, source_target_pairs={{1,0},{2,3},{5,4},{6,7},{9,8},{10,11},{13,12},{14,15},{17,16},{18,... | collective-permute-start | bytes 5345288 | tf_op jit(solution)/shard_map/ppermute | solution.py:1100
  788.9 7.9 collective-permute-start.39
  (25 other events, 209.7 us)

commit v3 on v2

--- a/solution.py
+++ b/solution.py
@@ -160,7 +160,15 @@
                 copy.wait()
 
 
-def forward_kernel(tick, unit, part_count, shard_count, first, handed, *refs):
+def forward_kernel(tick, units, *rest):
+    meta_ref = rest[5]
+
+    @pl.when(meta_ref[1 + tick] < units)
+    def _():
+        forward_body(tick, *rest)
+
+
+def forward_body(tick, unit, part_count, shard_count, first, handed, *refs):
     meta_ref, order_ref, vec_ref, fin_ref, cos_ref, sa_ref, sb_ref = refs[:7]
     if handed:
         recv_ref, *refs = refs[7:]
@@ -175,11 +183,11 @@
     length = xb_ref.shape[0]
     slot = meta_ref[1 + tick]
     weights = Weights(meta_ref[0], shards, mats, wsem)
-    width = looked.shape[2]
+    width = looked.shape[1]
 
     def assemble():
         copies = [
-            pltpu.make_async_copy(part.at[pl.ds(unit * length, length)], looked.at[k], isem.at[k])
+            pltpu.make_async_copy(part.at[:, pl.ds(unit * length, length)], looked.at[k], isem.at[k])
             for k, part in enumerate(parts)
         ]
         for copy in copies:
@@ -188,7 +196,7 @@
             copy.wait()
         found = jnp.zeros((length, D), f32)
         for k in range(part_count):
-            found = found + nn(looked[k], order_ref[k * width : (k + 1) * width, :])
+            found = found + tn(looked[k], order_ref[k * width : (k + 1) * width, :])
         kept[:, COL_X : COL_X + D] = found.astype(bf16)
 
     weights.start(0)
@@ -319,7 +327,7 @@
     before = len(operands)
     operands = operands + [*shards] + ([] if first else list(state))
     return pl.pallas_call(
-        functools.partial(forward_kernel, tick, unit, len(parts), count, first, handed),
+        functools.partial(forward_kernel, tick, slots, unit, len(parts), count, first, handed),
         out_shape=(
             jax.ShapeDtypeStruct((length, D), bf16),
             jax.ShapeDtypeStruct((8, D), f32),
@@ -338,7 +346,7 @@
             pltpu.VMEM((length, KEPT), bf16),
             pltpu.VMEM((length, D), f32),
             pltpu.VMEM((LSE_ROWS, length), f32),
-            pltpu.VMEM((len(parts), length, parts[0].shape[1]), bf16),
+            pltpu.VMEM((len(parts), parts[0].shape[0], length), bf16),
             pltpu.SemaphoreType.DMA((len(PLACES),)),
             pltpu.SemaphoreType.DMA((len(parts),)),
             pltpu.SemaphoreType.DMA((5 + 2 * (FF // CHUNK),)),
@@ -349,7 +357,15 @@
     )(*operands)
 
 
-def backward_kernel(tick, units, shard_count, handed, back_in, back_out, *refs):
+def backward_kernel(tick, units, *rest):
+    meta_ref = rest[4]
+
+    @pl.when(meta_ref[1 + units + 2 + tick] < units)
+    def _():
+        backward_body(tick, units, *rest)
+
+
+def backward_body(tick, units, shard_count, handed, back_in, back_out, *refs):
     meta_ref, flag_ref, order_ref, vec_ref, fin_ref, cos_ref, sa_ref, sb_ref = refs[:8]
     if handed:
         recv_ref, *refs = refs[8:]
@@ -563,54 +579,104 @@
     )(*operands)
 
 
-def product_kernel(left_at, right_at, count_ref, x_ref, y_ref, *refs):
-    sent_ref = refs[0] if len(refs) == 4 else None
-    out_ref, square_ref, turned = refs[-3:] if sent_ref is not None else (refs[0], None, refs[1])
+def product_kernel(shards, start, tiles, x_ref, y_ref, *refs):
+    sent_ref = refs[0] if len(refs) > 2 else None
+    turned = refs[-1]
     units, rows, width = x_ref.shape
     step = pl.program_id(0)
-    before = left_at[jnp.maximum(step - 1, 0)]
-
-    @pl.when(jnp.logical_or(step == 0, left_at[step] != before))
+    steps = pl.num_programs(0)
+    before = tiles[start + jnp.maximum(step - 1, 0)]
+
+    @pl.when(jnp.logical_or(step == 0, tiles[start + step] != before))
     def _():
         for unit in range(units):
             turned[:, unit * rows : (unit + 1) * rows] = jnp.transpose(x_ref[unit])
 
     found = nn(turned[...], y_ref[...].reshape(units * rows, -1))
     if sent_ref is None:
+        out_ref = refs[0]
         for i in range(out_ref.shape[0]):
-            out_ref[i] = found[:, i * TILE : (i + 1) * TILE]
+            out_ref[i] = found[:, i * TILE : (i + 1) * TILE].astype(bf16)
         return
+    square_ref, *out_refs = refs[1:-1]
 
     @pl.when(step == 0)
     def _():
         square_ref[...] = jnp.zeros_like(square_ref)
 
-    for i in range(out_ref.shape[0]):
-        whole = found[:, i * TILE : (i + 1) * TILE] + sent_ref[i]
-        out_ref[i] = whole.astype(bf16)
-        weight = count_ref[step * out_ref.shape[0] + i].astype(f32)
+    each = sent_ref.shape[0]
+    blocks = []
+    for i in range(each):
+        whole = found[:, i * TILE : (i + 1) * TILE] + sent_ref[i].astype(f32)
+        blocks.append(whole.astype(bf16))
+        weight = tiles[start + 2 * steps + step * each + i].astype(f32)
         square_ref[...] += weight * jnp.sum(whole * whole, axis=0, keepdims=True)
-
-
-def products(left_at, right_at, counted, kept, units, each, sent=None):
-    steps = left_at.shape[0]
+    per = steps // shards
+    for shard, out_ref in enumerate(out_refs):
+
+        @pl.when(step // per == shard)
+        def _(out_ref=out_ref):
+            for i in range(each):
+                out_ref[i] = blocks[i]
+
+
+def product_tiles(count, each):
+    total = len(PLACES) // count
+    part = (total + 1) // 2
+    rest = total - part
+    group = max(count // 2, 1)
+    left = [(0, 2, 4, 6)[m] + row for m, row, _ in PLACES]
+    right = [((14, 28, 20, 28)[m] + col) // each for m, _, col in PLACES]
+    found = []
+    for is_high in range(2):
+        for core in range(2):
+            row = []
+            for start in range(0, count, group):
+                shards = [shard_order(count, is_high)[step] for step in range(start, start + group)]
+                for half in (1 - core, core):
+                    places = [k * total + half * rest + i for k in shards for i in range(part)]
+                    row += [left[b] for b in places[::each]] + [right[b] for b in places[::each]]
+                    row += [0 if half == 1 and i < part - rest else 1 for _ in shards for i in range(part)]
+            found.append(row)
+    return found
+
+
+def shard_order(count, is_high):
+    low = count // 2 - 1
+    order = list(range(count - 1, low, -1)) + list(range(low + 1))
+    return [count - 1 - k for k in order] if is_high else order
+
+
+def products(shards, tiles, call, kept, units, each, sent=None):
+    part = (len(PLACES) // (2 * shards) + 1) // 2
+    steps = shards * part // each
+    start = call * (2 * steps + shards * part)
+    per = steps // shards
     length = kept.shape[1]
-    block = pl.BlockSpec((each, TILE, TILE), lambda i, a, b, c: (i, 0, 0))
-    shape = (steps * each, TILE, TILE)
+    block = pl.BlockSpec((each, TILE, TILE), lambda i, t: (i, 0, 0))
     if sent is None:
-        out_shape, out_specs, more = jax.ShapeDtypeStruct(shape, f32), block, []
+        out_shape, out_specs, more = jax.ShapeDtypeStruct((steps * each, TILE, TILE), bf16), block, []
     else:
-        out_shape = (jax.ShapeDtypeStruct(shape, bf16), jax.ShapeDtypeStruct((1, TILE), f32))
-        out_specs, more = (block, pl.BlockSpec((1, TILE), lambda i, a, b, c: (0, 0))), [sent]
+        out_shape = (jax.ShapeDtypeStruct((1, TILE), f32),)
+        out_shape += (jax.ShapeDtypeStruct((per * each, TILE, TILE), bf16),) * shards
+        out_specs = (pl.BlockSpec((1, TILE), lambda i, t: (0, 0)),)
+        for shard in range(shards):
+            out_specs += (
+                pl.BlockSpec(
+                    (each, TILE, TILE),
+                    lambda i, t, first=shard * per: (jnp.clip(i - first, 0, per - 1), 0, 0),
+                ),
+            )
+        more = [sent]
     return pl.pallas_call(
-        product_kernel,
+        functools.partial(product_kernel, shards, start),
         out_shape=out_shape,
         grid_spec=pltpu.PrefetchScalarGridSpec(
-            num_scalar_prefetch=3,
+            num_scalar_prefetch=1,
             grid=(steps,),
             in_specs=[
-                pl.BlockSpec((units, length, TILE), lambda i, a, b, c: (0, 0, a[i])),
-                pl.BlockSpec((units, length, each * TILE), lambda i, a, b, c: (0, 0, b[i])),
+                pl.BlockSpec((units, length, TILE), lambda i, t: (0, 0, t[start + i])),
+                pl.BlockSpec((units, length, each * TILE), lambda i, t: (0, 0, t[start + steps + i])),
             ]
             + [block] * len(more),
             out_specs=out_specs,
@@ -619,7 +685,7 @@
         compiler_params=pltpu.CompilerParams(vmem_limit_bytes=VMEM_LIMIT),
         cost_estimate=LIGHT,
         name="weight_products",
-    )(left_at, right_at, counted, kept, kept, *more)
+    )(tiles, kept, kept, *more)
 
 
 def lookup_kernel(ids_ref, embedding_ref, first_ref, rest_ref, table, wide):
@@ -650,9 +716,16 @@
             return carry
 
         lax.fori_loop(0, tokens // 16, fetch, 0)
-        first = first_ref.shape[0]
-        first_ref[...] = wide[:first, :features].astype(bf16)
-        rest_ref[...] = wide[first:, :features].astype(bf16)
+        start = 0
+        for ref in (first_ref, rest_ref):
+
+            def flat(i, carry, ref=ref, start=start):
+                rows = wide[pl.ds(pl.multiple_of(start + i * lanes, lanes), lanes), :]
+                ref[:, pl.ds(pl.multiple_of(i * lanes, lanes), lanes)] = jnp.transpose(rows)[:features].astype(bf16)
+                return carry
+
+            lax.fori_loop(0, ref.shape[1] // lanes, flat, 0)
+            start += ref.shape[1]
 
 
 def lookup(ids, embedding, first):
@@ -664,8 +737,8 @@
     return pl.pallas_call(
         lookup_kernel,
         out_shape=(
-            jax.ShapeDtypeStruct((first, features), bf16),
-            jax.ShapeDtypeStruct((tokens - first, features), bf16),
+            jax.ShapeDtypeStruct((features, first), bf16),
+            jax.ShapeDtypeStruct((features, tokens - first), bf16),
         ),
         grid=(steps,),
         in_specs=[
@@ -673,8 +746,8 @@
             pl.BlockSpec((features, vocab // steps), lambda i: (0, i)),
         ],
         out_specs=(
-            pl.BlockSpec((first, features), whole),
-            pl.BlockSpec((tokens - first, features), whole),
+            pl.BlockSpec((features, first), whole),
+            pl.BlockSpec((features, tokens - first), whole),
         ),
         scratch_shapes=[pltpu.VMEM((vocab, lanes), f32), pltpu.VMEM((tokens, lanes), f32)],
         compiler_params=pltpu.CompilerParams(vmem_limit_bytes=VMEM_LIMIT),
@@ -872,8 +945,7 @@
     place = lax.axis_index("dp")
     low, high = count // 2 - 1, count // 2
     is_high = place >= high
-    order_low = list(range(count - 1, low, -1)) + list(range(low + 1))
-    order_high = [count - 1 - k for k in order_low]
+    order_low, order_high = shard_order(count, False), shard_order(count, True)
     length = tokens.shape[2]
     units = tokens.shape[0] * count
     own_blocks = layer_blocks.shape[1]
@@ -924,21 +996,28 @@
         jnp.concatenate([ids_here[:, :1].reshape(-1), ids_here[:, 1:].reshape(-1)]), embedding, 2 * length
     )
 
-    def joined(rows):
-        half = rows.shape[0] // 2
-        return ordered(section, rows[:half], swapped(rows[half:]), 1)
-
-    def sent_on(rows):
-        return [rows if k == low else lax.ppermute(rows, "dp", [(k, low)]) for k in range(count)]
-
-    looked = [joined(rows) for rows in looked]
+    def joined(columns):
+        half = columns.shape[1] // 2
+        return ordered(section, columns[:, :half], swapped(columns[:, half:]), 0)
+
+    def sent_on(columns):
+        return [columns if k == low else lax.ppermute(columns, "dp", [(k, low)]) for k in range(count)]
+
+    looked = [joined(columns) for columns in looked]
     first = sent_on(looked[0])
     slot_at = jnp.arange(D)
     chip, within = slot_at // (2 * features), slot_at % (2 * features)
     feature_at = within // features * (D // 2) + chip * features + within % features
     order = (feature_at[:, None] == jnp.arange(D)[None, :]).astype(bf16)
-    first, later, received, vec, fin, tables, order = lax.optimization_barrier(
-        (first, looked[1], received, vec, fin, tables, order)
+    part = (own_blocks + 1) // 2
+    each = 2 if own_blocks % 4 == 0 else 1
+    group = max(count // 2, 1)
+    tiles = lax.dynamic_index_in_dim(
+        jnp.array(product_tiles(count, each), jnp.int32), is_high * 2 + section, 0, False
+    )
+
+    first, later, received, vec, fin, tables, order, tiles = lax.optimization_barrier(
+        (first, looked[1], received, vec, fin, tables, order, tiles)
     )
     relays = [
         lax.ppermute(
@@ -951,11 +1030,11 @@
     shards = [*received, *relays[1:], own, relays[0]]
     role = is_high * 2 + ((section == 1) == is_high) * 1
 
-    slots = units + 1
+    live_low, live_high = place == low, place == high
     early = [*range(units), units, units]
     late = [units, units, *range(units)]
-    meta = jnp.where(is_high, jnp.array([0, *late, *early]), jnp.array([0, *early, *late])).at[0].set(role)
-    meta = meta.astype(jnp.int32)
+    meta = jnp.where(live_high, jnp.array([0, *late, *early]), jnp.array([0, *early, *late]))
+    meta = jnp.where(live_low | live_high, meta, units).at[0].set(role).astype(jnp.int32)
     state = None
     arrived = []
     sums = []
@@ -973,7 +1052,7 @@
             tables,
             shards,
             state,
-            slots,
+            units,
         )
         if tick < units:
             arrived.append(lax.ppermute(result, "dp", [(low, high)]))
@@ -1003,12 +1082,10 @@
     )
 
     def returned(parts):
-        return chosen(
-            [place == k for k in range(count)],
-            [part if k == low else lax.ppermute(part, "dp", [(low, k)]) for k, part in enumerate(parts)],
-        )
-
-    def own_features(both_cores):
+        return [part if k == low else lax.ppermute(part, "dp", [(low, k)]) for k, part in enumerate(parts)]
+
+    def own_features(parts):
+        both_cores = chosen([place == k for k in range(count)], parts)
         mine, other = both_cores[:features], both_cores[features:]
         return [jnp.where(section == 0, mine, other), swapped(jnp.where(section == 0, other, mine))]
 
@@ -1036,103 +1113,72 @@
         )
         if tick < units:
             arrived.append(lax.ppermute(grad_in, "dp", [(high, low)]))
-        live = jnp.where(is_high, tick < units, tick >= 2)
-        vector_sum = vector_sum + jnp.where(live, vector_part, 0.0)
+        vector_sum = vector_sum + jnp.where(meta[1 + units + 2 + tick] < units, vector_part, 0.0)
     token_grads.append(returned(backs))
 
-    vector_pack = jnp.concatenate([vector_sum[0], jnp.where(place == high, final_local, 0.0)])
+    vector_pack = jnp.concatenate([vector_sum[0], jnp.where(live_high, final_local, 0.0)])
     vector_pack = vector_pack + swapped(vector_pack)
-    own_rows = own_vector + own_final
-    extra = -(-2 * own_rows // (16 * TILE)) * 16
-
-    def vector_rows(k):
-        values = jnp.concatenate(
-            [
-                lax.dynamic_slice_in_dim(vector_pack, k * own_vector, own_vector, 0),
-                lax.dynamic_slice_in_dim(vector_pack, V_END + (section * count + k) * own_final, own_final, 0),
-            ]
-        )
-        top = rounded(values)
-        halves = jnp.concatenate([top.astype(bf16), (values - top).astype(bf16)])
-        return jnp.pad(halves, (0, extra * TILE - 2 * own_rows)).reshape(extra, TILE)
-
-    left_at = jnp.array([(0, 2, 4, 6)[m] + row for m, row, _ in PLACES], jnp.int32)
-    right_at = jnp.array([(14, 28, 20, 28)[m] + col for m, _, col in PLACES], jnp.int32)
-    part = (own_blocks + 1) // 2
-    rest = own_blocks - part
-    kept = state[0]
-    each = 2 if own_blocks % 4 == 0 else 1
-
-    def tiles_of(shards, half):
-        places = jnp.concatenate([shard * own_blocks + half * rest + jnp.arange(0, part, each) for shard in shards])
-        return left_at[places], right_at[places] // each
-
-    live = (place == low) | (place == high)
-    token_grads[0], left_at = lax.optimization_barrier((token_grads[0], left_at))
-    squares = jnp.where(live & (section == 0), jnp.sum(vector_pack * vector_pack), 0.0)
-    counted = jnp.where((jnp.arange(part) < part - rest) & (section == 1), 0, 1).astype(jnp.int32)
-    group = max(count // 2, 1)
-    counted = jnp.concatenate([counted] * group)
-    sent, keeping, groups = [], [], []
-    for start in range(0, count, group):
-        steps = range(start, start + group)
-        groups.append([jnp.where(is_high, order_high[step], order_low[step]) for step in steps])
-        keeping.append(tiles_of(groups[-1], section))
-        sums = products(*tiles_of(groups[-1], 1 - section), counted, kept, units, each)
-        left_at, sums = lax.optimization_barrier((left_at, sums))
-        sent.append(swapped(sums))
-    pieces = []
-    for start, shards_here, tiles, others in zip(range(0, count, group), groups, keeping, sent):
-        if pieces:
-            tiles, pieces = lax.optimization_barrier((tiles, pieces))
-        total, block_squares = products(*tiles, counted, kept, units, each, others)
-        squares = squares + jnp.where(live, jnp.sum(block_squares), 0.0)
-        total = total.reshape(group, part * TILE, TILE)
-        pieces += [
-            jnp.concatenate([total[i], vector_rows(shard)], axis=0) for i, shard in enumerate(shards_here)
-        ]
-    for step in range(count - 1):
+
+    def to_owner(value, step):
         route = [
             (core * count + source, core * count + target)
             for core in range(2)
             for source, target in ((low, order_low[step]), (high, order_high[step]))
         ]
-        pieces[step] = lax.ppermute(pieces[step], both, route)
-    token_grads[1], pieces[-1] = lax.optimization_barrier((token_grads[1], pieces[-1]))
+        return lax.ppermute(value, both, route) if step < count - 1 else value
+
+    live = live_low | live_high
+    token_grads[0], tiles = lax.optimization_barrier((token_grads[0], tiles))
+    kept = state[0]
+    squares = jnp.where(live & (section == 0), jnp.sum(vector_pack * vector_pack), 0.0)
     ids_ordered = jnp.concatenate(
         [ids_here[0, :-1], ids_here[1, :-1], ids_here[0, -1:], ids_here[1, -1:]], axis=0
     ).reshape(-1)
+    sent, pieces = [], []
+    for index in range(count // group):
+        sums = products(group, tiles, 2 * index, kept, units, each)
+        if index == 0:
+            token_grads[1], sums = lax.optimization_barrier((token_grads[1], sums))
+        block_squares, *found = products(group, tiles, 2 * index + 1, kept, units, each, swapped(sums))
+        squares = squares + jnp.where(live, jnp.sum(block_squares), 0.0)
+        if index + 1 < count // group:
+            tiles, found = lax.optimization_barrier((tiles, found))
+            found = [to_owner(piece, index * group + i) for i, piece in enumerate(found)]
+        pieces += found
+    vectors = [to_owner(vector_pack, step) for step in range(count)]
+    token_grads, pieces[-1] = lax.optimization_barrier((token_grads, pieces[-1]))
     table_grad, table_squares = table_gradient(
         ids_ordered, own_features(token_grads[0]) + own_features(token_grads[1]), vocab
     )
 
+    squares = squares + jnp.sum(table_squares)
+    squares, pieces[: count - group] = lax.optimization_barrier((squares, pieces[: count - group]))
     loss = jnp.where(place == high, jnp.sum(pair_loss), 0.0)
-    square_total, loss_total = lax.psum((squares + jnp.sum(table_squares), loss), both)
+    square_total, loss_total = lax.psum((squares, loss), both)
     norm_value = jnp.sqrt(square_total)
     factor = clip_limit / jnp.maximum(norm_value, clip_limit)
+    pieces[count - group :], factor = lax.optimization_barrier((pieces[count - group :], factor))
+    pieces[count - group :] = [to_owner(pieces[step], step) for step in range(count - group, count)]
     embed_m, embed_v, embed_w = adam_step(
         embedding, embed_moment, embed_second, table_grad * factor, embed_rate, embed_decay
     )
     pieces, embed_w = lax.optimization_barrier((pieces, embed_w))
-    piece_low = chosen([place == k for k in order_low], pieces)
-    piece_high = chosen([place == k for k in order_high], pieces)
+    from_low = [place == k for k in order_low]
+    from_high = [place == k for k in order_high]
+    piece_low, piece_high = chosen(from_low, pieces), chosen(from_high, pieces)
     mine = jnp.where(section == 0, piece_low, piece_high)
-    other = swapped(jnp.where(section == 0, piece_high, piece_low)[: part * TILE])
-    block_part, other = (value.reshape(part, TILE, TILE) for value in (mine[: part * TILE], other))
+    other = swapped(jnp.where(section == 0, piece_high, piece_low))
     grad_blocks = jnp.concatenate(
-        [
-            jnp.where(section == 0, block_part, other),
-            jnp.where(section == 0, other, block_part)[2 * part - own_blocks :],
-        ],
+        [jnp.where(section == 0, mine, other), jnp.where(section == 0, other, mine)[2 * part - own_blocks :]],
         axis=0,
     )
-
-    def vectors_of(piece, start, width):
-        rows = piece[part * TILE :].reshape(-1)
-        return rows[start : start + width].astype(f32) + rows[own_rows + start : own_rows + start + width].astype(f32)
-
-    owned_vector = vectors_of(mine, 0, own_vector)[None]
-    owned_final = vectors_of(piece_high, own_vector, own_final)
+    vectors_high = chosen(from_high, vectors)
+    owned_vector = lax.dynamic_slice_in_dim(
+        jnp.where(section == 0, chosen(from_low, vectors), vectors_high), place * own_vector, own_vector, 0
+    )[None]
+    owned_final = lax.dynamic_slice_in_dim(
+        vectors_high, V_END + (section * count + place) * own_final, own_final, 0
+    )
 
     block_grad, new_blocks, new_left, new_right = (
         out[None]

time: 837 us -> 762 us (0.910)
  Pallas kernels: 509 us -> 244 us
  waiting for transfers between devices: 47.4 us -> 272 us
  local copies, waits for them, and re-layouts: 58.7 us -> 36.2 us
  blocking collectives: 48.2 us -> 38.7 us
    ppermute x6, waiting for transfers between devices: 12.3 us -> 225 us  [returned(): lax.ppermute(part, 'dp', [(low, k)])]
    pallas_call x11, Pallas kernels: 281 us -> 144 us  [the longest x4 67 us: products(): pl.pallas_call(functools.partial(product_kernel, shards, start), out_shap...]
    pallas_call x6, Pallas kernels: 166 us -> 38 us  [backward(): pl.pallas_call(functools.partial(backward_kernel, tick, units, count, han...]
    psum x1, blocking collectives: 48.2 us -> 38.7 us  [local(): square_total, loss_total = lax.psum((squares, loss), both)]
    gather x8 -> x0, local copies, waits for them, and re-layouts: 8.69 us -> none  [tiles_of(): return (left_at[places], right_at[places] // each)]
    ppermute x9 -> x12, waiting for transfers between devices: 31.5 us -> 39.6 us  [the longest x6 31 us: sent_on(): lax.ppermute(columns, 'dp', [(k, low)])]
    ppermute x9 -> x12, starting transfers between devices: 21.7 us -> 24 us  [the longest x6 16.1 us: sent_on(): lax.ppermute(columns, 'dp', [(k, low)])]
  transfers between devices with their start and end apart: 40 -> 43, of which waited for: 3 -> 7; matrix products, arithmetic and copies ran while one was open for 16% -> 13% of each run, Pallas kernels for 49% -> 22%
where the time goes in v3:
time: 762 us; the launch traced here: 753 us
  waiting for transfers between devices  272 us (36%)
  Pallas kernels  244 us (32%)
  other arithmetic  90.3 us (12%)
  starting transfers between devices  60.3 us (8%)
  blocking collectives  38.7 us (5%)
  local copies, waits for them, and re-layouts  36.2 us (5%)
  between operations  12.9 us (2%)
    ppermute x6, waiting for transfers between devices, returned(): lax.ppermute(part, 'dp', [(low, k)])  225 us
    pallas_call x4, Pallas kernels, products(): pl.pallas_call(functools.partial(product_kernel, shards, start), out_shap...  67 us
    pallas_call x6, Pallas kernels, forward(): pl.pallas_call(functools.partial(forward_kernel, tick, slots, unit, len(p...  56.1 us
    sub x3, other arithmetic, adam_step(): weight - rate * (corrected / scaled + decay * weight)  48.3 us
    psum x1, blocking collectives, local(): square_total, loss_total = lax.psum((squares, loss), both)  38.7 us
    pallas_call x6, Pallas kernels, backward(): pl.pallas_call(functools.partial(backward_kernel, tick, units, count, han...  38 us
    pallas_call x1, Pallas kernels, table_gradient(): pl.pallas_call(table_kernel, out_shape=(jax.ShapeDtypeStruct((features, v...  35 us
    ppermute x6, waiting for transfers between devices, sent_on(): lax.ppermute(columns, 'dp', [(k, low)])  31 us
  transfers between devices with their start and end apart: 43, of which 7 were waited for; matrix products, arithmetic and copies ran while one was open for 13% of the time, Pallas kernels for 22%

profile of v3, /device:TPU:0, one launch (start us, length us, event | category | flops | bytes accessed | tf_op | source)
XLA Modules:
  0.0 753.4 jit_solution(11562047260780082728)
XLA Ops:
  4.1 5.1 collective-permute-start.2
  11.3 3.5 bitcast_convert_fusion.rest_15_.rest_16_.rest_12_.rest_13_
  18.6 1.4 pad_maximum_fusion.3
  20.0 6.2 collective-permute-start.9
  26.2 2.4 collective-permute-start.8
  28.6 1.3 fusion.39.tiles
  30.6 2.6 fusion.4
  34.5 2.0 gather_fusion
  36.5 1.3 slice_convert_fusion
  39.2 1.5 slice.162
  41.3 1.3 pad_add_fusion.ids_ref
  42.6 21.3 %table_lookup.1 = (bf16[96,1024]{1,0:T(8,128)(2,1)}, bf16[96,3072]{1,0:T(8,128)(2,1)}) custom-call(s32[4096]{0:T(1024)} %pad_add_fusion.ids_ref, f32[96,50304]{1,0:T(8,128)} %embedding_ref.1), custom_call_target="tpu_custom_call" | custom-call | flops 1 | bytes 1 | tf_op jit(solution)/shard_map/table_lookup/pallas_call | solution.py:737
  64.0 1.5 slice.125
  66.0 1.7 slice.127
  69.0 1.5 reshape.231.rest_2_.rest_3_
  75.0 1.5 collective-permute-start.4
  78.6 26.0 %collective-permute-done.4.rest_7_ = bf16[192,512]{1,0:T(8,128)(2,1)S(1)} collective-permute-done((bf16[192,512]{1,0:T(8,128)(2,1)S(1)}, bf16[192,512]{1,0:T(8,128)(2,1)S(1)}, u32[]{:S(2)}, u32[]{:S(2)}) %collective-permute-start.4) | collective-permute-done | bytes 196640 | tf_op jit(solution)/shard_map/ppermute | solution.py:1004
  104.6 2.4 collective-permute-start.12
  107.0 2.4 collective-permute-start.13
  109.4 2.5 collective-permute-start.11
  111.9 1.4 fusion.56
  114.6 1.5 collective-permute-start.16
  116.1 11.0 %collective-permute-start.15 = (bf16[192,1536]{1,0:T(8,128)(2,1)}, bf16[192,1536]{1,0:T(8,128)(2,1)}, u32[]{:S(2)}, u32[]{:S(2)}) collective-permute-start(bf16[192,1536]{1,0:T(8,128)(2,1)} %pad_maximum_fusion.1.rest_8_.rest_9_), channel_id=1, source_target_pairs={{0,1},{4,5},{8,9},{12,13},{16,17},{20,21},{24,25},{28,29}} | collective-permute-start | bytes 1769480 | tf_op jit(solution)/shard_map/ppermute | solution.py:1004
  127.2 6.9 layer_forward.6
  134.9 4.9 collective-permute-done.15.rest_7_.rest_8_
  139.8 6.7 layer_forward.7
  148.1 9.9 %layer_forward.8 = (bf16[512,768]{1,0:T(8,128)(2,1)}, f32[8,768]{1,0:T(8,128)}, bf16[4,512,11520]{2,1,0:T(8,128)(2,1)}, f32[4,512,768]{2,1,0:T(8,128)}, f32[4,16,512]{2,1,0:T(8,128)}) custom-call(s32[13]{0:T(128)} %copy-done.28, bf16[768,768]{1,0:T(8,128)(2,1)} %fusion.1.rest_1_.rest_2_, ...), custom_call_target="tpu_custom_call", output_to_operand_aliasing={{2}: (18, {}), {3}: (19, {}), {4}: (20, {})} | custom-call | flops 10000000000 | bytes 30000000 | tf_op jit(solution)/shard_map/layer_forward/pallas_call | solution.py:329
  160.4 8.9 %layer_forward.9 = (bf16[512,768]{1,0:T(8,128)(2,1)}, f32[8,768]{1,0:T(8,128)}, bf16[4,512,11520]{2,1,0:T(8,128)(2,1)}, f32[4,512,768]{2,1,0:T(8,128)}, f32[4,16,512]{2,1,0:T(8,128)}) custom-call(s32[13]{0:T(128)} %copy-done.28, bf16[768,768]{1,0:T(8,128)(2,1)} %fusion.1.rest_1_.rest_2_, ...), custom_call_target="tpu_custom_call", output_to_operand_aliasing={{2}: (18, {}), {3}: (19, {}), {4}: (20, {})} | custom-call | flops 10000000000 | bytes 30000000 | tf_op jit(solution)/shard_map/layer_forward/pallas_call | solution.py:329
  171.6 9.1 %layer_forward.10 = (bf16[512,768]{1,0:T(8,128)(2,1)}, f32[8,768]{1,0:T(8,128)}, bf16[4,512,11520]{2,1,0:T(8,128)(2,1)}, f32[4,512,768]{2,1,0:T(8,128)}, f32[4,16,512]{2,1,0:T(8,128)}) custom-call(s32[13]{0:T(128)} %copy-done.28, bf16[768,768]{1,0:T(8,128)(2,1)} %fusion.1.rest_1_.rest_2_, ...), custom_call_target="tpu_custom_call", output_to_operand_aliasing={{2}: (18, {}), {3}: (19, {}), {4}: (20, {})} | custom-call | flops 10000000000 | bytes 30000000 | tf_op jit(solution)/shard_map/layer_forward/pallas_call | solution.py:329
  182.4 14.5 %layer_forward.11 = (bf16[512,768]{1,0:T(8,128)(2,1)}, f32[8,768]{1,0:T(8,128)}, bf16[4,512,11520]{2,1,0:T(8,128)(2,1)}, f32[4,512,768]{2,1,0:T(8,128)}, f32[4,16,512]{2,1,0:T(8,128)}) custom-call(s32[13]{0:T(128)} %copy-done.28, bf16[768,768]{1,0:T(8,128)(2,1)} %fusion.1.rest_1_.rest_2_, ...), custom_call_target="tpu_custom_call", output_to_operand_aliasing={{2}: (18, {}), {3}: (19, {}), {4}: (20, {})} | custom-call | flops 10000000000 | bytes 30000000 | tf_op jit(solution)/shard_map/layer_forward/pallas_call | solution.py:329
  200.5 2.9 layer_backward.6
  204.7 3.0 layer_backward.7
  209.3 5.5 layer_backward.8
  216.3 15.8 %layer_backward.9 = (bf16[512,768]{1,0:T(8,128)(2,1)}, f32[1,9984]{1,0:T(1,128)}, bf16[4,512,11520]{2,1,0:T(8,128)(2,1)}, bf16[192,1536]{1,0:T(8,128)(2,1)}, bf1...) custom-call(s32[13]{0:T(128)} %copy-done.28, ...), custom_call_target="tpu_custom_call", output_to_operand_aliasing={{2}: (15, {}), {3}: (18, {}), {4}: (19, {}), {5}: (20, {}),... | custom-call | flops 20000000000 | bytes 40000000 | tf_op jit(solution)/shard_map/layer_backward/pallas_call | solution.py:544
  233.7 7.2 layer_backward.10
  241.0 1.3 collective-permute-start.26
  244.6 3.6 layer_backward.11
  248.2 1.3 collective-permute-start.29
  250.2 217.4 %collective-permute-done.26 = bf16[192,1536]{1,0:T(8,128)(2,1)S(1)} collective-permute-done((bf16[192,1536]{1,0:T(8,128)(2,1)}, bf16[192,1536]{1,0:T(8,128)(2,1)S(1)}, u32[]{:S(2)}, u32[]{:S(2)}) %collective-permute-start.26) | collective-permute-done | bytes 589856 | tf_op jit(solution)/shard_map/ppermute | solution.py:1085
  468.3 16.1 %weight_products.4 = bf16[12,384,384]{2,1,0:T(8,128)(2,1)} custom-call(s32[96]{0:T(128)} %fusion.39.tiles, bf16[4,512,11520]{2,1,0:T(8,128)(2,1)} %get-tuple-element.224.x_ref.y_ref, bf16[4,512,11520]{2,1,0:T(8,128)(2,1)} %get-tuple-element.224.x_ref.y_ref), custom_call_target="tpu_custom_call" | custom-call | flops 1 | bytes 1 | tf_op jit(solution)/shard_map/weight_products/pallas_call | solution.py:671
  484.4 8.0 %collective-permute-done.29 = bf16[192,512]{1,0:T(8,128)(2,1)S(1)} collective-permute-done((bf16[192,512]{1,0:T(8,128)(2,1)}, bf16[192,512]{1,0:T(8,128)(2,1)S(1)}, u32[]{:S(2)}, u32[]{:S(2)}) %collective-permute-start.29) | collective-permute-done | bytes 196640 | tf_op jit(solution)/shard_map/ppermute | solution.py:1085
  493.9 6.4 collective-permute-done.32.refs_0_
  500.3 1.8 copy-done.3
  502.1 17.4 %weight_products.5 = (f32[1,384]{1,0:T(1,128)}, bf16[6,384,384]{2,1,0:T(8,128)(2,1)}, bf16[6,384,384]{2,1,0:T(8,128)(2,1)}) custom-call(s32[96]{0:T(128)} %fusion.39.tiles, bf16[4,512,11520]{2,1,0:T(8,128)(2,1)} %get-tuple-element.224.x_ref.y_ref, bf16[4,512,11520]{2,1,0:T(8,128)(2,1)} %get-tuple-element.224.x_ref.y_ref, bf16[12,384,384]{2,1,0:T(8,128)(2,1)} %copy-done.3), custom_call_target="tpu_custom_call" | custom-call | flops 1 | bytes 1 | tf_op jit(solution)/shard_map/weight_products/pallas_call | solution.py:671
  519.7 15.5 %weight_products.6 = bf16[12,384,384]{2,1,0:T(8,128)(2,1)} custom-call(s32[96]{0:T(128)} %fusion.39.tiles, bf16[4,512,11520]{2,1,0:T(8,128)(2,1)} %get-tuple-element.224.x_ref.y_ref, bf16[4,512,11520]{2,1,0:T(8,128)(2,1)} %get-tuple-element.224.x_ref.y_ref), custom_call_target="tpu_custom_call" | custom-call | flops 1 | bytes 1 | tf_op jit(solution)/shard_map/weight_products/pallas_call | solution.py:671
  535.1 1.6 collective-permute-start.33
  544.4 1.3 collective-permute-start.36
  545.7 1.9 collective-permute-start.37
  548.2 18.0 %weight_products.7 = (f32[1,384]{1,0:T(1,128)}, bf16[6,384,384]{2,1,0:T(8,128)(2,1)}, bf16[6,384,384]{2,1,0:T(8,128)(2,1)}) custom-call(s32[96]{0:T(128)} %fusion.39.tiles, bf16[4,512,11520]{2,1,0:T(8,128)(2,1)} %get-tuple-element.224.x_ref.y_ref, bf16[4,512,11520]{2,1,0:T(8,128)(2,1)} %get-tuple-element.224.x_ref.y_ref, ...), custom_call_target="tpu_custom_call" | custom-call | flops 1 | bytes 1 | tf_op jit(solution)/shard_map/weight_products/pallas_call | solution.py:671
  569.3 1.4 multiply_reduce_fusion
  571.4 1.3 reduce_sum.87
  573.3 1.3 reduce_sum.88
  576.0 35.0 %table_gradient.1 = (f32[96,50304]{1,0:T(8,128)}, f32[1,128]{1,0:T(1,128)}) custom-call(s32[4096]{0:T(1024)} %bitcast.62, bf16[96,1536]{1,0:T(8,128)(2,1)} %get-tuple-element.304.refs_0_, bf16[96,1536]{1,0:T(8,128)(2,1)} %copy-done.20, bf16[96,512]{1,0:T(8,128)(2,1)} %get-tuple-element.308.refs_2_, bf16[96,512]{1,0:T(8,128)(2,1)} %copy-done.33), custom_call_target="tpu_custom_call" | custom-call | flops 1 | bytes 1 | tf_op jit(solution)/shard_map/table_gradient/pallas_call | solution.py:820
  613.0 38.7 %all-reduce = (f32[1]{0:T(128)}, f32[]{:T(128)}) all-reduce(f32[1]{0:T(128)} %bitcast.10, f32[]{:T(128)S(6)} %add.251), channel_id=1, replica_groups=mesh['member'=4,'section'=2,'dp'=4] {'section','dp'}, use_global_device_ids=true, to_apply=%region_2.3 | all-reduce | flops 2 | bytes 16 | tf_op jit(solution)/shard_map/psum | solution.py:1157
  652.4 1.5 collective-permute-start.38
  653.8 46.9 %multiply_subtract_fusion = (f32[96,50304]{1,0:T(8,128)}, f32[96,50304]{1,0:T(8,128)}, f32[96,50304]{1,0:T(8,128)}) fusion(f32[96,50304]{1,0:T(8,128)} %embedding_ref.1, f32[96,50304]{1,0:T(8,128)} %get-tuple-element.263, f32[]{:T(128)} %div.112, f32[96,50304]{1,0:T(8,128)} %param.26, f32[96,50304]{1,0:T(8,128)} %param.27), kind=kLoop, calls=%fused_computation.3 | loop fusion | flops 77266944 | bytes 135217152 | tf_op jit(solution)/shard_map/sub | solution.py:899
  700.8 5.7 broadcast_select_fusion.2
  706.7 1.3 collective-permute-start.42
  708.6 1.3 collective-permute-start.40
  709.9 5.1 collective-permute-done.42
  715.0 3.5 collective-permute-done.40
  721.3 2.4 broadcast_select_fusion.1
  723.7 2.2 pad_maximum_fusion.g_ref
  725.9 26.3 %shampoo.1 = (f32[12,384,384]{2,1,0:T(8,128)}, f32[12,384,384]{2,1,0:T(8,128)}, f32[12,384,384]{2,1,0:T(8,128)}, f32[12,384,384]{2,1,0:T(8,128)}) custom-call(f32[1]{0:T(128)} %bitcast.22.factor_ref, bf16[12,384,384]{2,1,0:T(8,128)(2,1)} %pad_maximum_fusion.g_ref, f32[12,384,384]{2,1,0:T(8,128)} %bitcast.57, f32[12,384,384]{2,1,0:T(8,128)} %bitcast.58, ...), custom_call_target="tpu_custom_call" | custom-call | flops 1 | bytes 1 | tf_op jit(solution)/shard_map/shampoo/pallas_call | solution.py:869
  (248 shorter events, 56.4 us)
Async XLA Ops:
  4.1 12.3 %collective-permute-start.2 = (f32[3810]{0:T(1024)S(1)}, f32[3810]{0:T(1024)}, u32[]{:S(2)}, u32[]{:S(2)}) collective-permute-start(f32[3810]{0:T(1024)S(1)} %concatenate.29), channel_id=1, source_target_pairs={{0,3},{1,0},{2,1},{3,2},{4,7},{5,4},{6,5},{7,6},{8,11},{9,8},{10,9... | collective-permute-start | bytes 45728 | tf_op jit(solution)/shard_map/ppermute | solution.py:967
  9.2 7.9 %collective-permute-start.1 = (f32[3810]{0:T(1024)S(1)}, f32[3810]{0:T(1024)}, u32[]{:S(2)}, u32[]{:S(2)}) collective-permute-start(f32[3810]{0:T(1024)S(1)} %concatenate.29), channel_id=1, source_target_pairs={{0,2},{1,3},{2,0},{3,1},{4,6},{5,7},{6,4},{7,5},{8,10},{9,11},{10,... | collective-permute-start | bytes 45728 | tf_op jit(solution)/shard_map/ppermute | solution.py:967
  9.2 8.7 %collective-permute-start = (f32[3810]{0:T(1024)S(1)}, f32[3810]{0:T(1024)}, u32[]{:S(2)}, u32[]{:S(2)}) collective-permute-start(f32[3810]{0:T(1024)S(1)} %concatenate.29), channel_id=1, source_target_pairs={{0,1},{1,2},{2,3},{3,0},{4,5},{5,6},{6,7},{7,4},{8,9},{9,10},{10,1... | collective-permute-start | bytes 45728 | tf_op jit(solution)/shard_map/ppermute | solution.py:967
  14.8 92.2 %copy-start = (bf16[12,384,384]{2,1,0:T(8,128)(2,1)}, bf16[12,384,384]{2,1,0:T(8,128)(2,1)S(1)}, u32[]{:S(2)}) copy-start(bf16[12,384,384]{2,1,0:T(8,128)(2,1)S(1)} %bitcast_convert_fusion.rest_15_.rest_16_.rest_12_.rest_13_) | copy-start | bytes 10616836
  20.0 84.5 %collective-permute-start.9 = (bf16[12,384,384]{2,1,0:T(8,128)(2,1)S(1)}, bf16[12,384,384]{2,1,0:T(8,128)(2,1)}, u32[]{:S(2)}, u32[]{:S(2)}) collective-permute-start(bf16[12,384,384]{2,1,0:T(8,128)(2,1)S(1)} %bitcast_convert_fusion.rest_15_.rest_16_.rest_12_.rest_13_), channel_id=1, source_target_pairs={{0,1},{7,6},{8,9},{15,14},{16,17},{23,22},{24,25},{31,30}} | collective-permute-start | bytes 10616840 | tf_op jit(solution)/shard_map/ppermute | solution.py:979
  26.2 78.3 %collective-permute-start.8 = (bf16[12,384,384]{2,1,0:T(8,128)(2,1)S(1)}, bf16[12,384,384]{2,1,0:T(8,128)(2,1)}, u32[]{:S(2)}, u32[]{:S(2)}) collective-permute-start(bf16[12,384,384]{2,1,0:T(8,128)(2,1)S(1)} %bitcast_convert_fusion.rest_15_.rest_16_.rest_12_.rest_13_), channel_id=1, source_target_pairs={{3,1},{4,6},{2,5},{5,2},{11,9},{12,14},{10,13},{13,10},{19,17},{20... | collective-permute-start | bytes 10616840 | tf_op jit(solution)/shard_map/ppermute | solution.py:979
  41.3 26.4 %collective-permute-start.10 = (f32[4,2784]{1,0:T(4,128)}, f32[4,2784]{1,0:T(4,128)S(1)}, u32[]{:S(2)}, u32[]{:S(2)}) collective-permute-start(f32[4,2784]{1,0:T(4,128)} %slice.162), channel_id=1, source_target_pairs={{0,4},{4,0},{1,5},{5,1},{2,6},{6,2},{3,7},{7,3},{8,12},{12,8},{9,1... | collective-permute-start | bytes 133640 | tf_op jit(solution)/shard_map/ppermute | solution.py:920
  42.6 25.7 %copy-start.27 = (f32[4,2784]{1,0:T(4,128)S(1)}, f32[4,2784]{1,0:T(4,128)}, u32[]{:S(2)}) copy-start(f32[4,2784]{1,0:T(4,128)} %slice.162) | copy-start | bytes 133636
  42.6 69.2 %copy-start.57 = (s32[13]{0:T(128)S(1)}, s32[13]{0:T(128)}, u32[]{:S(2)}) copy-start(s32[13]{0:T(128)} %constant.210.clone) | copy-start | bytes 160
  65.5 7.2 collective-permute-start.3
  67.7 7.3 collective-permute-start.7
  72.7 41.3 %copy-start.5 = (f32[1,2304]{1,0:T(1,128)}, f32[1,2304]{1,0:T(1,128)S(1)}, u32[]{:S(2)}) copy-start(f32[1,2304]{1,0:T(1,128)S(1)} %reshape.232.rest_3_.rest_4_) | copy-start | bytes 27652
  73.7 35.7 %copy-start.23 = (bf16[192,512]{1,0:T(8,128)(2,1)}, bf16[192,512]{1,0:T(8,128)(2,1)S(1)}, u32[]{:S(2)}) copy-start(bf16[192,512]{1,0:T(8,128)(2,1)S(1)} %pad_maximum_fusion.2.rest_8_) | copy-start | bytes 589828
  73.7 4.9 collective-permute-start.6
  74.4 4.2 collective-permute-start.5
  75.0 29.5 %collective-permute-start.4 = (bf16[192,512]{1,0:T(8,128)(2,1)S(1)}, bf16[192,512]{1,0:T(8,128)(2,1)S(1)}, u32[]{:S(2)}, u32[]{:S(2)}) collective-permute-start(bf16[192,512]{1,0:T(8,128)(2,1)S(1)} %pad_maximum_fusion.2.rest_8_), channel_id=1, source_target_pairs={{0,1},{4,5},{8,9},{12,13},{16,17},{20,21},{24,25},{28,29}} | collective-permute-start | bytes 589832 | tf_op jit(solution)/shard_map/ppermute | solution.py:1004
  78.6 30.8 %copy-start.58 = (bf16[192,512]{1,0:T(8,128)(2,1)}, bf16[192,512]{1,0:T(8,128)(2,1)S(1)}, u32[]{:S(2)}) copy-start(bf16[192,512]{1,0:T(8,128)(2,1)S(1)} %collective-permute-done.6.rest_10_) | copy-start | bytes 589828
  78.6 30.8 %copy-start.59 = (bf16[192,512]{1,0:T(8,128)(2,1)}, bf16[192,512]{1,0:T(8,128)(2,1)S(1)}, u32[]{:S(2)}) copy-start(bf16[192,512]{1,0:T(8,128)(2,1)S(1)} %collective-permute-done.5.rest_9_) | copy-start | bytes 589828
  104.6 9.3 %collective-permute-start.12 = (bf16[12,384,384]{2,1,0:T(8,128)(2,1)}, bf16[12,384,384]{2,1,0:T(8,128)(2,1)}, u32[]{:S(2)}, u32[]{:S(2)}) collective-permute-start(bf16[12,384,384]{2,1,0:T(8,128)(2,1)} %collective-permute-done.9.rest_12_.rest_13_.rest_9_.rest_10_), channel_id=1, source_target_pairs={{1,5},{5,1},{2,6},{6,2},{9,13},{13,9},{10,14},{14,10},{17,21},{21,... | collective-permute-start | bytes 10616840 | tf_op jit(solution)/shard_map/ppermute | solution.py:1023
  107.0 20.2 %collective-permute-start.13 = (bf16[12,384,384]{2,1,0:T(8,128)(2,1)S(1)}, bf16[12,384,384]{2,1,0:T(8,128)(2,1)}, u32[]{:S(2)}, u32[]{:S(2)}) collective-permute-start(bf16[12,384,384]{2,1,0:T(8,128)(2,1)S(1)} %bitcast_convert_fusion.rest_15_.rest_16_.rest_12_.rest_13_), channel_id=1, source_target_pairs={{1,5},{5,1},{2,6},{6,2},{9,13},{13,9},{10,14},{14,10},{17,21},{21,... | collective-permute-start | bytes 10616840 | tf_op jit(solution)/shard_map/ppermute | solution.py:1023
  109.4 17.8 %collective-permute-start.11 = (bf16[12,384,384]{2,1,0:T(8,128)(2,1)}, bf16[12,384,384]{2,1,0:T(8,128)(2,1)}, u32[]{:S(2)}, u32[]{:S(2)}) collective-permute-start(bf16[12,384,384]{2,1,0:T(8,128)(2,1)} %collective-permute-done.8.rest_11_.rest_12_.rest_8_.rest_9_), channel_id=1, source_target_pairs={{1,5},{5,1},{2,6},{6,2},{9,13},{13,9},{10,14},{14,10},{17,21},{21,... | collective-permute-start | bytes 10616840 | tf_op jit(solution)/shard_map/ppermute | solution.py:1023
  113.9 20.9 %collective-permute-start.17 = (bf16[192,1536]{1,0:T(8,128)(2,1)}, bf16[192,1536]{1,0:T(8,128)(2,1)S(1)}, u32[]{:S(2)}, u32[]{:S(2)}) collective-permute-start(bf16[192,1536]{1,0:T(8,128)(2,1)} %pad_maximum_fusion.1.rest_8_.rest_9_), channel_id=1, source_target_pairs={{3,1},{7,5},{11,9},{15,13},{19,17},{23,21},{27,25},{31,29}} | collective-permute-start | bytes 1769480 | tf_op jit(solution)/shard_map/ppermute | solution.py:1004
  114.6 20.2 %collective-permute-start.16 = (bf16[192,1536]{1,0:T(8,128)(2,1)}, bf16[192,1536]{1,0:T(8,128)(2,1)}, u32[]{:S(2)}, u32[]{:S(2)}) collective-permute-start(bf16[192,1536]{1,0:T(8,128)(2,1)} %pad_maximum_fusion.1.rest_8_.rest_9_), channel_id=1, source_target_pairs={{2,1},{6,5},{10,9},{14,13},{18,17},{22,21},{26,25},{30,29}} | collective-permute-start | bytes 1769480 | tf_op jit(solution)/shard_map/ppermute | solution.py:1004
  116.1 23.7 %collective-permute-start.15 = (bf16[192,1536]{1,0:T(8,128)(2,1)}, bf16[192,1536]{1,0:T(8,128)(2,1)}, u32[]{:S(2)}, u32[]{:S(2)}) collective-permute-start(bf16[192,1536]{1,0:T(8,128)(2,1)} %pad_maximum_fusion.1.rest_8_.rest_9_), channel_id=1, source_target_pairs={{0,1},{4,5},{8,9},{12,13},{16,17},{20,21},{24,25},{28,29}} | collective-permute-start | bytes 1769480 | tf_op jit(solution)/shard_map/ppermute | solution.py:1004
  134.1 13.1 %collective-permute-start.14 = (bf16[512,768]{1,0:T(8,128)(2,1)}, bf16[512,768]{1,0:T(8,128)(2,1)S(1)}, u32[]{:S(2)}, u32[]{:S(2)}) collective-permute-start(bf16[512,768]{1,0:T(8,128)(2,1)} %get-tuple-element.168), channel_id=1, source_target_pairs={{1,2},{5,6},{9,10},{13,14},{17,18},{21,22},{25,26},{29,30}} | collective-permute-start | bytes 2359304 | tf_op jit(solution)/shard_map/ppermute | solution.py:1058
  146.5 13.0 %collective-permute-start.18 = (bf16[512,768]{1,0:T(8,128)(2,1)}, bf16[512,768]{1,0:T(8,128)(2,1)S(1)}, u32[]{:S(2)}, u32[]{:S(2)}) collective-permute-start(bf16[512,768]{1,0:T(8,128)(2,1)} %get-tuple-element.177), channel_id=1, source_target_pairs={{1,2},{5,6},{9,10},{13,14},{17,18},{21,22},{25,26},{29,30}} | collective-permute-start | bytes 2359304 | tf_op jit(solution)/shard_map/ppermute | solution.py:1058
  158.0 12.7 %collective-permute-start.19 = (bf16[512,768]{1,0:T(8,128)(2,1)}, bf16[512,768]{1,0:T(8,128)(2,1)S(1)}, u32[]{:S(2)}, u32[]{:S(2)}) collective-permute-start(bf16[512,768]{1,0:T(8,128)(2,1)} %get-tuple-element.182), channel_id=1, source_target_pairs={{1,2},{5,6},{9,10},{13,14},{17,18},{21,22},{25,26},{29,30}} | collective-permute-start | bytes 2359304 | tf_op jit(solution)/shard_map/ppermute | solution.py:1058
  169.3 12.2 %collective-permute-start.20 = (bf16[512,768]{1,0:T(8,128)(2,1)}, bf16[512,768]{1,0:T(8,128)(2,1)S(1)}, u32[]{:S(2)}, u32[]{:S(2)}) collective-permute-start(bf16[512,768]{1,0:T(8,128)(2,1)} %get-tuple-element.187), channel_id=1, source_target_pairs={{1,2},{5,6},{9,10},{13,14},{17,18},{21,22},{25,26},{29,30}} | collective-permute-start | bytes 2359304 | tf_op jit(solution)/shard_map/ppermute | solution.py:1058
  203.5 4.9 collective-permute-start.21
  207.6 7.8 %collective-permute-start.22 = (bf16[512,768]{1,0:T(8,128)(2,1)}, bf16[512,768]{1,0:T(8,128)(2,1)S(1)}, u32[]{:S(2)}, u32[]{:S(2)}) collective-permute-start(bf16[512,768]{1,0:T(8,128)(2,1)} %get-tuple-element.201), channel_id=1, source_target_pairs={{2,1},{6,5},{10,9},{14,13},{18,17},{22,21},{26,25},{30,29}} | collective-permute-start | bytes 2359304 | tf_op jit(solution)/shard_map/ppermute | solution.py:1115
  214.7 18.1 %collective-permute-start.23 = (bf16[512,768]{1,0:T(8,128)(2,1)}, bf16[512,768]{1,0:T(8,128)(2,1)S(1)}, u32[]{:S(2)}, u32[]{:S(2)}) collective-permute-start(bf16[512,768]{1,0:T(8,128)(2,1)} %get-tuple-element.208), channel_id=1, source_target_pairs={{2,1},{6,5},{10,9},{14,13},{18,17},{22,21},{26,25},{30,29}} | collective-permute-start | bytes 2359304 | tf_op jit(solution)/shard_map/ppermute | solution.py:1115
  232.1 11.5 %collective-permute-start.24 = (bf16[512,768]{1,0:T(8,128)(2,1)}, bf16[512,768]{1,0:T(8,128)(2,1)S(1)}, u32[]{:S(2)}, u32[]{:S(2)}) collective-permute-start(bf16[512,768]{1,0:T(8,128)(2,1)} %get-tuple-element.215), channel_id=1, source_target_pairs={{2,1},{6,5},{10,9},{14,13},{18,17},{22,21},{26,25},{30,29}} | collective-permute-start | bytes 2359304 | tf_op jit(solution)/shard_map/ppermute | solution.py:1115
  241.0 226.6 %collective-permute-start.26 = (bf16[192,1536]{1,0:T(8,128)(2,1)}, bf16[192,1536]{1,0:T(8,128)(2,1)S(1)}, u32[]{:S(2)}, u32[]{:S(2)}) collective-permute-start(bf16[192,1536]{1,0:T(8,128)(2,1)} %get-tuple-element.218), channel_id=1, source_target_pairs={{1,0},{5,4},{9,8},{13,12},{17,16},{21,20},{25,24},{29,28}} | collective-permute-start | bytes 1769480 | tf_op jit(solution)/shard_map/ppermute | solution.py:1085
  242.3 226.0 %collective-permute-start.27 = (bf16[192,1536]{1,0:T(8,128)(2,1)}, bf16[192,1536]{1,0:T(8,128)(2,1)S(1)}, u32[]{:S(2)}, u32[]{:S(2)}) collective-permute-start(bf16[192,1536]{1,0:T(8,128)(2,1)} %get-tuple-element.220), channel_id=1, source_target_pairs={{1,2},{5,6},{9,10},{13,14},{17,18},{21,22},{25,26},{29,30}} | collective-permute-start | bytes 1769480 | tf_op jit(solution)/shard_map/ppermute | solution.py:1085
  243.0 225.3 %collective-permute-start.28 = (bf16[192,1536]{1,0:T(8,128)(2,1)}, bf16[192,1536]{1,0:T(8,128)(2,1)S(1)}, u32[]{:S(2)}, u32[]{:S(2)}) collective-permute-start(bf16[192,1536]{1,0:T(8,128)(2,1)} %get-tuple-element.221), channel_id=1, source_target_pairs={{1,3},{5,7},{9,11},{13,15},{17,19},{21,23},{25,27},{29,31}} | collective-permute-start | bytes 1769480 | tf_op jit(solution)/shard_map/ppermute | solution.py:1085
  248.2 244.3 %collective-permute-start.29 = (bf16[192,512]{1,0:T(8,128)(2,1)}, bf16[192,512]{1,0:T(8,128)(2,1)S(1)}, u32[]{:S(2)}, u32[]{:S(2)}) collective-permute-start(bf16[192,512]{1,0:T(8,128)(2,1)} %get-tuple-element.225), channel_id=1, source_target_pairs={{1,0},{5,4},{9,8},{13,12},{17,16},{21,20},{25,24},{29,28}} | collective-permute-start | bytes 589832 | tf_op jit(solution)/shard_map/ppermute | solution.py:1085
  249.5 243.0 %collective-permute-start.30 = (bf16[192,512]{1,0:T(8,128)(2,1)}, bf16[192,512]{1,0:T(8,128)(2,1)S(1)}, u32[]{:S(2)}, u32[]{:S(2)}) collective-permute-start(bf16[192,512]{1,0:T(8,128)(2,1)} %get-tuple-element.227), channel_id=1, source_target_pairs={{1,2},{5,6},{9,10},{13,14},{17,18},{21,22},{25,26},{29,30}} | collective-permute-start | bytes 589832 | tf_op jit(solution)/shard_map/ppermute | solution.py:1085
  467.6 24.9 %collective-permute-start.31 = (bf16[192,512]{1,0:T(8,128)(2,1)}, bf16[192,512]{1,0:T(8,128)(2,1)S(1)}, u32[]{:S(2)}, u32[]{:S(2)}) collective-permute-start(bf16[192,512]{1,0:T(8,128)(2,1)} %get-tuple-element.228), channel_id=1, source_target_pairs={{1,3},{5,7},{9,11},{13,15},{17,19},{21,23},{25,27},{29,31}} | collective-permute-start | bytes 589832 | tf_op jit(solution)/shard_map/ppermute | solution.py:1085
  493.9 6.4 collective-permute-start.32
  519.5 22.5 %copy-start.53 = (f32[2]{0:T(128)S(1)}, f32[2]{0:T(128)}, u32[]{:S(2)}) copy-start(f32[2]{0:T(128)} %get-tuple-element.324) | copy-start | bytes 28
  519.5 22.5 %copy-start.54 = (f32[2]{0:T(128)S(1)}, f32[2]{0:T(128)}, u32[]{:S(2)}) copy-start(f32[2]{0:T(128)} %get-tuple-element.325) | copy-start | bytes 28
  519.5 22.5 %copy-start.55 = (f32[2]{0:T(128)S(1)}, f32[2]{0:T(128)}, u32[]{:S(2)}) copy-start(f32[2]{0:T(128)} %get-tuple-element.326) | copy-start | bytes 28
  519.5 22.5 %copy-start.56 = (f32[2]{0:T(128)S(1)}, f32[2]{0:T(128)}, u32[]{:S(2)}) copy-start(f32[2]{0:T(128)} %get-tuple-element.327) | copy-start | bytes 28
  519.6 24.3 %copy-start.32 = (f32[4,1,768]{2,1,0:T(1,128)S(1)}, f32[4,1,768]{2,1,0:T(1,128)}, u32[]{:S(2)}) copy-start(f32[4,1,768]{2,1,0:T(1,128)} %copy-done.31) | copy-start | bytes 36868
  519.6 24.3 %copy-start.35 = (f32[4,1,768]{2,1,0:T(1,128)S(1)}, f32[4,1,768]{2,1,0:T(1,128)}, u32[]{:S(2)}) copy-start(f32[4,1,768]{2,1,0:T(1,128)} %get-tuple-element.313) | copy-start | bytes 36868
  519.6 24.3 %copy-start.45 = (f32[4]{0:T(128)S(1)}, f32[4]{0:T(128)}, u32[]{:S(2)}) copy-start(f32[4]{0:T(128)} %div.111.rest_1_) | copy-start | bytes 52
  519.6 24.4 %copy-start.44 = (f32[768]{0:T(1024)S(1)}, f32[768]{0:T(1024)}, u32[]{:S(2)}) copy-start(f32[768]{0:T(1024)} %slice_reduce_fusion) | copy-start | bytes 9220
  519.6 24.5 %copy-start.37 = (f32[1,9984]{1,0:T(1,128)S(1)}, f32[1,9984]{1,0:T(1,128)}, u32[]{:S(2)}) copy-start(f32[1,9984]{1,0:T(1,128)} %get-tuple-element.195) | copy-start | bytes 119812
  519.6 24.5 %copy-start.38 = (f32[1,9984]{1,0:T(1,128)S(1)}, f32[1,9984]{1,0:T(1,128)}, u32[]{:S(2)}) copy-start(f32[1,9984]{1,0:T(1,128)} %get-tuple-element.197) | copy-start | bytes 119812
  519.6 24.5 %copy-start.39 = (f32[1,9984]{1,0:T(1,128)S(1)}, f32[1,9984]{1,0:T(1,128)}, u32[]{:S(2)}) copy-start(f32[1,9984]{1,0:T(1,128)} %get-tuple-element.200) | copy-start | bytes 119812
  519.6 24.5 %copy-start.40 = (f32[1,9984]{1,0:T(1,128)S(1)}, f32[1,9984]{1,0:T(1,128)}, u32[]{:S(2)}) copy-start(f32[1,9984]{1,0:T(1,128)} %get-tuple-element.207) | copy-start | bytes 119812
  519.6 24.5 %copy-start.41 = (f32[1,9984]{1,0:T(1,128)S(1)}, f32[1,9984]{1,0:T(1,128)}, u32[]{:S(2)}) copy-start(f32[1,9984]{1,0:T(1,128)} %get-tuple-element.214) | copy-start | bytes 119812
  519.6 24.5 %copy-start.42 = (f32[1,9984]{1,0:T(1,128)S(1)}, f32[1,9984]{1,0:T(1,128)}, u32[]{:S(2)}) copy-start(f32[1,9984]{1,0:T(1,128)} %get-tuple-element.217) | copy-start | bytes 119812
  535.1 13.1 %collective-permute-start.33 = (bf16[12,384,384]{2,1,0:T(8,128)(2,1)}, bf16[12,384,384]{2,1,0:T(8,128)(2,1)}, u32[]{:S(2)}, u32[]{:S(2)}) collective-permute-start(bf16[12,384,384]{2,1,0:T(8,128)(2,1)} %weight_products.6), channel_id=1, source_target_pairs={{0,4},{4,0},{1,5},{5,1},{2,6},{6,2},{3,7},{7,3},{8,12},{12,8},{9,1... | collective-permute-start | bytes 10616840 | tf_op jit(solution)/shard_map/ppermute | solution.py:920
  544.4 68.6 %collective-permute-start.36 = (bf16[6,384,384]{2,1,0:T(8,128)(2,1)}, bf16[6,384,384]{2,1,0:T(8,128)(2,1)S(1)}, u32[]{:S(2)}, u32[]{:S(2)}) collective-permute-start(bf16[6,384,384]{2,1,0:T(8,128)(2,1)} %get-tuple-element.253), channel_id=1, source_target_pairs={{1,3},{2,0},{5,7},{6,4},{9,11},{10,8},{13,15},{14,12},{17,19},{18,... | collective-permute-start | bytes 5308424 | tf_op jit(solution)/shard_map/ppermute | solution.py:1128
  545.7 67.3 %collective-permute-start.37 = (bf16[6,384,384]{2,1,0:T(8,128)(2,1)}, bf16[6,384,384]{2,1,0:T(8,128)(2,1)}, u32[]{:S(2)}, u32[]{:S(2)}) collective-permute-start(bf16[6,384,384]{2,1,0:T(8,128)(2,1)} %get-tuple-element.254), channel_id=1, source_target_pairs={{1,2},{2,1},{5,6},{6,5},{9,10},{10,9},{13,14},{14,13},{17,18},{18,... | collective-permute-start | bytes 5308424 | tf_op jit(solution)/shard_map/ppermute | solution.py:1128
  548.2 21.1 %collective-permute-start.25 = (f32[12288]{0:T(1024)}, f32[12288]{0:T(1024)}, u32[]{:S(2)}, u32[]{:S(2)}) collective-permute-start(f32[12288]{0:T(1024)} %pad_maximum_fusion.4), channel_id=1, source_target_pairs={{0,4},{4,0},{1,5},{5,1},{2,6},{6,2},{3,7},{7,3},{8,12},{12,8},{9,1... | collective-permute-start | bytes 147464 | tf_op jit(solution)/shard_map/ppermute | solution.py:920
  567.1 8.1 %collective-permute-start.34 = (bf16[96,1536]{1,0:T(8,128)(2,1)S(1)}, bf16[96,1536]{1,0:T(8,128)(2,1)S(1)}, u32[]{:S(2)}, u32[]{:S(2)}) collective-permute-start(bf16[96,1536]{1,0:T(8,128)(2,1)S(1)} %get-tuple-element.303), channel_id=1, source_target_pairs={{0,4},{4,0},{1,5},{5,1},{2,6},{6,2},{3,7},{7,3},{8,12},{12,8},{9,1... | collective-permute-start | bytes 884744 | tf_op jit(solution)/shard_map/ppermute | solution.py:920
  568.8 6.5 collective-permute-start.35
  652.4 48.4 %collective-permute-start.38 = (bf16[6,384,384]{2,1,0:T(8,128)(2,1)}, bf16[6,384,384]{2,1,0:T(8,128)(2,1)}, u32[]{:S(2)}, u32[]{:S(2)}) collective-permute-start(bf16[6,384,384]{2,1,0:T(8,128)(2,1)} %get-tuple-element.261), channel_id=1, source_target_pairs={{1,0},{2,3},{5,4},{6,7},{9,8},{10,11},{13,12},{14,15},{17,16},{18,... | collective-permute-start | bytes 5308424 | tf_op jit(solution)/shard_map/ppermute | solution.py:1128
  706.5 13.6 %collective-permute-start.39 = (bf16[6,384,384]{2,1,0:T(8,128)(2,1)}, bf16[6,384,384]{2,1,0:T(8,128)(2,1)S(1)}, u32[]{:S(2)}, u32[]{:S(2)}) collective-permute-start(bf16[6,384,384]{2,1,0:T(8,128)(2,1)} %get-tuple-element.287), channel_id=1, source_target_pairs={{0,4},{4,0},{1,5},{5,1},{2,6},{6,2},{3,7},{7,3},{8,12},{12,8},{9,1... | collective-permute-start | bytes 5308424 | tf_op jit(solution)/shard_map/ppermute | solution.py:920
  706.7 8.4 %collective-permute-start.42 = (f32[12288]{0:T(1024)S(1)}, f32[12288]{0:T(1024)S(1)}, u32[]{:S(2)}, u32[]{:S(2)}) collective-permute-start(f32[12288]{0:T(1024)S(1)} %get-tuple-element.294), channel_id=1, source_target_pairs={{1,3},{2,0},{5,7},{6,4},{9,11},{10,8},{13,15},{14,12},{17,19},{18,... | collective-permute-start | bytes 147464 | tf_op jit(solution)/shard_map/ppermute | solution.py:1128
  708.0 7.1 collective-permute-start.41
  708.6 9.9 %collective-permute-start.40 = (f32[12288]{0:T(1024)S(1)}, f32[12288]{0:T(1024)S(1)}, u32[]{:S(2)}, u32[]{:S(2)}) collective-permute-start(f32[12288]{0:T(1024)S(1)} %get-tuple-element.294), channel_id=1, source_target_pairs={{1,0},{2,3},{5,4},{6,7},{9,8},{10,11},{13,12},{14,15},{17,16},{18,... | collective-permute-start | bytes 147464 | tf_op jit(solution)/shard_map/ppermute | solution.py:1128
  (40 other events, 352.0 us)

commit v4 on v3

--- a/solution.py
+++ b/solution.py
@@ -300,11 +300,15 @@
     ]
     for copy in tails:
         copy.start()
-    hat, _ = normalized(out)
-    final = (hat * fin_ref[:, :D] + fin_ref[:, D : 2 * D]).astype(bf16)
-    red_ref[0:1, :] = jnp.sum(hat, axis=0, keepdims=True)
-    red_ref[1:2, :] = jnp.sum(final.astype(f32), axis=0, keepdims=True)
-    red_ref[2:8, :] = jnp.zeros((6, D), f32)
+
+    @pl.when(meta_ref[0] >= 2)
+    def _():
+        hat, _ = normalized(xo[...])
+        final = (hat * fin_ref[:, :D] + fin_ref[:, D : 2 * D]).astype(bf16)
+        red_ref[0:1, :] = jnp.sum(hat, axis=0, keepdims=True)
+        red_ref[1:2, :] = jnp.sum(final.astype(f32), axis=0, keepdims=True)
+        red_ref[2:8, :] = jnp.zeros((6, D), f32)
+
     for copy in stores + tails:
         copy.wait()
 
@@ -388,17 +392,25 @@
         pltpu.make_async_copy(kept_in.at[slot, :, pl.ds(COL_QKV, 3 * D)], qkv, isem.at[3]),
         pltpu.make_async_copy(lse_in.at[slot], lse, isem.at[4]),
     ]
-    loads[0].start()
+    is_high = meta_ref[0] >= 2
+    pl.when(is_high)(loads[0].start)
     weights.start(1)
     loads[3].start()
     loads[4].start()
-    loads[0].wait()
-    hat, scale = normalized(xo[...])
-    headed = fin_ref[:, 2 * D : 3 * D] * fin_ref[:, :D]
-    top = flag_ref[min(tick, units - 1)] * norm_back(1.0, headed, hat, scale)
+
+    @pl.when(is_high)
+    def _():
+        loads[0].wait()
+        hat, scale = normalized(xo[...])
+        headed = fin_ref[:, 2 * D : 3 * D] * fin_ref[:, :D]
+        xo[...] = flag_ref[min(tick, units - 1)] * norm_back(1.0, headed, hat, scale)
+
     if handed:
-        top = jnp.where(meta_ref[0] >= 2, top, recv_ref[...].astype(f32))
-    xo[...] = top
+
+        @pl.when(jnp.logical_not(is_high))
+        def _():
+            xo[...] = recv_ref[...].astype(f32)
+
     grads[:, COL_G : COL_G + D] = xo[...].astype(bf16)
     bias = jnp.sum(grads[:, COL_G : COL_G + D].astype(f32), axis=0, keepdims=True)
     vg_ref[:, V_O : V_O + D] = bias
@@ -512,15 +524,23 @@
     total = xo[...] + norm_back(one, vec_ref[:, V_G1 : V_G1 + D], hat, scale)
     dx_ref[...] = total.astype(bf16)
     if back_out:
-        turned[...] = nt(order_ref[...], dx_ref[...]).astype(bf16)
-        start = (tick - 2) * length if tick <= units else 0
-        width = backs[0].shape[0]
-        for k, back in enumerate(backs):
-            copy = pltpu.make_async_copy(
-                turned.at[pl.ds(k * width, width)], back.at[:, pl.ds(start, length)], bsem.at[k]
-            )
-            copy.start()
-            stores.append(copy)
+
+        @pl.when(jnp.logical_not(is_high))
+        def _():
+            turned[...] = nt(order_ref[...], dx_ref[...]).astype(bf16)
+            start = (tick - 2) * length if tick <= units else 0
+            width = backs[0].shape[0]
+            copies = [
+                pltpu.make_async_copy(
+                    turned.at[pl.ds(k * width, width)], back.at[:, pl.ds(start, length)], bsem.at[k]
+                )
+                for k, back in enumerate(backs)
+            ]
+            for copy in copies:
+                copy.start()
+            for copy in copies:
+                copy.wait()
+
     for copy in stores:
         copy.wait()
 
@@ -609,8 +629,8 @@
     for i in range(each):
         whole = found[:, i * TILE : (i + 1) * TILE] + sent_ref[i].astype(f32)
         blocks.append(whole.astype(bf16))
-        weight = tiles[start + 2 * steps + step * each + i].astype(f32)
-        square_ref[...] += weight * jnp.sum(whole * whole, axis=0, keepdims=True)
+        counts = tiles[start + 2 * steps + step * each + i] > 0
+        square_ref[...] += jnp.sum(jnp.where(counts, whole * whole, 0.0), axis=0, keepdims=True)
     per = steps // shards
     for shard, out_ref in enumerate(out_refs):
 
@@ -638,6 +658,7 @@
                     row += [left[b] for b in places[::each]] + [right[b] for b in places[::each]]
                     row += [0 if half == 1 and i < part - rest else 1 for _ in shards for i in range(part)]
             found.append(row)
+    found.append([0] * len(found[0]))
     return found
 
 
@@ -757,7 +778,7 @@
 
 
 def table_kernel(ids_ref, *refs):
-    parts = refs[:-5]
+    *parts, vectors_ref, first_ref, second_ref = refs[:-5]
     out_ref, square_ref, table, wide, total = refs[-5:]
     step = pl.program_id(0)
     features = out_ref.shape[0]
@@ -810,24 +831,31 @@
 
     @pl.when(step == pl.num_programs(0) - 1)
     def _():
-        square_ref[...] = jnp.sum(total[...], axis=0, keepdims=True)
-
-
-def table_gradient(ids, parts, vocab):
+        lanes_sum = jnp.sum(total[...], axis=0, keepdims=True)
+        others = jnp.sum(first_ref[...] + second_ref[...], axis=1, keepdims=True)
+        vectors = vectors_ref[...]
+        others = others + 0.5 * jnp.sum(vectors * vectors, axis=1, keepdims=True)
+        square_ref[...] = jnp.sum(lanes_sum, axis=1, keepdims=True) + others
+
+
+def table_gradient(ids, parts, vocab, vectors, first, second):
     tokens, features = ids.shape[0], parts[0].shape[0]
     lanes = 128
     steps = 3 if vocab % (3 * lanes) == 0 else 1
     return pl.pallas_call(
         table_kernel,
-        out_shape=(jax.ShapeDtypeStruct((features, vocab), f32), jax.ShapeDtypeStruct((1, lanes), f32)),
+        out_shape=(jax.ShapeDtypeStruct((features, vocab), f32), jax.ShapeDtypeStruct((1, 1), f32)),
         grid=(steps,),
         in_specs=[
             pl.BlockSpec(memory_space=pltpu.SMEM),
         ]
-        + [pl.BlockSpec(part.shape, lambda i: (0, 0), pipeline_mode=pl.Buffered(1)) for part in parts],
+        + [
+            pl.BlockSpec(part.shape, lambda i: (0, 0), pipeline_mode=pl.Buffered(1))
+            for part in (*parts, vectors, first, second)
+        ],
         out_specs=(
             pl.BlockSpec((features, vocab // steps), lambda i: (0, i)),
-            pl.BlockSpec((1, lanes), lambda i: (0, 0)),
+            pl.BlockSpec((1, 1), lambda i: (0, 0)),
         ),
         scratch_shapes=[
             pltpu.VMEM((vocab, lanes), f32),
@@ -837,7 +865,7 @@
         compiler_params=pltpu.CompilerParams(vmem_limit_bytes=VMEM_LIMIT),
         cost_estimate=LIGHT,
         name="table_gradient",
-    )(ids, *parts)
+    )(ids, *parts, vectors, first, second)
 
 
 def split(value):
@@ -1013,7 +1041,10 @@
     each = 2 if own_blocks % 4 == 0 else 1
     group = max(count // 2, 1)
     tiles = lax.dynamic_index_in_dim(
-        jnp.array(product_tiles(count, each), jnp.int32), is_high * 2 + section, 0, False
+        jnp.array(product_tiles(count, each), jnp.int32),
+        jnp.where((place == low) | (place == high), is_high * 2 + section, 4),
+        0,
+        False,
     )
 
     first, later, received, vec, fin, tables, order, tiles = lax.optimization_barrier(
@@ -1127,10 +1158,9 @@
         ]
         return lax.ppermute(value, both, route) if step < count - 1 else value
 
-    live = live_low | live_high
     token_grads[0], tiles = lax.optimization_barrier((token_grads[0], tiles))
     kept = state[0]
-    squares = jnp.where(live & (section == 0), jnp.sum(vector_pack * vector_pack), 0.0)
+    block_squares = []
     ids_ordered = jnp.concatenate(
         [ids_here[0, :-1], ids_here[1, :-1], ids_here[0, -1:], ids_here[1, -1:]], axis=0
     ).reshape(-1)
@@ -1139,23 +1169,32 @@
         sums = products(group, tiles, 2 * index, kept, units, each)
         if index == 0:
             token_grads[1], sums = lax.optimization_barrier((token_grads[1], sums))
-        block_squares, *found = products(group, tiles, 2 * index + 1, kept, units, each, swapped(sums))
-        squares = squares + jnp.where(live, jnp.sum(block_squares), 0.0)
+            vectors = [to_owner(vector_pack, step) for step in range(count)]
+            token_parts = own_features(token_grads[0]) + own_features(token_grads[1])
+        else:
+            vectors, token_parts, sums = lax.optimization_barrier((vectors, token_parts, sums))
+        tiles, sums = lax.optimization_barrier((tiles, sums))
+        sent.append(swapped(sums))
+    for index in range(count // group):
+        square, *found = products(group, tiles, 2 * index + 1, kept, units, each, sent[index])
+        block_squares.append(square)
+        tiles, found = lax.optimization_barrier((tiles, found))
         if index + 1 < count // group:
-            tiles, found = lax.optimization_barrier((tiles, found))
             found = [to_owner(piece, index * group + i) for i, piece in enumerate(found)]
         pieces += found
-    vectors = [to_owner(vector_pack, step) for step in range(count)]
-    token_grads, pieces[-1] = lax.optimization_barrier((token_grads, pieces[-1]))
-    table_grad, table_squares = table_gradient(
-        ids_ordered, own_features(token_grads[0]) + own_features(token_grads[1]), vocab
-    )
-
-    squares = squares + jnp.sum(table_squares)
-    squares, pieces[: count - group] = lax.optimization_barrier((squares, pieces[: count - group]))
+    token_parts, pieces[-1] = lax.optimization_barrier((token_parts, pieces[-1]))
+    table_grad, squares = table_gradient(
+        ids_ordered,
+        token_parts,
+        vocab,
+        vector_pack[None],
+        *block_squares,
+    )
+
+    squares, pieces[: count - group], vectors = lax.optimization_barrier((squares, pieces[: count - group], vectors))
     loss = jnp.where(place == high, jnp.sum(pair_loss), 0.0)
     square_total, loss_total = lax.psum((squares, loss), both)
-    norm_value = jnp.sqrt(square_total)
+    norm_value = jnp.sqrt(square_total[0, 0])
     factor = clip_limit / jnp.maximum(norm_value, clip_limit)
     pieces[count - group :], factor = lax.optimization_barrier((pieces[count - group :], factor))
     pieces[count - group :] = [to_owner(pieces[step], step) for step in range(count - group, count)]

time: 762 us -> 747 us (0.980)
  Pallas kernels: 244 us -> 232 us
  waiting for transfers between devices: 272 us -> 261 us
  blocking collectives: 38.7 us -> 47.4 us
    ppermute x6, waiting for transfers between devices: 225 us -> 215 us  [returned(): lax.ppermute(part, 'dp', [(low, k)])]
    pallas_call x4, Pallas kernels: 67 us -> 57.7 us  [products(): pl.pallas_call(functools.partial(product_kernel, shards, start), out_shap...]
    psum x1, blocking collectives: 38.7 us -> 47.4 us  [local(): square_total, loss_total = lax.psum((squares, loss), both)]
  transfers between devices with their start and end apart: 43 -> 43, of which waited for: 7 -> 5; matrix products, arithmetic and copies ran while one was open for 13% -> 13% of each run, Pallas kernels for 22% -> 25%
where the time goes in v4:
time: 747 us; the launch traced here: 736 us
  waiting for transfers between devices  261 us (35%)
  Pallas kernels  232 us (31%)
  other arithmetic  90.7 us (12%)
  starting transfers between devices  60.7 us (8%)
  blocking collectives  47.4 us (6%)
  local copies, waits for them, and re-layouts  34.8 us (5%)
  between operations  10.3 us (1%)
    ppermute x6, waiting for transfers between devices, returned(): lax.ppermute(part, 'dp', [(low, k)])  215 us
    pallas_call x4, Pallas kernels, products(): pl.pallas_call(functools.partial(product_kernel, shards, start), out_shap...  57.7 us
    pallas_call x6, Pallas kernels, forward(): pl.pallas_call(functools.partial(forward_kernel, tick, slots, unit, len(p...  56.2 us
    sub x3, other arithmetic, adam_step(): weight - rate * (corrected / scaled + decay * weight)  49.7 us
    psum x1, blocking collectives, local(): square_total, loss_total = lax.psum((squares, loss), both)  47.4 us
    pallas_call x1, Pallas kernels, table_gradient(): pl.pallas_call(table_kernel, out_shape=(jax.ShapeDtypeStruct((features, v...  35.5 us
    pallas_call x6, Pallas kernels, backward(): pl.pallas_call(functools.partial(backward_kernel, tick, units, count, han...  35 us
    ppermute x6, waiting for transfers between devices, sent_on(): lax.ppermute(columns, 'dp', [(k, low)])  31.3 us
  transfers between devices with their start and end apart: 43, of which 5 were waited for; matrix products, arithmetic and copies ran while one was open for 13% of the time, Pallas kernels for 25%

profile of v4, /device:TPU:0, one launch (start us, length us, event | category | flops | bytes accessed | tf_op | source)
XLA Modules:
  0.0 736.5 jit_solution(4632621005202580868)
XLA Ops:
  4.1 5.1 collective-permute-start.2
  11.3 3.5 bitcast_convert_fusion.rest_15_.rest_16_.rest_12_.rest_13_
  18.6 1.4 pad_maximum_fusion.3
  20.0 6.2 collective-permute-start.9
  26.2 2.4 collective-permute-start.8
  30.5 2.6 fusion.4
  33.2 1.3 fusion.1.rest_1_.rest_2_
  34.4 2.0 gather_fusion
  36.5 1.3 slice_convert_fusion
  39.2 1.5 slice.162
  41.3 1.3 pad_add_fusion.ids_ref
  42.6 21.3 %table_lookup.1 = (bf16[96,1024]{1,0:T(8,128)(2,1)}, bf16[96,3072]{1,0:T(8,128)(2,1)}) custom-call(s32[4096]{0:T(1024)} %pad_add_fusion.ids_ref, f32[96,50304]{1,0:T(8,128)} %embedding_ref.1), custom_call_target="tpu_custom_call" | custom-call | flops 1 | bytes 1 | tf_op jit(solution)/shard_map/table_lookup/pallas_call | solution.py:758
  63.9 1.5 slice.125
  66.0 1.7 slice.127
  68.9 1.5 reshape.237.rest_2_.rest_3_
  75.0 1.5 collective-permute-start.4
  78.5 26.0 %collective-permute-done.4.rest_7_ = bf16[192,512]{1,0:T(8,128)(2,1)S(1)} collective-permute-done((bf16[192,512]{1,0:T(8,128)(2,1)S(1)}, bf16[192,512]{1,0:T(8,128)(2,1)S(1)}, u32[]{:S(2)}, u32[]{:S(2)}) %collective-permute-start.4) | collective-permute-done | bytes 196640 | tf_op jit(solution)/shard_map/ppermute | solution.py:1032
  104.6 2.4 collective-permute-start.12
  107.0 2.4 collective-permute-start.13
  109.4 2.5 collective-permute-start.11
  117.1 1.4 fusion.56
  119.1 1.5 collective-permute-start.17
  120.5 1.5 collective-permute-start.16
  122.0 10.2 %collective-permute-start.15 = (bf16[192,1536]{1,0:T(8,128)(2,1)}, bf16[192,1536]{1,0:T(8,128)(2,1)}, u32[]{:S(2)}, u32[]{:S(2)}) collective-permute-start(bf16[192,1536]{1,0:T(8,128)(2,1)} %pad_maximum_fusion.1.rest_8_.rest_9_), channel_id=1, source_target_pairs={{0,1},{4,5},{8,9},{12,13},{16,17},{20,21},{24,25},{28,29}} | collective-permute-start | bytes 1769480 | tf_op jit(solution)/shard_map/ppermute | solution.py:1032
  132.2 6.6 layer_forward.6
  139.6 5.3 collective-permute-done.15.rest_7_.rest_8_
  144.9 6.9 layer_forward.7
  153.4 9.7 %layer_forward.8 = (bf16[512,768]{1,0:T(8,128)(2,1)}, f32[8,768]{1,0:T(8,128)}, bf16[4,512,11520]{2,1,0:T(8,128)(2,1)}, f32[4,512,768]{2,1,0:T(8,128)}, f32[4,16,512]{2,1,0:T(8,128)}) custom-call(s32[13]{0:T(128)} %copy-done.25, bf16[768,768]{1,0:T(8,128)(2,1)} %fusion.1.rest_1_.rest_2_, ...), custom_call_target="tpu_custom_call", output_to_operand_aliasing={{2}: (18, {}), {3}: (19, {}), {4}: (20, {})} | custom-call | flops 10000000000 | bytes 30000000 | tf_op jit(solution)/shard_map/layer_forward/pallas_call | solution.py:333
  165.5 9.3 %layer_forward.9 = (bf16[512,768]{1,0:T(8,128)(2,1)}, f32[8,768]{1,0:T(8,128)}, bf16[4,512,11520]{2,1,0:T(8,128)(2,1)}, f32[4,512,768]{2,1,0:T(8,128)}, f32[4,16,512]{2,1,0:T(8,128)}) custom-call(s32[13]{0:T(128)} %copy-done.25, bf16[768,768]{1,0:T(8,128)(2,1)} %fusion.1.rest_1_.rest_2_, ...), custom_call_target="tpu_custom_call", output_to_operand_aliasing={{2}: (18, {}), {3}: (19, {}), {4}: (20, {})} | custom-call | flops 10000000000 | bytes 30000000 | tf_op jit(solution)/shard_map/layer_forward/pallas_call | solution.py:333
  177.2 8.9 %layer_forward.10 = (bf16[512,768]{1,0:T(8,128)(2,1)}, f32[8,768]{1,0:T(8,128)}, bf16[4,512,11520]{2,1,0:T(8,128)(2,1)}, f32[4,512,768]{2,1,0:T(8,128)}, f32[4,16,512]{2,1,0:T(8,128)}) custom-call(s32[13]{0:T(128)} %copy-done.25, bf16[768,768]{1,0:T(8,128)(2,1)} %fusion.1.rest_1_.rest_2_, ...), custom_call_target="tpu_custom_call", output_to_operand_aliasing={{2}: (18, {}), {3}: (19, {}), {4}: (20, {})} | custom-call | flops 10000000000 | bytes 30000000 | tf_op jit(solution)/shard_map/layer_forward/pallas_call | solution.py:333
  187.7 14.7 %layer_forward.11 = (bf16[512,768]{1,0:T(8,128)(2,1)}, f32[8,768]{1,0:T(8,128)}, bf16[4,512,11520]{2,1,0:T(8,128)(2,1)}, f32[4,512,768]{2,1,0:T(8,128)}, f32[4,16,512]{2,1,0:T(8,128)}) custom-call(s32[13]{0:T(128)} %copy-done.25, bf16[768,768]{1,0:T(8,128)(2,1)} %fusion.1.rest_1_.rest_2_, ...), custom_call_target="tpu_custom_call", output_to_operand_aliasing={{2}: (18, {}), {3}: (19, {}), {4}: (20, {})} | custom-call | flops 10000000000 | bytes 30000000 | tf_op jit(solution)/shard_map/layer_forward/pallas_call | solution.py:333
  205.4 5.5 layer_backward.6
  211.6 3.0 layer_backward.7
  214.6 3.8 collective-permute-start.22
  220.1 8.5 %layer_backward.8 = (bf16[512,768]{1,0:T(8,128)(2,1)}, f32[1,9984]{1,0:T(1,128)}, bf16[4,512,11520]{2,1,0:T(8,128)(2,1)}, bf16[192,1536]{1,0:T(8,128)(2,1)}, bf1...) custom-call(s32[13]{0:T(128)} %copy-done.25, ...), custom_call_target="tpu_custom_call", output_to_operand_aliasing={{2}: (15, {})} | custom-call | flops 20000000000 | bytes 40000000 | tf_op jit(solution)/shard_map/layer_backward/pallas_call | solution.py:564
  230.2 7.3 layer_backward.9
  239.1 7.2 layer_backward.10
  246.4 1.3 collective-permute-start.29
  250.0 3.5 layer_backward.11
  253.5 1.3 collective-permute-start.33
  255.8 206.3 %collective-permute-done.29 = bf16[192,1536]{1,0:T(8,128)(2,1)S(1)} collective-permute-done((bf16[192,1536]{1,0:T(8,128)(2,1)}, bf16[192,1536]{1,0:T(8,128)(2,1)S(1)}, u32[]{:S(2)}, u32[]{:S(2)}) %collective-permute-start.29) | collective-permute-done | bytes 589856 | tf_op jit(solution)/shard_map/ppermute | solution.py:1116
  463.5 13.2 %weight_products.4 = bf16[12,384,384]{2,1,0:T(8,128)(2,1)} custom-call(s32[96]{0:T(128)} %fusion.39.tiles, bf16[4,512,11520]{2,1,0:T(8,128)(2,1)} %get-tuple-element.247.x_ref.y_ref, bf16[4,512,11520]{2,1,0:T(8,128)(2,1)} %get-tuple-element.247.x_ref.y_ref), custom_call_target="tpu_custom_call" | custom-call | flops 1 | bytes 1 | tf_op jit(solution)/shard_map/weight_products/pallas_call | solution.py:692
  476.8 8.9 %collective-permute-done.33 = bf16[192,512]{1,0:T(8,128)(2,1)S(1)} collective-permute-done((bf16[192,512]{1,0:T(8,128)(2,1)}, bf16[192,512]{1,0:T(8,128)(2,1)S(1)}, u32[]{:S(2)}, u32[]{:S(2)}) %collective-permute-start.33) | collective-permute-done | bytes 196640 | tf_op jit(solution)/shard_map/ppermute | solution.py:1116
  487.0 1.4 fusion.60
  488.5 1.3 collective-permute-start.28
  493.9 1.3 collective-permute-start.27
  495.2 13.9 %collective-permute-done.28 = f32[12288]{0:T(1024)} collective-permute-done((f32[12288]{0:T(1024)}, f32[12288]{0:T(1024)}, u32[]{:S(2)}, u32[]{:S(2)}) %collective-permute-start.28) | collective-permute-done | bytes 49184 | tf_op jit(solution)/shard_map/ppermute | solution.py:1159
  509.1 1.3 collective-permute-start.26
  510.4 13.1 %weight_products.5 = bf16[12,384,384]{2,1,0:T(8,128)(2,1)} custom-call(s32[96]{0:T(128)} %fusion.39.tiles, bf16[4,512,11520]{2,1,0:T(8,128)(2,1)} %get-tuple-element.247.x_ref.y_ref, bf16[4,512,11520]{2,1,0:T(8,128)(2,1)} %get-tuple-element.247.x_ref.y_ref), custom_call_target="tpu_custom_call" | custom-call | flops 1 | bytes 1 | tf_op jit(solution)/shard_map/weight_products/pallas_call | solution.py:692
  523.7 1.8 copy-done.2
  525.4 15.7 %weight_products.6 = (f32[1,384]{1,0:T(1,128)}, bf16[6,384,384]{2,1,0:T(8,128)(2,1)}, bf16[6,384,384]{2,1,0:T(8,128)(2,1)}) custom-call(s32[96]{0:T(128)} %fusion.39.tiles, bf16[4,512,11520]{2,1,0:T(8,128)(2,1)} %get-tuple-element.247.x_ref.y_ref, bf16[4,512,11520]{2,1,0:T(8,128)(2,1)} %get-tuple-element.247.x_ref.y_ref, bf16[12,384,384]{2,1,0:T(8,128)(2,1)} %copy-done.2), custom_call_target="tpu_custom_call" | custom-call | flops 1 | bytes 1 | tf_op jit(solution)/shard_map/weight_products/pallas_call | solution.py:692
  541.1 1.3 collective-permute-start.39
  545.2 1.3 fusion.47
  547.2 15.7 %weight_products.7 = (f32[1,384]{1,0:T(1,128)}, bf16[6,384,384]{2,1,0:T(8,128)(2,1)}, bf16[6,384,384]{2,1,0:T(8,128)(2,1)}) custom-call(s32[96]{0:T(128)} %fusion.39.tiles, bf16[4,512,11520]{2,1,0:T(8,128)(2,1)} %get-tuple-element.247.x_ref.y_ref, bf16[4,512,11520]{2,1,0:T(8,128)(2,1)} %get-tuple-element.247.x_ref.y_ref, ...), custom_call_target="tpu_custom_call" | custom-call | flops 1 | bytes 1 | tf_op jit(solution)/shard_map/weight_products/pallas_call | solution.py:692
  562.9 35.5 %table_gradient.1 = (f32[96,50304]{1,0:T(8,128)}, f32[1,1]{1,0:T(1,128)}) custom-call(s32[4096]{0:T(1024)} %bitcast.64, bf16[96,1536]{1,0:T(8,128)(2,1)} %get-tuple-element.268.refs_0_, bf16[96,1536]{1,0:T(8,128)(2,1)} %copy-done.18, bf16[96,512]{1,0:T(8,128)(2,1)} %get-tuple-element.270.refs_2_, bf16[96,512]{1,0:T(8,128)(2,1)} %collective-permute-done.36.refs_3_, ...), custom_call_target="tpu_custom_call" | custom-call | flops 1 | bytes 1 | tf_op jit(solution)/shard_map/table_gradient/pallas_call | solution.py:845
  598.5 47.4 %all-reduce = (f32[1]{0:T(128)}, f32[1,1]{1,0:T(1,128)}) all-reduce(f32[1]{0:T(128)} %bitcast.10, f32[1,1]{1,0:T(1,128)} %get-tuple-element.281), channel_id=1, replica_groups=mesh['member'=4,'section'=2,'dp'=4] {'section','dp'}, use_global_device_ids=true, to_apply=%region_2.3 | all-reduce | flops 2 | bytes 16 | tf_op jit(solution)/shard_map/psum | solution.py:1196
  646.6 1.5 collective-permute-start.41
  648.2 46.9 %multiply_subtract_fusion = (f32[96,50304]{1,0:T(8,128)}, f32[96,50304]{1,0:T(8,128)}, f32[96,50304]{1,0:T(8,128)}) fusion(f32[96,50304]{1,0:T(8,128)} %embedding_ref.1, f32[96,50304]{1,0:T(8,128)} %get-tuple-element.289, f32[]{:T(128)} %bitcast.23, f32[96,50304]{1,0:T(8,128)} %param.26, f32[96,50304]{1,0:T(8,128)} %param.27), kind=kLoop, calls=%fused_computation.3 | loop fusion | flops 77266944 | bytes 135217152 | tf_op jit(solution)/shard_map/sub | solution.py:927
  695.1 5.0 broadcast_select_fusion.2
  701.9 1.4 multiply_subtract_fusion.2
  703.2 1.4 multiply_subtract_fusion.1
  704.6 1.9 broadcast_select_fusion.1
  706.5 2.2 pad_maximum_fusion.g_ref
  708.7 26.3 %shampoo.1 = (f32[12,384,384]{2,1,0:T(8,128)}, f32[12,384,384]{2,1,0:T(8,128)}, f32[12,384,384]{2,1,0:T(8,128)}, f32[12,384,384]{2,1,0:T(8,128)}) custom-call(f32[1]{0:T(128)} %bitcast.24.factor_ref, bf16[12,384,384]{2,1,0:T(8,128)(2,1)} %pad_maximum_fusion.g_ref, f32[12,384,384]{2,1,0:T(8,128)} %bitcast.59, f32[12,384,384]{2,1,0:T(8,128)} %bitcast.60, ...), custom_call_target="tpu_custom_call" | custom-call | flops 1 | bytes 1 | tf_op jit(solution)/shard_map/shampoo/pallas_call | solution.py:897
  (207 shorter events, 53.3 us)
Async XLA Ops:
  4.1 12.3 %collective-permute-start.2 = (f32[3810]{0:T(1024)S(1)}, f32[3810]{0:T(1024)}, u32[]{:S(2)}, u32[]{:S(2)}) collective-permute-start(f32[3810]{0:T(1024)S(1)} %concatenate.29), channel_id=1, source_target_pairs={{0,3},{1,0},{2,1},{3,2},{4,7},{5,4},{6,5},{7,6},{8,11},{9,8},{10,9... | collective-permute-start | bytes 45728 | tf_op jit(solution)/shard_map/ppermute | solution.py:995
  9.2 7.9 %collective-permute-start.1 = (f32[3810]{0:T(1024)S(1)}, f32[3810]{0:T(1024)}, u32[]{:S(2)}, u32[]{:S(2)}) collective-permute-start(f32[3810]{0:T(1024)S(1)} %concatenate.29), channel_id=1, source_target_pairs={{0,2},{1,3},{2,0},{3,1},{4,6},{5,7},{6,4},{7,5},{8,10},{9,11},{10,... | collective-permute-start | bytes 45728 | tf_op jit(solution)/shard_map/ppermute | solution.py:995
  9.2 8.7 %collective-permute-start = (f32[3810]{0:T(1024)S(1)}, f32[3810]{0:T(1024)}, u32[]{:S(2)}, u32[]{:S(2)}) collective-permute-start(f32[3810]{0:T(1024)S(1)} %concatenate.29), channel_id=1, source_target_pairs={{0,1},{1,2},{2,3},{3,0},{4,5},{5,6},{6,7},{7,4},{8,9},{9,10},{10,1... | collective-permute-start | bytes 45728 | tf_op jit(solution)/shard_map/ppermute | solution.py:995
  14.8 92.2 %copy-start = (bf16[12,384,384]{2,1,0:T(8,128)(2,1)}, bf16[12,384,384]{2,1,0:T(8,128)(2,1)S(1)}, u32[]{:S(2)}) copy-start(bf16[12,384,384]{2,1,0:T(8,128)(2,1)S(1)} %bitcast_convert_fusion.rest_15_.rest_16_.rest_12_.rest_13_) | copy-start | bytes 10616836
  20.0 84.5 %collective-permute-start.9 = (bf16[12,384,384]{2,1,0:T(8,128)(2,1)S(1)}, bf16[12,384,384]{2,1,0:T(8,128)(2,1)}, u32[]{:S(2)}, u32[]{:S(2)}) collective-permute-start(bf16[12,384,384]{2,1,0:T(8,128)(2,1)S(1)} %bitcast_convert_fusion.rest_15_.rest_16_.rest_12_.rest_13_), channel_id=1, source_target_pairs={{0,1},{7,6},{8,9},{15,14},{16,17},{23,22},{24,25},{31,30}} | collective-permute-start | bytes 10616840 | tf_op jit(solution)/shard_map/ppermute | solution.py:1007
  26.2 78.4 %collective-permute-start.8 = (bf16[12,384,384]{2,1,0:T(8,128)(2,1)S(1)}, bf16[12,384,384]{2,1,0:T(8,128)(2,1)}, u32[]{:S(2)}, u32[]{:S(2)}) collective-permute-start(bf16[12,384,384]{2,1,0:T(8,128)(2,1)S(1)} %bitcast_convert_fusion.rest_15_.rest_16_.rest_12_.rest_13_), channel_id=1, source_target_pairs={{3,1},{4,6},{2,5},{5,2},{11,9},{12,14},{10,13},{13,10},{19,17},{20... | collective-permute-start | bytes 10616840 | tf_op jit(solution)/shard_map/ppermute | solution.py:1007
  41.3 26.4 %collective-permute-start.10 = (f32[4,2784]{1,0:T(4,128)}, f32[4,2784]{1,0:T(4,128)S(1)}, u32[]{:S(2)}, u32[]{:S(2)}) collective-permute-start(f32[4,2784]{1,0:T(4,128)} %slice.162), channel_id=1, source_target_pairs={{0,4},{4,0},{1,5},{5,1},{2,6},{6,2},{3,7},{7,3},{8,12},{12,8},{9,1... | collective-permute-start | bytes 133640 | tf_op jit(solution)/shard_map/ppermute | solution.py:948
  42.6 25.7 %copy-start.24 = (f32[4,2784]{1,0:T(4,128)S(1)}, f32[4,2784]{1,0:T(4,128)}, u32[]{:S(2)}) copy-start(f32[4,2784]{1,0:T(4,128)} %slice.162) | copy-start | bytes 133636
  65.4 7.2 collective-permute-start.3
  67.6 7.3 collective-permute-start.7
  72.6 59.6 %copy-start.5 = (f32[1,2304]{1,0:T(1,128)}, f32[1,2304]{1,0:T(1,128)S(1)}, u32[]{:S(2)}) copy-start(f32[1,2304]{1,0:T(1,128)S(1)} %reshape.238.rest_3_.rest_4_) | copy-start | bytes 27652
  73.6 35.8 %copy-start.20 = (bf16[192,512]{1,0:T(8,128)(2,1)}, bf16[192,512]{1,0:T(8,128)(2,1)S(1)}, u32[]{:S(2)}) copy-start(bf16[192,512]{1,0:T(8,128)(2,1)S(1)} %pad_maximum_fusion.2.rest_8_) | copy-start | bytes 589828
  73.6 4.9 collective-permute-start.6
  74.3 4.2 collective-permute-start.5
  75.0 29.6 %collective-permute-start.4 = (bf16[192,512]{1,0:T(8,128)(2,1)S(1)}, bf16[192,512]{1,0:T(8,128)(2,1)S(1)}, u32[]{:S(2)}, u32[]{:S(2)}) collective-permute-start(bf16[192,512]{1,0:T(8,128)(2,1)S(1)} %pad_maximum_fusion.2.rest_8_), channel_id=1, source_target_pairs={{0,1},{4,5},{8,9},{12,13},{16,17},{20,21},{24,25},{28,29}} | collective-permute-start | bytes 589832 | tf_op jit(solution)/shard_map/ppermute | solution.py:1032
  78.5 30.9 %copy-start.39 = (bf16[192,512]{1,0:T(8,128)(2,1)}, bf16[192,512]{1,0:T(8,128)(2,1)S(1)}, u32[]{:S(2)}) copy-start(bf16[192,512]{1,0:T(8,128)(2,1)S(1)} %collective-permute-done.6.rest_10_) | copy-start | bytes 589828
  78.5 30.9 %copy-start.40 = (bf16[192,512]{1,0:T(8,128)(2,1)}, bf16[192,512]{1,0:T(8,128)(2,1)S(1)}, u32[]{:S(2)}) copy-start(bf16[192,512]{1,0:T(8,128)(2,1)S(1)} %collective-permute-done.5.rest_9_) | copy-start | bytes 589828
  104.6 14.5 %collective-permute-start.12 = (bf16[12,384,384]{2,1,0:T(8,128)(2,1)}, bf16[12,384,384]{2,1,0:T(8,128)(2,1)}, u32[]{:S(2)}, u32[]{:S(2)}) collective-permute-start(bf16[12,384,384]{2,1,0:T(8,128)(2,1)} %collective-permute-done.9.rest_12_.rest_13_.rest_9_.rest_10_), channel_id=1, source_target_pairs={{1,5},{5,1},{2,6},{6,2},{9,13},{13,9},{10,14},{14,10},{17,21},{21,... | collective-permute-start | bytes 10616840 | tf_op jit(solution)/shard_map/ppermute | solution.py:1054
  107.0 25.2 %collective-permute-start.13 = (bf16[12,384,384]{2,1,0:T(8,128)(2,1)S(1)}, bf16[12,384,384]{2,1,0:T(8,128)(2,1)}, u32[]{:S(2)}, u32[]{:S(2)}) collective-permute-start(bf16[12,384,384]{2,1,0:T(8,128)(2,1)S(1)} %bitcast_convert_fusion.rest_15_.rest_16_.rest_12_.rest_13_), channel_id=1, source_target_pairs={{1,5},{5,1},{2,6},{6,2},{9,13},{13,9},{10,14},{14,10},{17,21},{21,... | collective-permute-start | bytes 10616840 | tf_op jit(solution)/shard_map/ppermute | solution.py:1054
  109.4 22.8 %collective-permute-start.11 = (bf16[12,384,384]{2,1,0:T(8,128)(2,1)}, bf16[12,384,384]{2,1,0:T(8,128)(2,1)}, u32[]{:S(2)}, u32[]{:S(2)}) collective-permute-start(bf16[12,384,384]{2,1,0:T(8,128)(2,1)} %collective-permute-done.8.rest_11_.rest_12_.rest_8_.rest_9_), channel_id=1, source_target_pairs={{1,5},{5,1},{2,6},{6,2},{9,13},{13,9},{10,14},{14,10},{17,21},{21,... | collective-permute-start | bytes 10616840 | tf_op jit(solution)/shard_map/ppermute | solution.py:1054
  112.6 19.6 %copy-start.25 = (s32[13]{0:T(128)}, s32[13]{0:T(128)S(1)}, u32[]{:S(2)}) copy-start(s32[13]{0:T(128)S(1)} %constant_dynamic-update-slice_fusion.rest_0_) | copy-start | bytes 160
  119.1 20.5 %collective-permute-start.17 = (bf16[192,1536]{1,0:T(8,128)(2,1)}, bf16[192,1536]{1,0:T(8,128)(2,1)}, u32[]{:S(2)}, u32[]{:S(2)}) collective-permute-start(bf16[192,1536]{1,0:T(8,128)(2,1)} %pad_maximum_fusion.1.rest_8_.rest_9_), channel_id=1, source_target_pairs={{3,1},{7,5},{11,9},{15,13},{19,17},{23,21},{27,25},{31,29}} | collective-permute-start | bytes 1769480 | tf_op jit(solution)/shard_map/ppermute | solution.py:1032
  120.5 19.1 %collective-permute-start.16 = (bf16[192,1536]{1,0:T(8,128)(2,1)}, bf16[192,1536]{1,0:T(8,128)(2,1)}, u32[]{:S(2)}, u32[]{:S(2)}) collective-permute-start(bf16[192,1536]{1,0:T(8,128)(2,1)} %pad_maximum_fusion.1.rest_8_.rest_9_), channel_id=1, source_target_pairs={{2,1},{6,5},{10,9},{14,13},{18,17},{22,21},{26,25},{30,29}} | collective-permute-start | bytes 1769480 | tf_op jit(solution)/shard_map/ppermute | solution.py:1032
  122.0 22.8 %collective-permute-start.15 = (bf16[192,1536]{1,0:T(8,128)(2,1)}, bf16[192,1536]{1,0:T(8,128)(2,1)}, u32[]{:S(2)}, u32[]{:S(2)}) collective-permute-start(bf16[192,1536]{1,0:T(8,128)(2,1)} %pad_maximum_fusion.1.rest_8_.rest_9_), channel_id=1, source_target_pairs={{0,1},{4,5},{8,9},{12,13},{16,17},{20,21},{24,25},{28,29}} | collective-permute-start | bytes 1769480 | tf_op jit(solution)/shard_map/ppermute | solution.py:1032
  138.9 13.7 %collective-permute-start.14 = (bf16[512,768]{1,0:T(8,128)(2,1)}, bf16[512,768]{1,0:T(8,128)(2,1)S(1)}, u32[]{:S(2)}, u32[]{:S(2)}) collective-permute-start(bf16[512,768]{1,0:T(8,128)(2,1)} %get-tuple-element.183), channel_id=1, source_target_pairs={{1,2},{5,6},{9,10},{13,14},{17,18},{21,22},{25,26},{29,30}} | collective-permute-start | bytes 2359304 | tf_op jit(solution)/shard_map/ppermute | solution.py:1089
  151.8 12.8 %collective-permute-start.18 = (bf16[512,768]{1,0:T(8,128)(2,1)}, bf16[512,768]{1,0:T(8,128)(2,1)S(1)}, u32[]{:S(2)}, u32[]{:S(2)}) collective-permute-start(bf16[512,768]{1,0:T(8,128)(2,1)} %get-tuple-element.192), channel_id=1, source_target_pairs={{1,2},{5,6},{9,10},{13,14},{17,18},{21,22},{25,26},{29,30}} | collective-permute-start | bytes 2359304 | tf_op jit(solution)/shard_map/ppermute | solution.py:1089
  163.2 13.1 %collective-permute-start.19 = (bf16[512,768]{1,0:T(8,128)(2,1)}, bf16[512,768]{1,0:T(8,128)(2,1)S(1)}, u32[]{:S(2)}, u32[]{:S(2)}) collective-permute-start(bf16[512,768]{1,0:T(8,128)(2,1)} %get-tuple-element.197), channel_id=1, source_target_pairs={{1,2},{5,6},{9,10},{13,14},{17,18},{21,22},{25,26},{29,30}} | collective-permute-start | bytes 2359304 | tf_op jit(solution)/shard_map/ppermute | solution.py:1089
  174.8 12.0 %collective-permute-start.20 = (bf16[512,768]{1,0:T(8,128)(2,1)}, bf16[512,768]{1,0:T(8,128)(2,1)S(1)}, u32[]{:S(2)}, u32[]{:S(2)}) collective-permute-start(bf16[512,768]{1,0:T(8,128)(2,1)} %get-tuple-element.202), channel_id=1, source_target_pairs={{1,2},{5,6},{9,10},{13,14},{17,18},{21,22},{25,26},{29,30}} | collective-permute-start | bytes 2359304 | tf_op jit(solution)/shard_map/ppermute | solution.py:1089
  187.7 15.5 %copy-start.34 = (f32[768]{0:T(1024)S(1)}, f32[768]{0:T(1024)}, u32[]{:S(2)}) copy-start(f32[768]{0:T(1024)} %slice_reduce_fusion) | copy-start | bytes 9220
  187.7 15.7 %copy-start.37 = (f32[4,1]{1,0:T(4,128)S(1)}, f32[4,1]{1,0:T(4,128)}, u32[]{:S(2)}) copy-start(f32[4,1]{1,0:T(4,128)} %get-tuple-element.339) | copy-start | bytes 52
  187.7 15.7 %copy-start.38 = (f32[4,1]{1,0:T(4,128)S(1)}, f32[4,1]{1,0:T(4,128)}, u32[]{:S(2)}) copy-start(f32[4,1]{1,0:T(4,128)} %get-tuple-element.340) | copy-start | bytes 52
  210.9 8.3 %collective-permute-start.21 = (bf16[512,768]{1,0:T(8,128)(2,1)}, bf16[512,768]{1,0:T(8,128)(2,1)S(1)}, u32[]{:S(2)}, u32[]{:S(2)}) collective-permute-start(bf16[512,768]{1,0:T(8,128)(2,1)} %get-tuple-element.213), channel_id=1, source_target_pairs={{2,1},{6,5},{10,9},{14,13},{18,17},{22,21},{26,25},{30,29}} | collective-permute-start | bytes 2359304 | tf_op jit(solution)/shard_map/ppermute | solution.py:1146
  211.6 7.4 %copy-start.35 = (f32[4]{0:T(128)S(1)}, f32[4]{0:T(128)}, u32[]{:S(2)}) copy-start(f32[4]{0:T(128)} %div.114.rest_1_) | copy-start | bytes 52
  214.6 14.7 %collective-permute-start.22 = (bf16[512,768]{1,0:T(8,128)(2,1)}, bf16[512,768]{1,0:T(8,128)(2,1)S(1)}, u32[]{:S(2)}, u32[]{:S(2)}) collective-permute-start(bf16[512,768]{1,0:T(8,128)(2,1)} %get-tuple-element.216), channel_id=1, source_target_pairs={{2,1},{6,5},{10,9},{14,13},{18,17},{22,21},{26,25},{30,29}} | collective-permute-start | bytes 2359304 | tf_op jit(solution)/shard_map/ppermute | solution.py:1146
  219.2 243.6 %copy-start.26 = (f32[2304]{0:T(1024)}, f32[2304]{0:T(1024)S(1)}, u32[]{:S(2)}) copy-start(f32[2304]{0:T(1024)S(1)} %maximum_select_fusion) | copy-start | bytes 27652
  228.5 9.7 %collective-permute-start.23 = (bf16[512,768]{1,0:T(8,128)(2,1)}, bf16[512,768]{1,0:T(8,128)(2,1)S(1)}, u32[]{:S(2)}, u32[]{:S(2)}) collective-permute-start(bf16[512,768]{1,0:T(8,128)(2,1)} %get-tuple-element.223), channel_id=1, source_target_pairs={{2,1},{6,5},{10,9},{14,13},{18,17},{22,21},{26,25},{30,29}} | collective-permute-start | bytes 2359304 | tf_op jit(solution)/shard_map/ppermute | solution.py:1146
  237.5 11.6 %collective-permute-start.24 = (bf16[512,768]{1,0:T(8,128)(2,1)}, bf16[512,768]{1,0:T(8,128)(2,1)S(1)}, u32[]{:S(2)}, u32[]{:S(2)}) collective-permute-start(bf16[512,768]{1,0:T(8,128)(2,1)} %get-tuple-element.230), channel_id=1, source_target_pairs={{2,1},{6,5},{10,9},{14,13},{18,17},{22,21},{26,25},{30,29}} | collective-permute-start | bytes 2359304 | tf_op jit(solution)/shard_map/ppermute | solution.py:1146
  246.4 215.7 %collective-permute-start.29 = (bf16[192,1536]{1,0:T(8,128)(2,1)}, bf16[192,1536]{1,0:T(8,128)(2,1)S(1)}, u32[]{:S(2)}, u32[]{:S(2)}) collective-permute-start(bf16[192,1536]{1,0:T(8,128)(2,1)} %get-tuple-element.233), channel_id=1, source_target_pairs={{1,0},{5,4},{9,8},{13,12},{17,16},{21,20},{25,24},{29,28}} | collective-permute-start | bytes 1769480 | tf_op jit(solution)/shard_map/ppermute | solution.py:1116
  247.7 215.7 %collective-permute-start.30 = (bf16[192,1536]{1,0:T(8,128)(2,1)}, bf16[192,1536]{1,0:T(8,128)(2,1)S(1)}, u32[]{:S(2)}, u32[]{:S(2)}) collective-permute-start(bf16[192,1536]{1,0:T(8,128)(2,1)} %get-tuple-element.235), channel_id=1, source_target_pairs={{1,2},{5,6},{9,10},{13,14},{17,18},{21,22},{25,26},{29,30}} | collective-permute-start | bytes 1769480 | tf_op jit(solution)/shard_map/ppermute | solution.py:1116
  248.4 215.1 %collective-permute-start.31 = (bf16[192,1536]{1,0:T(8,128)(2,1)}, bf16[192,1536]{1,0:T(8,128)(2,1)S(1)}, u32[]{:S(2)}, u32[]{:S(2)}) collective-permute-start(bf16[192,1536]{1,0:T(8,128)(2,1)} %get-tuple-element.236), channel_id=1, source_target_pairs={{1,3},{5,7},{9,11},{13,15},{17,19},{21,23},{25,27},{29,31}} | collective-permute-start | bytes 1769480 | tf_op jit(solution)/shard_map/ppermute | solution.py:1116
  253.5 232.1 %collective-permute-start.33 = (bf16[192,512]{1,0:T(8,128)(2,1)}, bf16[192,512]{1,0:T(8,128)(2,1)S(1)}, u32[]{:S(2)}, u32[]{:S(2)}) collective-permute-start(bf16[192,512]{1,0:T(8,128)(2,1)} %get-tuple-element.242), channel_id=1, source_target_pairs={{1,0},{5,4},{9,8},{13,12},{17,16},{21,20},{25,24},{29,28}} | collective-permute-start | bytes 589832 | tf_op jit(solution)/shard_map/ppermute | solution.py:1116
  254.8 230.8 %collective-permute-start.34 = (bf16[192,512]{1,0:T(8,128)(2,1)}, bf16[192,512]{1,0:T(8,128)(2,1)S(1)}, u32[]{:S(2)}, u32[]{:S(2)}) collective-permute-start(bf16[192,512]{1,0:T(8,128)(2,1)} %get-tuple-element.244), channel_id=1, source_target_pairs={{1,2},{5,6},{9,10},{13,14},{17,18},{21,22},{25,26},{29,30}} | collective-permute-start | bytes 589832 | tf_op jit(solution)/shard_map/ppermute | solution.py:1116
  255.8 207.6 %copy-start.17 = (f32[9984]{0:T(1024)}, f32[9984]{0:T(1024)S(1)}, u32[]{:S(2)}) copy-start(f32[9984]{0:T(1024)S(1)} %fusion.12) | copy-start | bytes 119812
  462.1 14.7 %copy-start.14 = (bf16[192,1536]{1,0:T(8,128)(2,1)}, bf16[192,1536]{1,0:T(8,128)(2,1)S(1)}, u32[]{:S(2)}) copy-start(bf16[192,1536]{1,0:T(8,128)(2,1)S(1)} %collective-permute-done.29) | copy-start | bytes 1769476
  462.1 23.5 %collective-permute-start.35 = (bf16[192,512]{1,0:T(8,128)(2,1)}, bf16[192,512]{1,0:T(8,128)(2,1)S(1)}, u32[]{:S(2)}, u32[]{:S(2)}) collective-permute-start(bf16[192,512]{1,0:T(8,128)(2,1)} %get-tuple-element.245), channel_id=1, source_target_pairs={{1,3},{5,7},{9,11},{13,15},{17,19},{21,23},{25,27},{29,31}} | collective-permute-start | bytes 589832 | tf_op jit(solution)/shard_map/ppermute | solution.py:1116
  463.4 13.4 %copy-start.15 = (bf16[192,1536]{1,0:T(8,128)(2,1)}, bf16[192,1536]{1,0:T(8,128)(2,1)S(1)}, u32[]{:S(2)}) copy-start(bf16[192,1536]{1,0:T(8,128)(2,1)S(1)} %collective-permute-done.30) | copy-start | bytes 1769476
  463.4 23.6 %collective-permute-start.25 = (f32[12288]{0:T(1024)}, f32[12288]{0:T(1024)}, u32[]{:S(2)}, u32[]{:S(2)}) collective-permute-start(f32[12288]{0:T(1024)} %pad_maximum_fusion.4), channel_id=1, source_target_pairs={{0,4},{4,0},{1,5},{5,1},{2,6},{6,2},{3,7},{7,3},{8,12},{12,8},{9,1... | collective-permute-start | bytes 147464 | tf_op jit(solution)/shard_map/ppermute | solution.py:948
  463.5 13.3 %copy-start.16 = (bf16[192,1536]{1,0:T(8,128)(2,1)}, bf16[192,1536]{1,0:T(8,128)(2,1)S(1)}, u32[]{:S(2)}) copy-start(bf16[192,1536]{1,0:T(8,128)(2,1)S(1)} %collective-permute-done.31) | copy-start | bytes 1769476
  463.5 26.3 %copy-start.1 = (bf16[192,1536]{1,0:T(8,128)(2,1)S(1)}, bf16[192,1536]{1,0:T(8,128)(2,1)}, u32[]{:S(2)}) copy-start(bf16[192,1536]{1,0:T(8,128)(2,1)} %get-tuple-element.239) | copy-start | bytes 1769476
  487.0 36.6 %collective-permute-start.37 = (bf16[12,384,384]{2,1,0:T(8,128)(2,1)}, bf16[12,384,384]{2,1,0:T(8,128)(2,1)S(1)}, u32[]{:S(2)}, u32[]{:S(2)}) collective-permute-start(bf16[12,384,384]{2,1,0:T(8,128)(2,1)} %weight_products.4), channel_id=1, source_target_pairs={{0,4},{4,0},{1,5},{5,1},{2,6},{6,2},{3,7},{7,3},{8,12},{12,8},{9,1... | collective-permute-start | bytes 10616840 | tf_op jit(solution)/shard_map/ppermute | solution.py:948
  488.5 20.6 %collective-permute-start.28 = (f32[12288]{0:T(1024)}, f32[12288]{0:T(1024)}, u32[]{:S(2)}, u32[]{:S(2)}) collective-permute-start(f32[12288]{0:T(1024)} %fusion.60), channel_id=1, source_target_pairs={{1,0},{2,3},{5,4},{6,7},{9,8},{10,11},{13,12},{14,15},{17,16},{18,... | collective-permute-start | bytes 147464 | tf_op jit(solution)/shard_map/ppermute | solution.py:1159
  491.7 31.8 %collective-permute-start.32 = (bf16[96,1536]{1,0:T(8,128)(2,1)S(1)}, bf16[96,1536]{1,0:T(8,128)(2,1)S(1)}, u32[]{:S(2)}, u32[]{:S(2)}) collective-permute-start(bf16[96,1536]{1,0:T(8,128)(2,1)S(1)} %get-tuple-element.331), channel_id=1, source_target_pairs={{0,4},{4,0},{1,5},{5,1},{2,6},{6,2},{3,7},{7,3},{8,12},{12,8},{9,1... | collective-permute-start | bytes 884744 | tf_op jit(solution)/shard_map/ppermute | solution.py:948
  493.9 29.6 %collective-permute-start.36 = (bf16[96,512]{1,0:T(8,128)(2,1)}, bf16[96,512]{1,0:T(8,128)(2,1)}, u32[]{:S(2)}, u32[]{:S(2)}) collective-permute-start(bf16[96,512]{1,0:T(8,128)(2,1)} %get-tuple-element.335), channel_id=1, source_target_pairs={{0,4},{4,0},{1,5},{5,1},{2,6},{6,2},{3,7},{7,3},{8,12},{12,8},{9,1... | collective-permute-start | bytes 294920 | tf_op jit(solution)/shard_map/ppermute | solution.py:948
  493.9 29.6 %collective-permute-start.27 = (f32[12288]{0:T(1024)}, f32[12288]{0:T(1024)}, u32[]{:S(2)}, u32[]{:S(2)}) collective-permute-start(f32[12288]{0:T(1024)} %fusion.60), channel_id=1, source_target_pairs={{1,2},{2,1},{5,6},{6,5},{9,10},{10,9},{13,14},{14,13},{17,18},{18,... | collective-permute-start | bytes 147464 | tf_op jit(solution)/shard_map/ppermute | solution.py:1159
  509.1 14.4 %collective-permute-start.26 = (f32[12288]{0:T(1024)}, f32[12288]{0:T(1024)}, u32[]{:S(2)}, u32[]{:S(2)}) collective-permute-start(f32[12288]{0:T(1024)} %fusion.60), channel_id=1, source_target_pairs={{1,3},{2,0},{5,7},{6,4},{9,11},{10,8},{13,15},{14,12},{17,19},{18,... | collective-permute-start | bytes 147464 | tf_op jit(solution)/shard_map/ppermute | solution.py:1159
  523.5 17.6 %copy-start.18 = (bf16[96,1536]{1,0:T(8,128)(2,1)}, bf16[96,1536]{1,0:T(8,128)(2,1)S(1)}, u32[]{:S(2)}) copy-start(bf16[96,1536]{1,0:T(8,128)(2,1)S(1)} %collective-permute-done.32.refs_1_) | copy-start | bytes 884740
  523.6 23.7 %collective-permute-start.38 = (bf16[12,384,384]{2,1,0:T(8,128)(2,1)}, bf16[12,384,384]{2,1,0:T(8,128)(2,1)}, u32[]{:S(2)}, u32[]{:S(2)}) collective-permute-start(bf16[12,384,384]{2,1,0:T(8,128)(2,1)} %weight_products.5), channel_id=1, source_target_pairs={{0,4},{4,0},{1,5},{5,1},{2,6},{6,2},{3,7},{7,3},{8,12},{12,8},{9,1... | collective-permute-start | bytes 10616840 | tf_op jit(solution)/shard_map/ppermute | solution.py:948
  541.1 57.4 %collective-permute-start.39 = (bf16[6,384,384]{2,1,0:T(8,128)(2,1)}, bf16[6,384,384]{2,1,0:T(8,128)(2,1)S(1)}, u32[]{:S(2)}, u32[]{:S(2)}) collective-permute-start(bf16[6,384,384]{2,1,0:T(8,128)(2,1)} %get-tuple-element.275), channel_id=1, source_target_pairs={{1,3},{2,0},{5,7},{6,4},{9,11},{10,8},{13,15},{14,12},{17,19},{18,... | collective-permute-start | bytes 5308424 | tf_op jit(solution)/shard_map/ppermute | solution.py:1159
  542.4 56.1 %collective-permute-start.40 = (bf16[6,384,384]{2,1,0:T(8,128)(2,1)}, bf16[6,384,384]{2,1,0:T(8,128)(2,1)S(1)}, u32[]{:S(2)}, u32[]{:S(2)}) collective-permute-start(bf16[6,384,384]{2,1,0:T(8,128)(2,1)} %get-tuple-element.276), channel_id=1, source_target_pairs={{1,2},{2,1},{5,6},{6,5},{9,10},{10,9},{13,14},{14,13},{17,18},{18,... | collective-permute-start | bytes 5308424 | tf_op jit(solution)/shard_map/ppermute | solution.py:1159
  598.5 96.6 %copy-start.3 = (bf16[6,384,384]{2,1,0:T(8,128)(2,1)}, bf16[6,384,384]{2,1,0:T(8,128)(2,1)S(1)}, u32[]{:S(2)}) copy-start(bf16[6,384,384]{2,1,0:T(8,128)(2,1)S(1)} %collective-permute-done.39) | copy-start | bytes 5308420
  598.5 96.6 %copy-start.4 = (bf16[6,384,384]{2,1,0:T(8,128)(2,1)}, bf16[6,384,384]{2,1,0:T(8,128)(2,1)S(1)}, u32[]{:S(2)}) copy-start(bf16[6,384,384]{2,1,0:T(8,128)(2,1)S(1)} %collective-permute-done.40) | copy-start | bytes 5308420
  646.6 48.5 %collective-permute-start.41 = (bf16[6,384,384]{2,1,0:T(8,128)(2,1)}, bf16[6,384,384]{2,1,0:T(8,128)(2,1)}, u32[]{:S(2)}, u32[]{:S(2)}) collective-permute-start(bf16[6,384,384]{2,1,0:T(8,128)(2,1)} %get-tuple-element.287), channel_id=1, source_target_pairs={{1,0},{2,3},{5,4},{6,7},{9,8},{10,11},{13,12},{14,15},{17,16},{18,... | collective-permute-start | bytes 5308424 | tf_op jit(solution)/shard_map/ppermute | solution.py:1159
  695.1 8.1 %copy-start.28 = (f32[1,2496]{1,0:T(1,128)S(1)}, f32[1,2496]{1,0:T(1,128)}, u32[]{:S(2)}) copy-start(f32[1,2496]{1,0:T(1,128)} %param.33) | copy-start | bytes 29956
  700.2 4.5 collective-permute-start.42
  (21 other events, 51.4 us)
